TPU v7x, 256 devices: a whole 4x4x8 slice. The times are simulated.
256 devices in a mesh: dp: 32 (over x_hi, z, core), fsdp: 8 (over x_lo, y).
Axes of the slice: x: 4 (x_hi: 2, x_lo: 2; x = x_hi * 2 + x_lo), y: 4, z: 8, core: 2. Of those that a mesh axis runs over, the one named last changes fastest.
Arguments:
- states: bfloat16 [49152, 5120], P(('dp', 'fsdp')), may hold values from -24 to 24
- steps: int32 [256], P(('dp', 'fsdp')), may hold values from 0 to 999
- frozen_query_rows: bfloat16 [49152, 5120], P(('dp', 'fsdp')), may hold values from -6 to 6
- frozen_key_rows: bfloat16 [49152, 5120], P(('dp', 'fsdp')), may hold values from -18 to 18
- frozen_value_rows: bfloat16 [49152, 5120], P(('dp', 'fsdp')), may hold values from -6 to 6
- cotangent: bfloat16 [49152, 5120], P(('dp', 'fsdp')), may hold values from -24 to 24
- adapter_down_maps: bfloat16 [2, 5120, 128], P(None, 'fsdp'), may hold values from -0.078125 to 0.078125
- adapter_up_maps: bfloat16 [2, 128, 5120], P(None, None, 'fsdp'), may hold values from -0.5 to 0.5
Outputs:
- grad_down: float32 [2, 5120, 128], P(None, 'fsdp')
- grad_up: float32 [2, 128, 5120], P(None, None, 'fsdp')
All inputs are finite; a program needn't handle non-finite values.
Results may differ from a plain program's by a relative error of at most 0.012.
Values may be sent and summed in bfloat16 or wider, within the bound.
No kernel may reach another device: no remote copies, remote signals or barrier semaphores. Data moves between devices by JAX's collectives and lax.ppermute only.
A program may use at most 128 MiB of HBM per device.

v0:
```python
import math

import jax
import jax.numpy as jnp
from jax import lax
from jax.sharding import PartitionSpec as P

HEADS = 40
NSTEPS = 1000


def rounded(value):
    return lax.optimization_barrier(value.astype(jnp.bfloat16)).astype(jnp.float32)


def clip_objective(
    down_matrix,
    up_matrix,
    states,
    frozen_query_rows,
    frozen_key_rows,
    frozen_value_rows,
    cotangent,
    weight,
):
    highest = lax.Precision.HIGHEST
    length = states.shape[0]
    width = states.shape[1]
    head_size = width // HEADS
    inputs = states.astype(jnp.float32)
    center = inputs - jnp.mean(inputs, axis=1, keepdims=True)
    spread = jnp.mean(center * center, axis=1, keepdims=True)
    normed = rounded(center * lax.rsqrt(spread + 1e-06))
    low = rounded(jnp.einsum("td,jdr->jtr", normed, down_matrix, precision=highest))
    delta = jnp.einsum("jtr,jrd->jtd", low, up_matrix, precision=highest)
    query = rounded(frozen_query_rows.astype(jnp.float32) + delta[0]).reshape(
        length, HEADS, head_size
    )
    value = rounded(frozen_value_rows.astype(jnp.float32) + delta[1]).reshape(
        length, HEADS, head_size
    )
    keys = frozen_key_rows.astype(jnp.float32).reshape(length, HEADS, head_size)
    scores = jnp.einsum("qhe,khe->hqk", query, keys, precision=highest) * (
        1.0 / math.sqrt(head_size)
    )
    probs = rounded(jax.nn.softmax(scores, axis=-1))
    attended = jnp.einsum("hqk,khe->qhe", probs, value, precision=highest).reshape(length, width)
    return weight * jnp.sum(attended * cotangent.astype(jnp.float32))


def local(
    states,
    steps,
    frozen_query_rows,
    frozen_key_rows,
    frozen_value_rows,
    cotangent,
    adapter_down_maps,
    adapter_up_maps,
):
    down_matrix, up_matrix = (
        lax.all_gather(adapter_down_maps, "fsdp", axis=1, tiled=True),
        lax.all_gather(adapter_up_maps, "fsdp", axis=2, tiled=True),
    )
    weight = (steps[0].astype(jnp.float32) + 1.0) / NSTEPS
    grad_fn = jax.grad(clip_objective, argnums=(0, 1))
    local_down, local_up = grad_fn(
        down_matrix.astype(jnp.float32),
        up_matrix.astype(jnp.float32),
        states,
        frozen_query_rows,
        frozen_key_rows,
        frozen_value_rows,
        cotangent,
        weight,
    )
    data_count = lax.axis_size("dp")
    group_count = lax.axis_size("fsdp")
    width = local_down.shape[1]
    rank_size = local_down.shape[2]
    factor = 1.0 / math.sqrt(states.shape[0] * data_count * group_count)
    rows = width // (data_count * group_count)
    pieces_down = (
        local_down.reshape(2, group_count, data_count, rows, rank_size)
        .transpose(2, 1, 0, 3, 4)
        .reshape(data_count * group_count, 2, rows, rank_size)
    )
    pieces_up = (
        local_up.reshape(2, rank_size, group_count, data_count, rows)
        .transpose(3, 2, 0, 1, 4)
        .reshape(data_count * group_count, 2, rank_size, rows)
    )
    summed_down, summed_up = (
        lax.psum_scatter(pieces_down, ("dp", "fsdp"), scatter_dimension=0, tiled=True),
        lax.psum_scatter(pieces_up, ("dp", "fsdp"), scatter_dimension=0, tiled=True),
    )
    joined_down, joined_up = (
        lax.all_gather(summed_down, "dp", axis=0, tiled=True),
        lax.all_gather(summed_up, "dp", axis=0, tiled=True),
    )
    shard_down = joined_down.transpose(1, 0, 2, 3).reshape(2, data_count * rows, rank_size)
    shard_up = joined_up.transpose(1, 2, 0, 3).reshape(2, rank_size, data_count * rows)
    return (shard_down * factor, shard_up * factor)


def solution(mesh):
    in_specs = (
        P(("dp", "fsdp"), None),
        P(("dp", "fsdp")),
        P(("dp", "fsdp"), None),
        P(("dp", "fsdp"), None),
        P(("dp", "fsdp"), None),
        P(("dp", "fsdp"), None),
        P(None, "fsdp", None),
        P(None, None, "fsdp"),
    )
    out_specs = (P(None, "fsdp", None), P(None, None, "fsdp"))
    return jax.shard_map(local, mesh=mesh, in_specs=in_specs, out_specs=out_specs, check_vma=False)
```

profile of v0, /device:TPU:1, one launch (start us, length us, event | category | flops | bytes accessed | tf_op | source)
XLA Modules:
  0.0 570.8 jit_solution(748312822632556784)
XLA Ops:
  7.2 0.0 copy-start
  7.2 0.0 all-gather.3.cloned.1.call-start
  7.2 0.7 all-gather.3.cloned.1.call-update
  7.9 0.0 all-gather.5.cloned.1.call-start
  8.0 0.7 all-gather.5.cloned.1.call-update
  8.7 0.0 all-reduce.7.cloned.1.call-start
  8.7 0.0 copy-start.2
  8.7 2.0 convert_reduce_fusion
  10.8 2.2 fusion.19
  13.0 1.9 fusion.20
  15.6 39.7 %all-gather.3.cloned.1.call-done = bf16[2,5120,128]{2,1,0:T(8,128)(2,1)} async-done(((bf16[2,640,128]{2,1,0:T(8,128)(2,1)}), bf16[2,5120,128]{2,1,0:T(8,128)(2,1)}) %all-gather.3.cloned.1.call-update) | async-done | bytes 2621456 | tf_op jit(solution)/shard_map/all_gather | solution.py:62
  55.2 3.0 fusion.54
  58.3 43.5 %all-gather.5.cloned.1.call-done = bf16[2,128,5120]{2,1,0:T(8,128)(2,1)} async-done(((bf16[2,128,640]{2,1,0:T(8,128)(2,1)}), bf16[2,128,5120]{2,1,0:T(8,128)(2,1)}) %all-gather.5.cloned.1.call-update) | async-done | bytes 2621456 | tf_op jit(solution)/shard_map/all_gather | solution.py:63
  101.8 3.1 fusion.63
  104.9 1.2 fusion.24
  106.1 1.2 fusion.37
  107.3 0.0 copy-start.7
  107.3 6.3 %fusion.62 = (f32[40,192]{1,0:T(8,128)S(1)}, f32[40,192,192]{1,2,0:T(8,128)S(1)}) fusion(f32[40,192,192]{1,2,0:T(8,128)S(1)} %fusion.37), kind=kOutput, calls=%fused_computation.77 | output fusion | flops 5898431 | bytes 11827200 | tf_op jit(solution)/shard_map/jvp()/sub | solution.py:46
  113.7 3.6 fusion.33
  117.3 2.9 divide_convert_fusion
  120.2 11.1 %convert_bitcast_fusion = bf16[40,24,8,128]{3,2,1,0:T(8,128)(2,1)} fusion(f32[40,192,192]{1,2,0:T(8,128)S(1)} %get-tuple-element.13, bf16[40,192,192]{1,2,0:T(8,128)(2,1)} %copy-done.3, f32[40,192]{1,0:T(8,128)S(1)} %neg.6, f32[40,192]{1,0:T(8,128)S(1)} %get-tuple-element.12, bf16[192,5120]{1,0:T(8,128)(2,1)S(1)} %copy-done), kind=kOutput, calls=%fused_computation.58 | convolution fusion | flops 2273280000 | bytes 12840960 | tf_op jit(solution)/shard_map/transpose(jvp(qhe,khe->hqk))/dot_general | solution.py:43
  131.3 2.2 copy.93
  133.5 3.6 convert_bitcast_fusion.1
  137.1 0.9 copy.94
  138.0 0.0 copy-start.4
  138.0 1.3 copy-done.4
  139.3 5.6 fusion.8
  144.9 8.7 %copy.46 = f32[2,128,5120]{1,0,2:T(2,128)} copy(f32[2,128,5120]{2,1,0:T(8,128)} %fusion.8) | data formatting | bytes 10485760 | tf_op jit(solution)/shard_map/transpose(jvp(jtr,jrd->jtd))/dot_general | solution.py:35
  153.6 5.5 copy.91
  159.1 0.0 copy-start.5
  159.1 0.0 copy-start.9
  159.2 6.3 %copy.48 = f32[256,2,128,20]{2,1,3,0:T(2,128)} copy(f32[256,2,128,20]{2,0,3,1:T(8,128)S(1)} %bitcast.118) | data formatting | bytes 10485760 | tf_op jit(solution)/shard_map/reshape | solution.py:91
  165.5 3.6 fusion.53
  169.1 3.2 convolution_bitcast_fusion
  172.3 8.8 %copy.43 = f32[2,5120,128]{2,0,1:T(2,128)} copy(f32[2,5120,128]{1,2,0:T(8,128)} %convolution_bitcast_fusion) | data formatting | bytes 10485760 | tf_op jit(solution)/shard_map/transpose(jvp(td,jdr->jtr))/transpose | solution.py:34
  181.2 5.5 copy.92
  186.7 6.3 %copy.45 = f32[256,2,20,128]{3,1,2,0:T(2,128)} copy(f32[256,2,20,128]{3,0,2,1:T(8,128)S(1)} %bitcast.120) | data formatting | bytes 10485760 | tf_op jit(solution)/shard_map/reshape | solution.py:86
  193.0 0.0 all-reduce.7.cloned.1.call-update
  193.0 0.0 copy-start.1
  193.0 285.5 %all-reduce.7.cloned.1.call-done = (f32[256,2,20,128]{3,1,2,0:T(2,128)}, f32[256,2,128,20]{2,1,3,0:T(2,128)}) async-done(((f32[256,2,20,128]{3,1,2,0:T(2,128)}, f32[256,2,128,20]{2,1,3,0:T(2,128)}), (f32[256,2,20,128]{3,1,2,0:T(2,128)}, f32[256,2,128,20]{2,1,3,0:T(2,128)})) %all-reduce.7.cloned.1.call-update) | async-done | bytes 10485776
  478.5 0.7 constant_dynamic-slice_fusion.1
  479.2 42.7 %all_gather.14 = f32[32,2,20,128]{3,1,2,0:T(2,128)S(1)} all-gather(f32[1,2,20,128]{3,1,2,0:T(2,128)S(1)} %constant_dynamic-slice_fusion.1), channel_id=1, replica_groups=mesh['dp'=32,'fsdp'=8] {'dp'}, dimensions={0}, use_global_device_ids=true | all-gather | bytes 675840 | tf_op jit(solution)/shard_map/all_gather | solution.py:98
  521.9 0.3 broadcast_multiply_fusion.1
  522.3 0.9 copy.49
  523.1 0.7 constant_dynamic-slice_fusion
  523.9 38.5 %all_gather.15 = f32[32,2,128,20]{2,1,3,0:T(2,128)S(1)} all-gather(f32[1,2,128,20]{2,1,3,0:T(2,128)S(1)} %constant_dynamic-slice_fusion), channel_id=1, replica_groups=mesh['dp'=32,'fsdp'=8] {'dp'}, dimensions={0}, use_global_device_ids=true | all-gather | bytes 675840 | tf_op jit(solution)/shard_map/all_gather | solution.py:99
  562.3 0.3 broadcast_multiply_fusion
  562.7 1.4 copy.50
  (20 shorter events, 0.1 us)
Async XLA Ops:
  7.2 98.9 %copy-start = (bf16[192,5120]{1,0:T(8,128)(2,1)S(1)}, bf16[192,5120]{1,0:T(8,128)(2,1)}, u32[]{:S(2)}) copy-start(bf16[192,5120]{1,0:T(8,128)(2,1)} %param.11) | copy-start | bytes 5898244
  7.2 48.1 %all-gather.3.cloned.1.call-start = ((), (), s32[]{:S(2)}) async-start(), calls=%async_computation | async-start | bytes 2949120 | tf_op jit(solution)/shard_map/all_gather | solution.py:62
  7.9 93.9 %all-gather.5.cloned.1.call-start = ((), (), s32[]{:S(2)}) async-start(), calls=%async_computation.1 | async-start | bytes 2949120 | tf_op jit(solution)/shard_map/all_gather | solution.py:63
  8.7 469.9 %all-reduce.7.cloned.1.call-start = ((), (), s32[]{:S(2)}) async-start(), calls=%async_computation.2 | async-start | bytes 20971520
  8.7 4.3 copy-start.2
  101.8 3.1 copy-start.10
  101.8 3.1 copy-start.11
  107.3 6.3 %copy-start.7 = (bf16[192,5120]{1,0:T(8,128)(2,1)S(1)}, bf16[192,5120]{1,0:T(8,128)(2,1)}, u32[]{:S(2)}) copy-start(bf16[192,5120]{1,0:T(8,128)(2,1)} %param.13) | copy-start | bytes 5898244
  117.3 2.9 copy-start.3
  131.3 2.2 copy-start.8
  138.0 1.3 copy-start.4
  159.1 6.4 %copy-start.5 = (bf16[40,24,8,128]{3,2,0,1:T(8,128)(2,1)S(1)}, bf16[40,24,8,128]{3,2,0,1:T(8,128)(2,1)}, u32[]{:S(2)}) copy-start(bf16[40,24,8,128]{3,2,0,1:T(8,128)(2,1)} %copy-done.4) | copy-start | bytes 5898244
  159.1 6.4 %copy-start.9 = (bf16[2,128,5120]{2,1,0:T(8,128)(2,1)S(1)}, bf16[2,128,5120]{2,1,0:T(8,128)(2,1)}, u32[]{:S(2)}) copy-start(bf16[2,128,5120]{2,1,0:T(8,128)(2,1)} %all-gather.5.cloned.1.call-done) | copy-start | bytes 7864324
  165.5 3.6 copy-start.6
  193.0 371.0 %copy-start.1 = (bf16[192,5120]{1,0:T(8,128)(2,1)S(1)}, bf16[192,5120]{1,0:T(8,128)(2,1)}, u32[]{:S(2)}) copy-start(bf16[192,5120]{1,0:T(8,128)(2,1)} %param.11) | copy-start | bytes 5898244
Sparse Core Ops, SparseCore 0:
  9.8 45.3 all-gather.2
  57.0 44.7 all-gather.4
  193.1 285.3 all-reduce.6
where the time goes:
time: 578 us; the launch traced here: 571 us
  waiting for transfers between devices  370 us (64%)
  blocking collectives  81.1 us (14%)
  local copies, waits for them, and re-layouts  49.4 us (9%)
  matrix products  37.9 us (7%)
  other arithmetic  17.3 us (3%)
  between operations  14.8 us (3%)
    unnamed x4, waiting for transfers between devices  287 us
    all_gather x1, waiting for transfers between devices, local(): lax.all_gather(adapter_up_maps, 'fsdp', axis=2, tiled=True)  43.5 us
    all_gather x1, blocking collectives, local(): lax.all_gather(summed_down, 'dp', axis=0, tiled=True)  42.7 us
    all_gather x1, waiting for transfers between devices, local(): lax.all_gather(adapter_down_maps, 'fsdp', axis=1, tiled=True)  39.7 us
    all_gather x1, blocking collectives, local(): lax.all_gather(summed_up, 'dp', axis=0, tiled=True)  38.5 us
    dot_general x3, matrix products, clip_objective(): delta = jnp.einsum('jtr,jrd->jtd', low, up_matrix, precision=highest)  12.3 us
    dot_general x2, matrix products, clip_objective(): jnp.einsum('qhe,khe->hqk', query, keys, precision=highest)  12.3 us
  transfers between devices with their start and end apart: 3, of which 3 were waited for; matrix products, arithmetic and copies ran while one was open for 2% of the time, Pallas kernels for 0%

commit v1 on v0

v1 whole, which is shorter than its diff:
```python
import functools
import math

import jax
import jax.numpy as jnp
from jax import lax
from jax.experimental import pallas as pl
from jax.experimental.pallas import tpu as pltpu
from jax.sharding import PartitionSpec as P

HEADS = 40
NSTEPS = 1000
AXES = ("dp", "fsdp")
NX, NY, NZ, NC = 4, 4, 8, 2
BF16 = jnp.bfloat16
F32 = jnp.float32

CLIP = 192
WIDTH = 5120
HALF = WIDTH // 2
SHARD = 640
RANK = 128
HEAD = 128
LOCAL_HEADS = SHARD // HEAD
NORM_ROWS = 32
VMEM_LIMIT = 24 * 1024 * 1024


def linear(x, y, z, c):
    x, y, z, c = x % NX, y % NY, z % NZ, c % NC
    return (((x // 2) * NZ + z) * NC + c) * 8 + (x % 2) * NY + y


def permutation(target):
    pairs = []
    for x in range(NX):
        for y in range(NY):
            for z in range(NZ):
                for c in range(NC):
                    pairs.append((linear(x, y, z, c), linear(*target(x, y, z, c))))
    return pairs


def send(value, target):
    return lax.ppermute(value, AXES, permutation(target))


def swap_cores(value):
    return send(value, lambda x, y, z, c: (x, y, z, 1 - c))


def send_y(value, step):
    return send(value, lambda x, y, z, c: (x, y + step, z, c))


Z_GROUPS = [
    [linear(x, y, z, c) for z in range(NZ)]
    for x in range(NX)
    for y in range(NY)
    for c in range(NC)
]


def exchange_z(value):
    return lax.all_to_all(value, AXES, 0, 0, axis_index_groups=Z_GROUPS, tiled=True)


def dot(a, b, ca, cb):
    return lax.dot_general(a, b, (((ca,), (cb,)), ((), ())), preferred_element_type=F32)


def whole(shape):
    return pl.BlockSpec(shape, lambda *_: (0,) * len(shape))


def normalize_kernel(place, states, q, k, v, g, nown, nsend):
    mine = pl.multiple_of(place[0] * HALF, HALF)
    other = pl.multiple_of((1 - place[0]) * HALF, HALF)
    for start in range(0, NORM_ROWS, 16):
        rows = slice(start, start + 16)
        inputs = states[rows, :].astype(F32)
        center = inputs - jnp.mean(inputs, axis=1, keepdims=True)
        spread = jnp.mean(center * center, axis=1, keepdims=True)
        inverse = lax.rsqrt(spread + 1e-06)
        mean = jnp.mean(inputs, axis=1, keepdims=True)
        for begin, out in ((mine, nown), (other, nsend.at[4])):
            part = states[rows, pl.ds(begin, HALF)].astype(F32)
            out[rows, :] = ((part - mean) * inverse).astype(BF16)
    for n, src in enumerate((q, k, v, g)):
        nsend[n] = src[...]


def normalize(place, states, q, k, v, g):
    half = pl.BlockSpec((NORM_ROWS, HALF), lambda i, place: (i, 1 - place[0]))
    return pl.pallas_call(
        normalize_kernel,
        grid_spec=pltpu.PrefetchScalarGridSpec(
            num_scalar_prefetch=1,
            grid=(CLIP // NORM_ROWS,),
            in_specs=[pl.BlockSpec((NORM_ROWS, WIDTH), lambda i, place: (i, 0))] + [half] * 4,
            out_specs=(
                pl.BlockSpec((NORM_ROWS, HALF), lambda i, place: (i, 0)),
                pl.BlockSpec((5, NORM_ROWS, HALF), lambda i, place: (0, i, 0)),
            ),
        ),
        out_shape=(
            jax.ShapeDtypeStruct((CLIP, HALF), BF16),
            jax.ShapeDtypeStruct((5, CLIP, HALF), BF16),
        ),
        compiler_params=pltpu.CompilerParams(vmem_limit_bytes=VMEM_LIMIT),
        cost_estimate=pl.CostEstimate(flops=0, bytes_accessed=14000000, transcendentals=0),
        name="normalize",
    )(place, states, q, k, v, g)


def lower_kernel(place, nown, npeer, own0, other0, own, other, weight, out):
    core, y = place[2], place[1]
    for clip in range(2):
        totals = [jnp.zeros((CLIP, RANK), F32) for _ in range(2)]
        for step in range(NY):
            start = pl.multiple_of(lax.rem(y + step, NY) * SHARD, SHARD)
            if clip == 0:
                rows = nown[:, pl.ds(start, SHARD)]
            else:
                rows = npeer[0, :, pl.ds(start, SHARD)]
            totals[0] += dot(rows, own[step - 1] if step else own0[0], 1, 0)
            totals[1] += dot(rows, other[step - 1] if step else other0[0], 1, 0)
        out[clip, core, :CLIP] = totals[0]
        out[clip, 1 - core, :CLIP] = totals[1]
        out[clip, 0, CLIP:] = weight[...]
        out[clip, 1, CLIP:] = weight[...]


def lower(place, nown, peer, *downs_and_weight):
    return pl.pallas_call(
        lower_kernel,
        grid=(1,),
        out_shape=jax.ShapeDtypeStruct((2, 2, CLIP + 8, RANK), F32),
        in_specs=[
            pl.BlockSpec(memory_space=pltpu.SMEM),
            whole((CLIP, HALF)),
            pl.BlockSpec((1, CLIP, HALF), lambda i: (4, 0, 0)),
        ]
        + [whole(a.shape) for a in downs_and_weight],
        out_specs=whole((2, 2, CLIP + 8, RANK)),
        compiler_params=pltpu.CompilerParams(vmem_limit_bytes=VMEM_LIMIT),
        name="lower",
    )(place, nown, peer, *downs_and_weight)


def attend_kernel(step, place, *refs):
    q0, k0, v0, g0, q1, k1, v1, g1, up_own, up_other = refs[:10]
    if step == 0:
        low_mine, low_peer, gup, dlow, low, weights, ups, dqs, dvs = refs[10:]
        for j in range(2):
            for clip in range(2):
                total = low_mine[clip, j, :CLIP] + low_peer[1 - clip, j, :CLIP]
                low[j, clip * CLIP : (clip + 1) * CLIP] = total.astype(BF16)
        weights[0] = low_mine[0, 0, CLIP:]
        weights[1] = low_peer[0, 0, CLIP:]
    else:
        low, weights, dlow_in, gup, dlow, ups, dqs, dvs = refs[10:]
    core = place[2]
    scale = 1.0 / math.sqrt(HEAD)
    slot = 0 if up_own.shape[0] == 1 else step - 1
    ups[core] = up_own[slot]
    ups[1 - core] = up_other[slot]
    for clip in range(2):
        rows = slice(clip * CLIP, (clip + 1) * CLIP)
        weight = weights[clip, :1]
        if clip == 0:
            q, k, v, g = (r[...] for r in (q0, k0, v0, g0))
        else:
            q, k, v, g = (r[0] for r in (q1, k1, v1, g1))
        query = (q.astype(F32) + dot(low[0, rows], ups[0], 1, 0)).astype(BF16)
        value = (v.astype(F32) + dot(low[1, rows], ups[1], 1, 0)).astype(BF16)
        for h in range(LOCAL_HEADS):
            cols = slice(h * HEAD, (h + 1) * HEAD)
            kh, gh = k[:, cols], g[:, cols]
            scores = dot(kh, query[:, cols], 1, 1) * scale
            powers = jnp.exp(scores - jnp.max(scores, axis=0, keepdims=True))
            probs = powers * (1.0 / jnp.sum(powers, axis=0, keepdims=True))
            dv = dot(probs.astype(BF16), gh, 1, 0)
            dprobs = dot(value[:, cols], gh, 1, 1)
            inner = jnp.sum(probs * dprobs, axis=0, keepdims=True)
            dscores = (probs * (dprobs - inner)).astype(BF16)
            dq = dot(dscores, kh, 0, 0)
            dqs[rows, cols] = (dq * (weight * scale)).astype(BF16)
            dvs[rows, cols] = (dv * weight).astype(BF16)
    for j, grads in enumerate((dqs, dvs)):
        for clip in range(2):
            rows = slice(clip * CLIP, (clip + 1) * CLIP)
            total = dot(grads[rows], ups[j], 1, 1)
            dlow[clip, j] = total if step == 0 else dlow_in[clip, j] + total
        store_pieces(gup, j, dot(low[j], grads[...], 0, 0))


def store_pieces(out, j, total):
    for piece in range(RANK // 8):
        part = total[piece * 8 : (piece + 1) * 8]
        part = jnp.concatenate(
            [part[:, h * HEAD : (h + 1) * HEAD] for h in range(LOCAL_HEADS)], axis=0
        )
        at = j * (RANK // 8) + piece
        out[at // NZ, at % NZ] = part.astype(BF16)


PIECES = (4, NZ, 40, 128)
LOWS = (2, 2, CLIP, RANK)


def attend(step, place, arrays, peer, up_own, up_other, *lows):
    def shard(place):
        return lax.rem(place[1] + step, NY)

    own_spec = pl.BlockSpec((CLIP, SHARD), lambda i, place: (0, place[0] * NY + shard(place)))
    peer_specs = [
        pl.BlockSpec((1, CLIP, SHARD), lambda i, place, n=n: (n, 0, shard(place)))
        for n in range(4)
    ]
    out_shape = [jax.ShapeDtypeStruct(PIECES, BF16), jax.ShapeDtypeStruct(LOWS, F32)]
    if step == 0:
        out_shape += [
            jax.ShapeDtypeStruct((2, 2 * CLIP, RANK), BF16),
            jax.ShapeDtypeStruct((2, 8, RANK), F32),
        ]
    return pl.pallas_call(
        functools.partial(attend_kernel, step),
        grid_spec=pltpu.PrefetchScalarGridSpec(
            num_scalar_prefetch=1,
            grid=(1,),
            in_specs=[own_spec] * 4
            + peer_specs
            + [whole(a.shape) for a in (up_own, up_other, *lows)],
            out_specs=[whole(a.shape) for a in out_shape],
            scratch_shapes=[
                pltpu.VMEM((2, RANK, SHARD), BF16),
                pltpu.VMEM((2 * CLIP, SHARD), BF16),
                pltpu.VMEM((2 * CLIP, SHARD), BF16),
            ],
        ),
        out_shape=out_shape,
        compiler_params=pltpu.CompilerParams(vmem_limit_bytes=24 * 1024 * 1024),
        cost_estimate=pl.CostEstimate(
            flops=4000000000, bytes_accessed=3000000, transcendentals=400000
        ),
        name="attend",
    )(place, *arrays, peer, peer, peer, peer, up_own, up_other, *lows)


def down_kernel(place, n0, n1, mine, peer, *refs):
    outs, dlow = refs[:NY], refs[NY]

    @pl.when(pl.program_id(0) == 0)
    def _():
        for j in range(2):
            for clip in range(2):
                total = mine[clip, j] + peer[1 - clip, j]
                dlow[j * RANK : (j + 1) * RANK, clip * CLIP : (clip + 1) * CLIP] = total.astype(
                    BF16
                ).T

    normed = jnp.concatenate([n0[...], n1[0]], axis=0)
    total = dot(dlow[...], normed, 1, 0)
    for step in range(NY):

        @pl.when(pl.program_id(0) == step)
        def _(out=outs[step]):
            for j in range(2):
                store_pieces(out, j, total[j * RANK : (j + 1) * RANK])


def down_grads(place, nown, peer, mine, theirs):
    def shard(i, place):
        return lax.rem(place[1] + i, NY)

    return pl.pallas_call(
        down_kernel,
        grid_spec=pltpu.PrefetchScalarGridSpec(
            num_scalar_prefetch=1,
            grid=(NY,),
            in_specs=[
                pl.BlockSpec((CLIP, SHARD), lambda i, place: (0, shard(i, place))),
                pl.BlockSpec((1, CLIP, SHARD), lambda i, place: (4, 0, shard(i, place))),
                whole(LOWS),
                whole(LOWS),
            ],
            out_specs=[whole(PIECES)] * NY,
            scratch_shapes=[pltpu.VMEM((2 * RANK, 2 * CLIP), BF16)],
        ),
        out_shape=[jax.ShapeDtypeStruct(PIECES, BF16)] * NY,
        compiler_params=pltpu.CompilerParams(vmem_limit_bytes=24 * 1024 * 1024),
        cost_estimate=pl.CostEstimate(
            flops=3000000000, bytes_accessed=5000000, transcendentals=0
        ),
        name="down_grads",
    )(place, nown, peer, mine, theirs)


def sum_y_kernel(place, *refs):
    ups, downs, outs = refs[:4], refs[4:8], refs[8:]
    x = place[3]
    for quarter in range(4):
        source = lax.rem(quarter + x, 4)
        for z in range(NZ):
            up = sum(r[source, z].astype(F32) for r in ups)
            down = sum(r[source, z].astype(F32) for r in downs)
            outs[quarter][z] = jnp.concatenate([up, down], axis=0).astype(BF16)


def sum_y(place, ups, downs):
    return pl.pallas_call(
        sum_y_kernel,
        out_shape=[jax.ShapeDtypeStruct((NZ, 80, 128), BF16)] * 4,
        in_specs=[pl.BlockSpec(memory_space=pltpu.SMEM)]
        + [pl.BlockSpec(memory_space=pltpu.VMEM)] * 8,
        out_specs=[pl.BlockSpec(memory_space=pltpu.VMEM)] * 4,
        compiler_params=pltpu.CompilerParams(vmem_limit_bytes=VMEM_LIMIT),
        name="sum_y",
    )(place, *ups, *downs)


def finish_kernel(factor, place, own, first, second, first_peer, second_peer, down, up, flat):
    core, x = place[2], place[3]

    def write(step, ref):
        quarter = lax.rem(x + step, 4)
        for z in range(NZ):
            part = ref[z].astype(F32) * factor
            for out, begin in ((up, 0), (flat, 40)):
                out[quarter * NZ + z] = jnp.concatenate(
                    [part[begin + h * 8 : begin + (h + 1) * 8] for h in range(LOCAL_HEADS)], axis=1
                )

    @pl.when(core == 0)
    def _():
        for step, ref in enumerate((own, second, first_peer, first)):
            write(step, ref)

    @pl.when(core == 1)
    def _():
        for step, ref in enumerate((second, second_peer, first, first_peer)):
            write(step, ref)

    for j in range(2):
        rows = flat[j * 2 * NZ : (j + 1) * 2 * NZ].reshape(RANK, SHARD)
        down[j] = rows.T


def finish(factor, place, *parts):
    return pl.pallas_call(
        functools.partial(finish_kernel, factor),
        out_shape=(
            jax.ShapeDtypeStruct((2, SHARD, RANK), F32),
            jax.ShapeDtypeStruct((4 * NZ, 8, SHARD), F32),
        ),
        in_specs=[pl.BlockSpec(memory_space=pltpu.SMEM)]
        + [pl.BlockSpec(memory_space=pltpu.VMEM)] * 5,
        out_specs=(pl.BlockSpec(memory_space=pltpu.VMEM),) * 2,
        scratch_shapes=[pltpu.VMEM((4 * NZ, 8, SHARD), F32)],
        compiler_params=pltpu.CompilerParams(vmem_limit_bytes=VMEM_LIMIT),
        name="finish",
    )(place, *parts)


def cross_x(part):
    other = send(part, lambda x, y, z, c: (x - 1, y, z, 1) if c == 0 else (x, y, z, 0))
    own = send(part, lambda x, y, z, c: (x, y, z, 0) if c == 0 else (x + 1, y, z, 1))
    return own, other


def gather(part):
    first = cross_x(part[None])
    rest = cross_x(jnp.stack([send_y(part, -step) for step in range(1, NY)]))
    return first, rest


def local(states, steps, q, k, v, g, down_maps, up_maps):
    dp, fsdp = lax.axis_index("dp"), lax.axis_index("fsdp")
    core, x_lo, y = dp % 2, fsdp // NY, fsdp % NY
    x = (dp // (2 * NZ)) * 2 + x_lo
    place = jnp.stack([x_lo ^ core, y, core, x]).astype(jnp.int32)
    weight = (steps[0].astype(F32) + 1.0) / NSTEPS
    weight = jnp.full((8, RANK), weight, F32)

    down_part = lax.dynamic_index_in_dim(down_maps, core, 0, keepdims=False)
    up_part = lax.dynamic_index_in_dim(up_maps, core, 0, keepdims=False)
    down_first, down_rest = gather(down_part)
    nown, nsend = normalize(place, states, q, k, v, g)
    peer = swap_cores(nsend)
    up_first, up_rest = gather(up_part)

    low_mine = lower(place, nown, peer, *down_first, *down_rest, weight)
    low_peer = swap_cores(low_mine)
    rows = (place, (q, k, v, g), peer)
    gup, dlow, low, weights = attend(0, *rows, *up_first, low_mine, low_peer)
    ups = [gup]
    for step in range(1, NY):
        gup, dlow = attend(step, *rows, *up_rest, low, weights, dlow)
        ups.append(send_y(gup, step))
    downs = down_grads(place, nown, peer, dlow, swap_cores(dlow))
    downs = [downs[0]] + [send_y(downs[step], step) for step in range(1, NY)]

    quarters = sum_y(place, ups, downs)
    parts = [
        quarters[0],
        send(quarters[1], lambda x, y, z, c: (x + 1, y, z, 1 - c)),
        send(quarters[2], lambda x, y, z, c: (x + 2, y, z, c)),
        send(quarters[3], lambda x, y, z, c: (x - 1, y, z, 1 - c)),
    ]
    eighths = sum(part.astype(F32) for part in parts).astype(BF16)
    eighths = exchange_z(eighths)
    piece = jnp.sum(eighths.astype(F32), axis=0).astype(BF16)
    quarter = exchange_z(jnp.broadcast_to(piece, (NZ, 80, 128)))

    first = send(
        quarter, lambda x, y, z, c: (x + 2, y, z, 1) if c == 0 else (x + 1, y, z, 0)
    )
    second = send(
        quarter, lambda x, y, z, c: (x, y, z, 1) if c == 0 else (x - 1, y, z, 0)
    )
    first_peer = swap_cores(first)
    second_peer = swap_cores(second)
    data_count = lax.axis_size("dp") * lax.axis_size("fsdp")
    factor = 1.0 / math.sqrt(CLIP * data_count)
    grad_down, grad_up = finish(
        factor, place, quarter, first, second, first_peer, second_peer
    )
    return (grad_down, grad_up.reshape(2, RANK, SHARD))


def solution(mesh):
    in_specs = (
        P(("dp", "fsdp"), None),
        P(("dp", "fsdp")),
        P(("dp", "fsdp"), None),
        P(("dp", "fsdp"), None),
        P(("dp", "fsdp"), None),
        P(("dp", "fsdp"), None),
        P(None, "fsdp", None),
        P(None, None, "fsdp"),
    )
    out_specs = (P(None, "fsdp", None), P(None, None, "fsdp"))
    return jax.shard_map(local, mesh=mesh, in_specs=in_specs, out_specs=out_specs, check_vma=False)
```

time: 578 us -> 169 us (0.29); the launches traced: 571 us -> 169 us
  waiting for transfers between devices: 370 us -> 56.8 us
  blocking collectives: 81.1 us -> 27.5 us
  starting transfers between devices: 0.11 us -> 41.8 us
  local copies, waits for them, and re-layouts: 49.4 us -> 7.86 us
  matrix products: 37.9 us -> 0 us
  Pallas kernels: 0 us -> 32.9 us
  other arithmetic: 17.3 us -> 0.32 us
  between operations: 14.8 us -> 1.65 us
    unnamed x4 -> x0, waiting for transfers between devices: 287 us -> none
    all_gather x2 -> x0, waiting for transfers between devices: 83.2 us -> none  [the longest x1 43.5 us: local(): lax.all_gather(adapter_up_maps, 'fsdp', axis=2, tiled=True)]
    all_gather x2 -> x0, blocking collectives: 81.1 us -> none  [the longest x1 42.7 us: local(): lax.all_gather(summed_down, 'dp', axis=0, tiled=True)]
    ppermute x0 -> x30, waiting for transfers between devices: none -> 56.8 us  [send(): return lax.ppermute(value, AXES, permutation(target))]
    ppermute x0 -> x30, starting transfers between devices: none -> 41.8 us  [send(): return lax.ppermute(value, AXES, permutation(target))]
    dot_general x9 -> x0, matrix products: 37.9 us -> none  [the longest x3 12.3 us: clip_objective(): delta = jnp.einsum('jtr,jrd->jtd', low, up_matrix, precision=highest)]
    pallas_call x0 -> x9, Pallas kernels: none -> 32.9 us  [the longest x4 18.6 us: attend(): pl.pallas_call(functools.partial(attend_kernel, step), grid_spec=pltpu.Pr...]
    all_to_all x0 -> x2, blocking collectives: none -> 27.5 us  [exchange_z(): lax.all_to_all(value, AXES, 0, 0, axis_index_groups=Z_GROUPS, tiled=True)]
  transfers between devices with their start and end apart: 3 -> 30, of which waited for: 3 -> 17; matrix products, arithmetic and copies ran while one was open for 2% -> 0% of each run, Pallas kernels for 0% -> 5%
where the time goes in v1:
time: 169 us
  waiting for transfers between devices  56.8 us (34%)
  starting transfers between devices  41.8 us (25%)
  Pallas kernels  32.9 us (19%)
  blocking collectives  27.5 us (16%)
  local copies, waits for them, and re-layouts  7.86 us (5%)
    ppermute x30, waiting for transfers between devices, send(): return lax.ppermute(value, AXES, permutation(target))  56.8 us
    ppermute x30, starting transfers between devices, send(): return lax.ppermute(value, AXES, permutation(target))  41.8 us
    all_to_all x2, blocking collectives, exchange_z(): lax.all_to_all(value, AXES, 0, 0, axis_index_groups=Z_GROUPS, tiled=True)  27.5 us
    pallas_call x4, Pallas kernels, attend(): pl.pallas_call(functools.partial(attend_kernel, step), grid_spec=pltpu.Pr...  18.6 us
    unnamed x22, local copies, waits for them, and re-layouts  7.77 us
    pallas_call x1, Pallas kernels, normalize(): pl.pallas_call(normalize_kernel, grid_spec=pltpu.PrefetchScalarGridSpec(n...  5 us
    pallas_call x1, Pallas kernels, down_grads(): pl.pallas_call(down_kernel, grid_spec=pltpu.PrefetchScalarGridSpec(num_sc...  4.03 us
  transfers between devices with their start and end apart: 30, of which 17 were waited for; matrix products, arithmetic and copies ran while one was open for 0% of the time, Pallas kernels for 5%

profile of v1, /device:TPU:1, one launch (start us, length us, event | category | flops | bytes accessed | tf_op | source)
XLA Modules:
  0.0 168.9 jit_solution(16689333089576577904)
XLA Ops:
  0.8 1.5 copy-done.1
  2.3 1.5 copy-done.3
  3.9 1.5 copy-done.5
  5.4 1.5 copy-done.7
  6.9 1.5 copy-done.9
  8.5 5.0 %normalize.1 = (bf16[192,2560]{1,0:T(8,128)(2,1)S(1)}, bf16[5,192,2560]{2,1,0:T(8,128)(2,1)}) custom-call(s32[4]{0:T(128)S(1)} %pad_add_fusion.place, bf16[192,5120]{1,0:T(8,128)(2,1)S(1)} %copy-done.9, bf16[192,5120]{1,0:T(8,128)(2,1)S(1)} %copy-done.1, bf16[192,5120]{1,0:T(8,128)(2,1)S(1)} %copy-done.3, bf16[192,5120]{1,0:T(8,128)(2,1)S(1)} %copy-done.5, ...), custom_call_target="tpu_custom_call" | custom-call | bytes 14000000 | tf_op jit(solution)/shard_map/normalize/pallas_call | solution.py:95
  13.5 3.2 %collective-permute-start = (bf16[5,192,2560]{2,1,0:T(8,128)(2,1)}, bf16[5,192,2560]{2,1,0:T(8,128)(2,1)}, u32[]{:S(2)}, u32[]{:S(2)}) collective-permute-start(bf16[5,192,2560]{2,1,0:T(8,128)(2,1)} %get-tuple-element.24), channel_id=1, source_target_pairs={{0,8},{8,0},{16,24},{24,16},{32,40},{40,32},{48,56},{56,48},{64,72... | collective-permute-start | bytes 14745608 | tf_op jit(solution)/shard_map/ppermute | solution.py:45
  16.7 1.1 collective-permute-start.5
  18.2 0.7 collective-permute-start.7
  18.9 3.8 %collective-permute-done.5 = bf16[640,128]{1,0:T(8,128)(2,1)S(1)} collective-permute-done((bf16[640,128]{1,0:T(8,128)(2,1)S(1)}, bf16[640,128]{1,0:T(8,128)(2,1)S(1)}, u32[]{:S(2)}, u32[]{:S(2)}) %collective-permute-start.5) | collective-permute-done | bytes 163872 | tf_op jit(solution)/shard_map/ppermute | solution.py:45
  22.7 2.2 %collective-permute-done.6 = bf16[640,128]{1,0:T(8,128)(2,1)S(1)} collective-permute-done((bf16[640,128]{1,0:T(8,128)(2,1)S(1)}, bf16[640,128]{1,0:T(8,128)(2,1)S(1)}, u32[]{:S(2)}, u32[]{:S(2)}) %collective-permute-start.6) | collective-permute-done | bytes 163872 | tf_op jit(solution)/shard_map/ppermute | solution.py:45
  24.9 4.1 %collective-permute-done.7 = bf16[640,128]{1,0:T(8,128)(2,1)S(1)} collective-permute-done((bf16[640,128]{1,0:T(8,128)(2,1)S(1)}, bf16[640,128]{1,0:T(8,128)(2,1)S(1)}, u32[]{:S(2)}, u32[]{:S(2)}) %collective-permute-start.7) | collective-permute-done | bytes 163872 | tf_op jit(solution)/shard_map/ppermute | solution.py:45
  29.0 3.1 %collective-permute-start.8 = (bf16[3,640,128]{2,1,0:T(8,128)(2,1)S(1)}, bf16[3,640,128]{2,1,0:T(8,128)(2,1)S(1)}, u32[]{:S(2)}, u32[]{:S(2)}) collective-permute-start(bf16[3,640,128]{2,1,0:T(8,128)(2,1)S(1)} %pad_maximum_fusion), channel_id=1, source_target_pairs={{0,0},{8,12},{16,16},{24,28},{32,32},{40,44},{48,48},{56,60},{64,6... | collective-permute-start | bytes 1474568 | tf_op jit(solution)/shard_map/ppermute | solution.py:45
  32.2 3.2 %collective-permute-start.3 = (bf16[1,640,128]{2,1,0:T(8,128)(2,1)S(1)}, bf16[1,640,128]{2,1,0:T(8,128)(2,1)S(1)}, u32[]{:S(2)}, u32[]{:S(2)}) collective-permute-start(bf16[1,640,128]{2,1,0:T(8,128)(2,1)S(1)} %constant_dynamic-slice_fusion), channel_id=1, source_target_pairs={{0,0},{8,12},{16,16},{24,28},{32,32},{40,44},{48,48},{56,60},{64,6... | collective-permute-start | bytes 491528 | tf_op jit(solution)/shard_map/ppermute | solution.py:45
  36.1 5.4 %collective-permute-done.3.own0 = bf16[1,640,128]{2,1,0:T(8,128)(2,1)S(1)} collective-permute-done((bf16[1,640,128]{2,1,0:T(8,128)(2,1)S(1)}, bf16[1,640,128]{2,1,0:T(8,128)(2,1)S(1)}, u32[]{:S(2)}, u32[]{:S(2)}) %collective-permute-start.3) | collective-permute-done | bytes 163872 | tf_op jit(solution)/shard_map/ppermute | solution.py:45
  42.2 2.6 %lower.1.refs_10_ = f32[2,2,200,128]{3,2,1,0:T(8,128)S(1)} custom-call(s32[4]{0:T(128)S(1)} %pad_add_fusion.place, bf16[192,2560]{1,0:T(8,128)(2,1)S(1)} %get-tuple-element.25.nown.n0, bf16[5,192,2560]{2,1,0:T(8,128)(2,1)} %collective-permute-done.npeer.refs_4_.refs_5_.refs_6_.refs_7_.n1, bf16[1,640,128]{2,1,0:T(8,128)(2,1)S(1)} %collective-permute-done.3.own0, ...), custom_call_target="tpu_custom_call" | custom-call | tf_op jit(solution)/shard_map/lower/pallas_call | solution.py:135
  45.5 1.0 collective-permute-start.13
  46.5 3.1 %collective-permute-start.1 = (bf16[1,128,640]{2,1,0:T(8,128)(2,1)S(1)}, bf16[1,128,640]{2,1,0:T(8,128)(2,1)S(1)}, u32[]{:S(2)}, u32[]{:S(2)}) collective-permute-start(bf16[1,128,640]{2,1,0:T(8,128)(2,1)S(1)} %constant_dynamic-slice_fusion.1), channel_id=1, source_target_pairs={{0,0},{8,12},{16,16},{24,28},{32,32},{40,44},{48,48},{56,60},{64,6... | collective-permute-start | bytes 491528 | tf_op jit(solution)/shard_map/ppermute | solution.py:45
  49.7 0.7 collective-permute-done.11
  50.3 2.2 %collective-permute-start.2 = (bf16[1,128,640]{2,1,0:T(8,128)(2,1)S(1)}, bf16[1,128,640]{2,1,0:T(8,128)(2,1)S(1)}, u32[]{:S(2)}, u32[]{:S(2)}) collective-permute-start(bf16[1,128,640]{2,1,0:T(8,128)(2,1)S(1)} %constant_dynamic-slice_fusion.1), channel_id=1, source_target_pairs={{0,140},{8,0},{16,156},{24,16},{32,172},{40,32},{48,188},{56,48},{... | collective-permute-start | bytes 491528 | tf_op jit(solution)/shard_map/ppermute | solution.py:45
  52.6 3.7 %collective-permute-done.13 = bf16[128,640]{1,0:T(8,128)(2,1)S(1)} collective-permute-done((bf16[128,640]{1,0:T(8,128)(2,1)S(1)}, bf16[128,640]{1,0:T(8,128)(2,1)S(1)}, u32[]{:S(2)}, u32[]{:S(2)}) %collective-permute-start.13) | collective-permute-done | bytes 163872 | tf_op jit(solution)/shard_map/ppermute | solution.py:45
  56.4 3.3 %collective-permute-start.14 = (bf16[3,128,640]{2,1,0:T(8,128)(2,1)S(1)}, bf16[3,128,640]{2,1,0:T(8,128)(2,1)S(1)}, u32[]{:S(2)}, u32[]{:S(2)}) collective-permute-start(bf16[3,128,640]{2,1,0:T(8,128)(2,1)S(1)} %pad_maximum_fusion.1), channel_id=1, source_target_pairs={{0,0},{8,12},{16,16},{24,28},{32,32},{40,44},{48,48},{56,60},{64,6... | collective-permute-start | bytes 1474568 | tf_op jit(solution)/shard_map/ppermute | solution.py:45
  59.8 4.7 %attend.4 = (bf16[4,8,40,128]{3,2,1,0:T(8,128)(2,1)S(1)}, f32[2,2,192,128]{3,2,1,0:T(8,128)S(1)}, bf16[2,384,128]{2,1,0:T(8,128)(2,1)S(1)}, f32[2,8,128]{2,1,0:T(8,128)S(1)}) custom-call(s32[4]{0:T(128)S(1)} %pad_add_fusion.place, bf16[192,5120]{1,0:T(8,128)(2,1)S(1)} %copy-done.2, bf16[192,5120]{1,0:T(8,128)(2,1)S(1)} %copy-done.4, ...), custom_call_target="tpu_custom_call" | custom-call | flops 4000000000 | bytes 3000000 | tf_op jit(solution)/shard_map/attend/pallas_call | solution.py:227
  64.5 2.7 %collective-permute-done.14.refs_8_ = bf16[3,128,640]{2,1,0:T(8,128)(2,1)S(1)} collective-permute-done((bf16[3,128,640]{2,1,0:T(8,128)(2,1)S(1)}, bf16[3,128,640]{2,1,0:T(8,128)(2,1)S(1)}, u32[]{:S(2)}, u32[]{:S(2)}) %collective-permute-start.14) | collective-permute-done | bytes 491552 | tf_op jit(solution)/shard_map/ppermute | solution.py:45
  67.2 0.8 collective-permute-done.15.refs_9_
  67.9 4.6 %attend.5 = (bf16[4,8,40,128]{3,2,1,0:T(8,128)(2,1)S(1)}, f32[2,2,192,128]{3,2,1,0:T(8,128)S(1)}) custom-call(s32[4]{0:T(128)S(1)} %pad_add_fusion.place, bf16[192,5120]{1,0:T(8,128)(2,1)S(1)} %copy-done.2, bf16[192,5120]{1,0:T(8,128)(2,1)S(1)} %copy-done.4, bf16[192,5120]{1,0:T(8,128)(2,1)S(1)} %copy-done.6, bf16[192,5120]{1,0:T(8,128)(2,1)S(1)} %copy-done.8, ...), custom_call_target="tpu_custom_call" | custom-call | flops 4000000000 | bytes 3000000 | tf_op jit(solution)/shard_map/attend/pallas_call | solution.py:227
  72.6 4.7 %attend.6 = (bf16[4,8,40,128]{3,2,1,0:T(8,128)(2,1)S(1)}, f32[2,2,192,128]{3,2,1,0:T(8,128)S(1)}) custom-call(s32[4]{0:T(128)S(1)} %pad_add_fusion.place, bf16[192,5120]{1,0:T(8,128)(2,1)S(1)} %copy-done.2, bf16[192,5120]{1,0:T(8,128)(2,1)S(1)} %copy-done.4, bf16[192,5120]{1,0:T(8,128)(2,1)S(1)} %copy-done.6, bf16[192,5120]{1,0:T(8,128)(2,1)S(1)} %copy-done.8, ...), custom_call_target="tpu_custom_call" | custom-call | flops 4000000000 | bytes 3000000 | tf_op jit(solution)/shard_map/attend/pallas_call | solution.py:227
  77.2 4.7 %attend.7 = (bf16[4,8,40,128]{3,2,1,0:T(8,128)(2,1)S(1)}, f32[2,2,192,128]{3,2,1,0:T(8,128)S(1)}) custom-call(s32[4]{0:T(128)S(1)} %pad_add_fusion.place, bf16[192,5120]{1,0:T(8,128)(2,1)S(1)} %copy-done.2, bf16[192,5120]{1,0:T(8,128)(2,1)S(1)} %copy-done.4, bf16[192,5120]{1,0:T(8,128)(2,1)S(1)} %copy-done.6, bf16[192,5120]{1,0:T(8,128)(2,1)S(1)} %copy-done.8, ...), custom_call_target="tpu_custom_call" | custom-call | flops 4000000000 | bytes 3000000 | tf_op jit(solution)/shard_map/attend/pallas_call | solution.py:227
  82.7 1.0 collective-permute-start.16
  83.8 4.0 %down_grads.1 = (bf16[4,8,40,128]{3,2,1,0:T(8,128)(2,1)S(1)}, bf16[4,8,40,128]{3,2,1,0:T(8,128)(2,1)S(1)}, bf16[4,8,40,128]{3,2,1,0:T(8,128)(2,1)S(1)}, bf16[4,8,40,128]{3,2,1,0:T(8,128)(2,1)S(1)}) custom-call(s32[4]{0:T(128)S(1)} %pad_add_fusion.place, bf16[192,2560]{1,0:T(8,128)(2,1)S(1)} %get-tuple-element.25.nown.n0, ...), custom_call_target="tpu_custom_call" | custom-call | flops 3000000000 | bytes 5000000 | tf_op jit(solution)/shard_map/down_grads/pallas_call | solution.py:277
  87.8 1.3 collective-permute-start.20
  89.2 2.4 %collective-permute-start.21 = (bf16[4,8,40,128]{3,2,1,0:T(8,128)(2,1)S(1)}, bf16[4,8,40,128]{3,2,1,0:T(8,128)(2,1)S(1)}, u32[]{:S(2)}, u32[]{:S(2)}) collective-permute-start(bf16[4,8,40,128]{3,2,1,0:T(8,128)(2,1)S(1)} %get-tuple-element.38), channel_id=1, source_target_pairs={{0,2},{8,10},{16,18},{24,26},{32,34},{40,42},{48,50},{56,58},{64,6... | collective-permute-start | bytes 983048 | tf_op jit(solution)/shard_map/ppermute | solution.py:45
  91.6 2.0 %collective-permute-start.22 = (bf16[4,8,40,128]{3,2,1,0:T(8,128)(2,1)S(1)}, bf16[4,8,40,128]{3,2,1,0:T(8,128)(2,1)S(1)}, u32[]{:S(2)}, u32[]{:S(2)}) collective-permute-start(bf16[4,8,40,128]{3,2,1,0:T(8,128)(2,1)S(1)} %get-tuple-element.39), channel_id=1, source_target_pairs={{0,3},{8,11},{16,19},{24,27},{32,35},{40,43},{48,51},{56,59},{64,6... | collective-permute-start | bytes 983048 | tf_op jit(solution)/shard_map/ppermute | solution.py:45
  93.5 7.0 %collective-permute-done.16.refs_1_ = bf16[4,8,40,128]{3,2,1,0:T(8,128)(2,1)S(1)} collective-permute-done((bf16[4,8,40,128]{3,2,1,0:T(8,128)(2,1)S(1)}, bf16[4,8,40,128]{3,2,1,0:T(8,128)(2,1)S(1)}, u32[]{:S(2)}, u32[]{:S(2)}) %collective-permute-start.16) | collective-permute-done | bytes 327712 | tf_op jit(solution)/shard_map/ppermute | solution.py:45
  100.6 7.6 %collective-permute-done.20.refs_5_ = bf16[4,8,40,128]{3,2,1,0:T(8,128)(2,1)S(1)} collective-permute-done((bf16[4,8,40,128]{3,2,1,0:T(8,128)(2,1)S(1)}, bf16[4,8,40,128]{3,2,1,0:T(8,128)(2,1)S(1)}, u32[]{:S(2)}, u32[]{:S(2)}) %collective-permute-start.20) | collective-permute-done | bytes 327712 | tf_op jit(solution)/shard_map/ppermute | solution.py:45
  108.2 5.8 %collective-permute-done.21.refs_6_ = bf16[4,8,40,128]{3,2,1,0:T(8,128)(2,1)S(1)} collective-permute-done((bf16[4,8,40,128]{3,2,1,0:T(8,128)(2,1)S(1)}, bf16[4,8,40,128]{3,2,1,0:T(8,128)(2,1)S(1)}, u32[]{:S(2)}, u32[]{:S(2)}) %collective-permute-start.21) | collective-permute-done | bytes 327712 | tf_op jit(solution)/shard_map/ppermute | solution.py:45
  114.0 0.9 sum_y.1
  114.9 2.0 %collective-permute-start.23 = (bf16[8,80,128]{2,1,0:T(8,128)(2,1)S(1)}, bf16[8,80,128]{2,1,0:T(8,128)(2,1)S(1)}, u32[]{:S(2)}, u32[]{:S(2)}) collective-permute-start(bf16[8,80,128]{2,1,0:T(8,128)(2,1)S(1)} %get-tuple-element.41), channel_id=1, source_target_pairs={{0,12},{8,4},{16,28},{24,20},{32,44},{40,36},{48,60},{56,52},{64,7... | collective-permute-start | bytes 491528 | tf_op jit(solution)/shard_map/ppermute | solution.py:45
  116.9 2.9 %collective-permute-start.24 = (bf16[8,80,128]{2,1,0:T(8,128)(2,1)S(1)}, bf16[8,80,128]{2,1,0:T(8,128)(2,1)S(1)}, u32[]{:S(2)}, u32[]{:S(2)}) collective-permute-start(bf16[8,80,128]{2,1,0:T(8,128)(2,1)S(1)} %get-tuple-element.42), channel_id=1, source_target_pairs={{0,128},{8,136},{16,144},{24,152},{32,160},{40,168},{48,176},{56,1... | collective-permute-start | bytes 491528 | tf_op jit(solution)/shard_map/ppermute | solution.py:45
  120.2 2.9 %collective-permute-done.23 = bf16[8,80,128]{2,1,0:T(8,128)(2,1)S(1)} collective-permute-done((bf16[8,80,128]{2,1,0:T(8,128)(2,1)S(1)}, bf16[8,80,128]{2,1,0:T(8,128)(2,1)S(1)}, u32[]{:S(2)}, u32[]{:S(2)}) %collective-permute-start.23) | collective-permute-done | bytes 163872 | tf_op jit(solution)/shard_map/ppermute | solution.py:45
  123.1 4.2 %collective-permute-done.24 = bf16[8,80,128]{2,1,0:T(8,128)(2,1)S(1)} collective-permute-done((bf16[8,80,128]{2,1,0:T(8,128)(2,1)S(1)}, bf16[8,80,128]{2,1,0:T(8,128)(2,1)S(1)}, u32[]{:S(2)}, u32[]{:S(2)}) %collective-permute-start.24) | collective-permute-done | bytes 163872 | tf_op jit(solution)/shard_map/ppermute | solution.py:45
  127.4 16.8 %all_to_all.10 = bf16[8,80,128]{2,1,0:T(8,128)(2,1)S(1)} all-to-all(bf16[8,80,128]{2,1,0:T(8,128)(2,1)S(1)} %add_convert_fusion), channel_id=1, replica_groups={{0,16,32,48,64,80,96,112},{8,24,40,56,72,88,104,120},{1,17,33,49,65,81,..., dimensions={0} | all-to-all | bytes 327680 | tf_op jit(solution)/shard_map/all_to_all | solution.py:65
  144.3 10.7 %all_to_all.11.own = bf16[8,80,128]{2,1,0:T(8,128)(2,1)S(1)} all-to-all(bf16[8,80,128]{2,1,0:T(8,128)(2,1)S(1)} %broadcast_in_dim.9), channel_id=1, replica_groups={{0,16,32,48,64,80,96,112},{8,24,40,56,72,88,104,120},{1,17,33,49,65,81,..., dimensions={0} | all-to-all | bytes 327680 | tf_op jit(solution)/shard_map/all_to_all | solution.py:65
  155.0 4.8 %collective-permute-start.26 = (bf16[8,80,128]{2,1,0:T(8,128)(2,1)S(1)}, bf16[8,80,128]{2,1,0:T(8,128)(2,1)S(1)}, u32[]{:S(2)}, u32[]{:S(2)}) collective-permute-start(bf16[8,80,128]{2,1,0:T(8,128)(2,1)S(1)} %all_to_all.11.own), channel_id=1, source_target_pairs={{0,136},{8,4},{16,152},{24,20},{32,168},{40,36},{48,184},{56,52},{... | collective-permute-start | bytes 491528 | tf_op jit(solution)/shard_map/ppermute | solution.py:45
  160.4 3.8 %collective-permute-done.26.first = bf16[8,80,128]{2,1,0:T(8,128)(2,1)S(1)} collective-permute-done((bf16[8,80,128]{2,1,0:T(8,128)(2,1)S(1)}, bf16[8,80,128]{2,1,0:T(8,128)(2,1)S(1)}, u32[]{:S(2)}, u32[]{:S(2)}) %collective-permute-start.26) | collective-permute-done | bytes 163872 | tf_op jit(solution)/shard_map/ppermute | solution.py:45
  164.2 1.5 collective-permute-start.28
  165.7 1.0 collective-permute-done.28.first_peer
  167.1 1.7 %finish.1 = (f32[2,640,128]{2,1,0:T(8,128)}, f32[32,8,640]{2,1,0:T(8,128)}) custom-call(s32[4]{0:T(128)S(1)} %pad_add_fusion.place, bf16[8,80,128]{2,1,0:T(8,128)(2,1)S(1)} %all_to_all.11.own, bf16[8,80,128]{2,1,0:T(8,128)(2,1)S(1)} %collective-permute-done.26.first, bf16[8,80,128]{2,1,0:T(8,128)(2,1)S(1)} %collective-permute-done.27.second, ...), custom_call_target="tpu_custom_call" | custom-call | tf_op jit(solution)/shard_map/finish/pallas_call | solution.py:351
  (56 shorter events, 4.2 us)
Async XLA Ops:
  0.6 16.1 %copy-start = (bf16[2,640,128]{2,1,0:T(8,128)(2,1)S(1)}, bf16[2,640,128]{2,1,0:T(8,128)(2,1)}, u32[]{:S(2)}) copy-start(bf16[2,640,128]{2,1,0:T(8,128)(2,1)} %param.14) | copy-start | bytes 983044
  0.8 1.5 copy-start.1
  2.3 1.5 copy-start.3
  3.9 1.5 copy-start.5
  5.4 1.5 copy-start.7
  6.9 1.5 copy-start.9
  13.5 28.7 %collective-permute-start = (bf16[5,192,2560]{2,1,0:T(8,128)(2,1)}, bf16[5,192,2560]{2,1,0:T(8,128)(2,1)}, u32[]{:S(2)}, u32[]{:S(2)}) collective-permute-start(bf16[5,192,2560]{2,1,0:T(8,128)(2,1)} %get-tuple-element.24), channel_id=1, source_target_pairs={{0,8},{8,0},{16,24},{24,16},{32,40},{40,32},{48,56},{56,48},{64,72... | collective-permute-start | bytes 14745608 | tf_op jit(solution)/shard_map/ppermute | solution.py:45
  16.7 5.9 %collective-permute-start.5 = (bf16[640,128]{1,0:T(8,128)(2,1)S(1)}, bf16[640,128]{1,0:T(8,128)(2,1)S(1)}, u32[]{:S(2)}, u32[]{:S(2)}) collective-permute-start(bf16[640,128]{1,0:T(8,128)(2,1)S(1)} %fusion.1), channel_id=1, source_target_pairs={{0,3},{8,11},{16,19},{24,27},{32,35},{40,43},{48,51},{56,59},{64,6... | collective-permute-start | bytes 491528 | tf_op jit(solution)/shard_map/ppermute | solution.py:45
  17.8 7.1 %collective-permute-start.6 = (bf16[640,128]{1,0:T(8,128)(2,1)S(1)}, bf16[640,128]{1,0:T(8,128)(2,1)S(1)}, u32[]{:S(2)}, u32[]{:S(2)}) collective-permute-start(bf16[640,128]{1,0:T(8,128)(2,1)S(1)} %fusion.1), channel_id=1, source_target_pairs={{0,2},{8,10},{16,18},{24,26},{32,34},{40,42},{48,50},{56,58},{64,6... | collective-permute-start | bytes 491528 | tf_op jit(solution)/shard_map/ppermute | solution.py:45
  18.2 10.8 %collective-permute-start.7 = (bf16[640,128]{1,0:T(8,128)(2,1)S(1)}, bf16[640,128]{1,0:T(8,128)(2,1)S(1)}, u32[]{:S(2)}, u32[]{:S(2)}) collective-permute-start(bf16[640,128]{1,0:T(8,128)(2,1)S(1)} %fusion.1), channel_id=1, source_target_pairs={{0,1},{8,9},{16,17},{24,25},{32,33},{40,41},{48,49},{56,57},{64,65... | collective-permute-start | bytes 491528 | tf_op jit(solution)/shard_map/ppermute | solution.py:45
  29.0 13.2 %collective-permute-start.8 = (bf16[3,640,128]{2,1,0:T(8,128)(2,1)S(1)}, bf16[3,640,128]{2,1,0:T(8,128)(2,1)S(1)}, u32[]{:S(2)}, u32[]{:S(2)}) collective-permute-start(bf16[3,640,128]{2,1,0:T(8,128)(2,1)S(1)} %pad_maximum_fusion), channel_id=1, source_target_pairs={{0,0},{8,12},{16,16},{24,28},{32,32},{40,44},{48,48},{56,60},{64,6... | collective-permute-start | bytes 1474568 | tf_op jit(solution)/shard_map/ppermute | solution.py:45
  32.2 10.0 %collective-permute-start.9 = (bf16[3,640,128]{2,1,0:T(8,128)(2,1)S(1)}, bf16[3,640,128]{2,1,0:T(8,128)(2,1)S(1)}, u32[]{:S(2)}, u32[]{:S(2)}) collective-permute-start(bf16[3,640,128]{2,1,0:T(8,128)(2,1)S(1)} %pad_maximum_fusion), channel_id=1, source_target_pairs={{0,140},{8,0},{16,156},{24,16},{32,172},{40,32},{48,188},{56,48},{... | collective-permute-start | bytes 1474568 | tf_op jit(solution)/shard_map/ppermute | solution.py:45
  32.2 12.8 %copy-start.10 = (bf16[2,128,640]{2,1,0:T(8,128)(2,1)S(1)}, bf16[2,128,640]{2,1,0:T(8,128)(2,1)}, u32[]{:S(2)}) copy-start(bf16[2,128,640]{2,1,0:T(8,128)(2,1)} %param.15) | copy-start | bytes 983044
  32.2 9.3 %collective-permute-start.3 = (bf16[1,640,128]{2,1,0:T(8,128)(2,1)S(1)}, bf16[1,640,128]{2,1,0:T(8,128)(2,1)S(1)}, u32[]{:S(2)}, u32[]{:S(2)}) collective-permute-start(bf16[1,640,128]{2,1,0:T(8,128)(2,1)S(1)} %constant_dynamic-slice_fusion), channel_id=1, source_target_pairs={{0,0},{8,12},{16,16},{24,28},{32,32},{40,44},{48,48},{56,60},{64,6... | collective-permute-start | bytes 491528 | tf_op jit(solution)/shard_map/ppermute | solution.py:45
  35.5 6.7 %collective-permute-start.4 = (bf16[1,640,128]{2,1,0:T(8,128)(2,1)S(1)}, bf16[1,640,128]{2,1,0:T(8,128)(2,1)S(1)}, u32[]{:S(2)}, u32[]{:S(2)}) collective-permute-start(bf16[1,640,128]{2,1,0:T(8,128)(2,1)S(1)} %constant_dynamic-slice_fusion), channel_id=1, source_target_pairs={{0,140},{8,0},{16,156},{24,16},{32,172},{40,32},{48,188},{56,48},{... | collective-permute-start | bytes 491528 | tf_op jit(solution)/shard_map/ppermute | solution.py:45
  42.2 17.5 %copy-start.2 = (bf16[192,5120]{1,0:T(8,128)(2,1)S(1)}, bf16[192,5120]{1,0:T(8,128)(2,1)}, u32[]{:S(2)}) copy-start(bf16[192,5120]{1,0:T(8,128)(2,1)} %refs_0_.7) | copy-start | bytes 5898244
  42.2 17.5 %copy-start.4 = (bf16[192,5120]{1,0:T(8,128)(2,1)S(1)}, bf16[192,5120]{1,0:T(8,128)(2,1)}, u32[]{:S(2)}) copy-start(bf16[192,5120]{1,0:T(8,128)(2,1)} %refs_1_.7) | copy-start | bytes 5898244
  42.2 17.5 %copy-start.6 = (bf16[192,5120]{1,0:T(8,128)(2,1)S(1)}, bf16[192,5120]{1,0:T(8,128)(2,1)}, u32[]{:S(2)}) copy-start(bf16[192,5120]{1,0:T(8,128)(2,1)} %refs_2_.7) | copy-start | bytes 5898244
  42.2 17.5 %copy-start.8 = (bf16[192,5120]{1,0:T(8,128)(2,1)S(1)}, bf16[192,5120]{1,0:T(8,128)(2,1)}, u32[]{:S(2)}) copy-start(bf16[192,5120]{1,0:T(8,128)(2,1)} %refs_3_.7) | copy-start | bytes 5898244
  44.8 14.9 %collective-permute-start.10 = (f32[2,2,200,128]{3,2,1,0:T(8,128)S(1)}, f32[2,2,200,128]{3,2,1,0:T(8,128)S(1)}, u32[]{:S(2)}, u32[]{:S(2)}) collective-permute-start(f32[2,2,200,128]{3,2,1,0:T(8,128)S(1)} %lower.1.refs_10_), channel_id=1, source_target_pairs={{0,8},{8,0},{16,24},{24,16},{32,40},{40,32},{48,56},{56,48},{64,72... | collective-permute-start | bytes 1228808 | tf_op jit(solution)/shard_map/ppermute | solution.py:45
  45.0 5.4 %collective-permute-start.11 = (bf16[128,640]{1,0:T(8,128)(2,1)S(1)}, bf16[128,640]{1,0:T(8,128)(2,1)S(1)}, u32[]{:S(2)}, u32[]{:S(2)}) collective-permute-start(bf16[128,640]{1,0:T(8,128)(2,1)S(1)} %fusion), channel_id=1, source_target_pairs={{0,3},{8,11},{16,19},{24,27},{32,35},{40,43},{48,51},{56,59},{64,6... | collective-permute-start | bytes 491528 | tf_op jit(solution)/shard_map/ppermute | solution.py:45
  45.1 7.5 %collective-permute-start.12 = (bf16[128,640]{1,0:T(8,128)(2,1)S(1)}, bf16[128,640]{1,0:T(8,128)(2,1)S(1)}, u32[]{:S(2)}, u32[]{:S(2)}) collective-permute-start(bf16[128,640]{1,0:T(8,128)(2,1)S(1)} %fusion), channel_id=1, source_target_pairs={{0,2},{8,10},{16,18},{24,26},{32,34},{40,42},{48,50},{56,58},{64,6... | collective-permute-start | bytes 491528 | tf_op jit(solution)/shard_map/ppermute | solution.py:45
  45.5 10.8 %collective-permute-start.13 = (bf16[128,640]{1,0:T(8,128)(2,1)S(1)}, bf16[128,640]{1,0:T(8,128)(2,1)S(1)}, u32[]{:S(2)}, u32[]{:S(2)}) collective-permute-start(bf16[128,640]{1,0:T(8,128)(2,1)S(1)} %fusion), channel_id=1, source_target_pairs={{0,1},{8,9},{16,17},{24,25},{32,33},{40,41},{48,49},{56,57},{64,65... | collective-permute-start | bytes 491528 | tf_op jit(solution)/shard_map/ppermute | solution.py:45
  46.5 13.2 %collective-permute-start.1 = (bf16[1,128,640]{2,1,0:T(8,128)(2,1)S(1)}, bf16[1,128,640]{2,1,0:T(8,128)(2,1)S(1)}, u32[]{:S(2)}, u32[]{:S(2)}) collective-permute-start(bf16[1,128,640]{2,1,0:T(8,128)(2,1)S(1)} %constant_dynamic-slice_fusion.1), channel_id=1, source_target_pairs={{0,0},{8,12},{16,16},{24,28},{32,32},{40,44},{48,48},{56,60},{64,6... | collective-permute-start | bytes 491528 | tf_op jit(solution)/shard_map/ppermute | solution.py:45
  50.3 9.4 %collective-permute-start.2 = (bf16[1,128,640]{2,1,0:T(8,128)(2,1)S(1)}, bf16[1,128,640]{2,1,0:T(8,128)(2,1)S(1)}, u32[]{:S(2)}, u32[]{:S(2)}) collective-permute-start(bf16[1,128,640]{2,1,0:T(8,128)(2,1)S(1)} %constant_dynamic-slice_fusion.1), channel_id=1, source_target_pairs={{0,140},{8,0},{16,156},{24,16},{32,172},{40,32},{48,188},{56,48},{... | collective-permute-start | bytes 491528 | tf_op jit(solution)/shard_map/ppermute | solution.py:45
  56.4 10.8 %collective-permute-start.14 = (bf16[3,128,640]{2,1,0:T(8,128)(2,1)S(1)}, bf16[3,128,640]{2,1,0:T(8,128)(2,1)S(1)}, u32[]{:S(2)}, u32[]{:S(2)}) collective-permute-start(bf16[3,128,640]{2,1,0:T(8,128)(2,1)S(1)} %pad_maximum_fusion.1), channel_id=1, source_target_pairs={{0,0},{8,12},{16,16},{24,28},{32,32},{40,44},{48,48},{56,60},{64,6... | collective-permute-start | bytes 1474568 | tf_op jit(solution)/shard_map/ppermute | solution.py:45
  59.7 8.3 %collective-permute-start.15 = (bf16[3,128,640]{2,1,0:T(8,128)(2,1)S(1)}, bf16[3,128,640]{2,1,0:T(8,128)(2,1)S(1)}, u32[]{:S(2)}, u32[]{:S(2)}) collective-permute-start(bf16[3,128,640]{2,1,0:T(8,128)(2,1)S(1)} %pad_maximum_fusion.1), channel_id=1, source_target_pairs={{0,140},{8,0},{16,156},{24,16},{32,172},{40,32},{48,188},{56,48},{... | collective-permute-start | bytes 1474568 | tf_op jit(solution)/shard_map/ppermute | solution.py:45
  81.9 1.9 %collective-permute-start.19 = (f32[2,2,192,128]{3,2,1,0:T(8,128)S(1)}, f32[2,2,192,128]{3,2,1,0:T(8,128)S(1)}, u32[]{:S(2)}, u32[]{:S(2)}) collective-permute-start(f32[2,2,192,128]{3,2,1,0:T(8,128)S(1)} %get-tuple-element.35.mine), channel_id=1, source_target_pairs={{0,8},{8,0},{16,24},{24,16},{32,40},{40,32},{48,56},{56,48},{64,72... | collective-permute-start | bytes 1179656 | tf_op jit(solution)/shard_map/ppermute | solution.py:45
  82.0 9.6 %collective-permute-start.18 = (bf16[4,8,40,128]{3,2,1,0:T(8,128)(2,1)S(1)}, bf16[4,8,40,128]{3,2,1,0:T(8,128)(2,1)S(1)}, u32[]{:S(2)}, u32[]{:S(2)}) collective-permute-start(bf16[4,8,40,128]{3,2,1,0:T(8,128)(2,1)S(1)} %get-tuple-element.34), channel_id=1, source_target_pairs={{0,3},{8,11},{16,19},{24,27},{32,35},{40,43},{48,51},{56,59},{64,6... | collective-permute-start | bytes 983048 | tf_op jit(solution)/shard_map/ppermute | solution.py:45
  82.3 11.2 %collective-permute-start.17 = (bf16[4,8,40,128]{3,2,1,0:T(8,128)(2,1)S(1)}, bf16[4,8,40,128]{3,2,1,0:T(8,128)(2,1)S(1)}, u32[]{:S(2)}, u32[]{:S(2)}) collective-permute-start(bf16[4,8,40,128]{3,2,1,0:T(8,128)(2,1)S(1)} %get-tuple-element.32), channel_id=1, source_target_pairs={{0,2},{8,10},{16,18},{24,26},{32,34},{40,42},{48,50},{56,58},{64,6... | collective-permute-start | bytes 983048 | tf_op jit(solution)/shard_map/ppermute | solution.py:45
  82.7 17.8 %collective-permute-start.16 = (bf16[4,8,40,128]{3,2,1,0:T(8,128)(2,1)S(1)}, bf16[4,8,40,128]{3,2,1,0:T(8,128)(2,1)S(1)}, u32[]{:S(2)}, u32[]{:S(2)}) collective-permute-start(bf16[4,8,40,128]{3,2,1,0:T(8,128)(2,1)S(1)} %get-tuple-element.30), channel_id=1, source_target_pairs={{0,1},{8,9},{16,17},{24,25},{32,33},{40,41},{48,49},{56,57},{64,65... | collective-permute-start | bytes 983048 | tf_op jit(solution)/shard_map/ppermute | solution.py:45
  87.8 20.4 %collective-permute-start.20 = (bf16[4,8,40,128]{3,2,1,0:T(8,128)(2,1)S(1)}, bf16[4,8,40,128]{3,2,1,0:T(8,128)(2,1)S(1)}, u32[]{:S(2)}, u32[]{:S(2)}) collective-permute-start(bf16[4,8,40,128]{3,2,1,0:T(8,128)(2,1)S(1)} %get-tuple-element.37), channel_id=1, source_target_pairs={{0,1},{8,9},{16,17},{24,25},{32,33},{40,41},{48,49},{56,57},{64,65... | collective-permute-start | bytes 983048 | tf_op jit(solution)/shard_map/ppermute | solution.py:45
  89.2 24.8 %collective-permute-start.21 = (bf16[4,8,40,128]{3,2,1,0:T(8,128)(2,1)S(1)}, bf16[4,8,40,128]{3,2,1,0:T(8,128)(2,1)S(1)}, u32[]{:S(2)}, u32[]{:S(2)}) collective-permute-start(bf16[4,8,40,128]{3,2,1,0:T(8,128)(2,1)S(1)} %get-tuple-element.38), channel_id=1, source_target_pairs={{0,2},{8,10},{16,18},{24,26},{32,34},{40,42},{48,50},{56,58},{64,6... | collective-permute-start | bytes 983048 | tf_op jit(solution)/shard_map/ppermute | solution.py:45
  91.6 22.4 %collective-permute-start.22 = (bf16[4,8,40,128]{3,2,1,0:T(8,128)(2,1)S(1)}, bf16[4,8,40,128]{3,2,1,0:T(8,128)(2,1)S(1)}, u32[]{:S(2)}, u32[]{:S(2)}) collective-permute-start(bf16[4,8,40,128]{3,2,1,0:T(8,128)(2,1)S(1)} %get-tuple-element.39), channel_id=1, source_target_pairs={{0,3},{8,11},{16,19},{24,27},{32,35},{40,43},{48,51},{56,59},{64,6... | collective-permute-start | bytes 983048 | tf_op jit(solution)/shard_map/ppermute | solution.py:45
  114.9 8.3 %collective-permute-start.23 = (bf16[8,80,128]{2,1,0:T(8,128)(2,1)S(1)}, bf16[8,80,128]{2,1,0:T(8,128)(2,1)S(1)}, u32[]{:S(2)}, u32[]{:S(2)}) collective-permute-start(bf16[8,80,128]{2,1,0:T(8,128)(2,1)S(1)} %get-tuple-element.41), channel_id=1, source_target_pairs={{0,12},{8,4},{16,28},{24,20},{32,44},{40,36},{48,60},{56,52},{64,7... | collective-permute-start | bytes 491528 | tf_op jit(solution)/shard_map/ppermute | solution.py:45
  116.9 10.4 %collective-permute-start.24 = (bf16[8,80,128]{2,1,0:T(8,128)(2,1)S(1)}, bf16[8,80,128]{2,1,0:T(8,128)(2,1)S(1)}, u32[]{:S(2)}, u32[]{:S(2)}) collective-permute-start(bf16[8,80,128]{2,1,0:T(8,128)(2,1)S(1)} %get-tuple-element.42), channel_id=1, source_target_pairs={{0,128},{8,136},{16,144},{24,152},{32,160},{40,168},{48,176},{56,1... | collective-permute-start | bytes 491528 | tf_op jit(solution)/shard_map/ppermute | solution.py:45
  119.8 7.5 %collective-permute-start.25 = (bf16[8,80,128]{2,1,0:T(8,128)(2,1)S(1)}, bf16[8,80,128]{2,1,0:T(8,128)(2,1)S(1)}, u32[]{:S(2)}, u32[]{:S(2)}) collective-permute-start(bf16[8,80,128]{2,1,0:T(8,128)(2,1)S(1)} %get-tuple-element.43), channel_id=1, source_target_pairs={{0,140},{8,132},{16,156},{24,148},{32,172},{40,164},{48,188},{56,1... | collective-permute-start | bytes 491528 | tf_op jit(solution)/shard_map/ppermute | solution.py:45
  155.0 9.2 %collective-permute-start.26 = (bf16[8,80,128]{2,1,0:T(8,128)(2,1)S(1)}, bf16[8,80,128]{2,1,0:T(8,128)(2,1)S(1)}, u32[]{:S(2)}, u32[]{:S(2)}) collective-permute-start(bf16[8,80,128]{2,1,0:T(8,128)(2,1)S(1)} %all_to_all.11.own), channel_id=1, source_target_pairs={{0,136},{8,4},{16,152},{24,20},{32,168},{40,36},{48,184},{56,52},{... | collective-permute-start | bytes 491528 | tf_op jit(solution)/shard_map/ppermute | solution.py:45
  159.9 5.8 %collective-permute-start.27 = (bf16[8,80,128]{2,1,0:T(8,128)(2,1)S(1)}, bf16[8,80,128]{2,1,0:T(8,128)(2,1)S(1)}, u32[]{:S(2)}, u32[]{:S(2)}) collective-permute-start(bf16[8,80,128]{2,1,0:T(8,128)(2,1)S(1)} %all_to_all.11.own), channel_id=1, source_target_pairs={{0,8},{8,132},{16,24},{24,148},{32,40},{40,164},{48,56},{56,180},{... | collective-permute-start | bytes 491528 | tf_op jit(solution)/shard_map/ppermute | solution.py:45
  164.2 2.6 %collective-permute-start.28 = (bf16[8,80,128]{2,1,0:T(8,128)(2,1)S(1)}, bf16[8,80,128]{2,1,0:T(8,128)(2,1)S(1)}, u32[]{:S(2)}, u32[]{:S(2)}) collective-permute-start(bf16[8,80,128]{2,1,0:T(8,128)(2,1)S(1)} %collective-permute-done.26.first), channel_id=1, source_target_pairs={{0,8},{8,0},{16,24},{24,16},{32,40},{40,32},{48,56},{56,48},{64,72... | collective-permute-start | bytes 491528 | tf_op jit(solution)/shard_map/ppermute | solution.py:45
  165.7 1.4 collective-permute-start.29

commit v2 on v1

--- a/solution.py
+++ b/solution.py
@@ -24,6 +24,7 @@
 LOCAL_HEADS = SHARD // HEAD
 NORM_ROWS = 32
 VMEM_LIMIT = 24 * 1024 * 1024
+SMALL = pl.CostEstimate(flops=1000, bytes_accessed=1000, transcendentals=0)
 
 
 def linear(x, y, z, c):
@@ -61,6 +62,19 @@
 ]
 
 
+def scatter_x(parts):
+    return [
+        parts[0],
+        send(parts[1], lambda x, y, z, c: (x + 1, y, z, 1 - c)),
+        send(parts[2], lambda x, y, z, c: (x + 2, y, z, c)),
+        send(parts[3], lambda x, y, z, c: (x - 1, y, z, 1 - c)),
+    ]
+
+
+def scatter_y(parts):
+    return [parts[0]] + [send_y(parts[step], step) for step in range(1, NY)]
+
+
 def exchange_z(value):
     return lax.all_to_all(value, AXES, 0, 0, axis_index_groups=Z_GROUPS, tiled=True)
 
@@ -79,10 +93,10 @@
     for start in range(0, NORM_ROWS, 16):
         rows = slice(start, start + 16)
         inputs = states[rows, :].astype(F32)
-        center = inputs - jnp.mean(inputs, axis=1, keepdims=True)
+        mean = jnp.mean(inputs, axis=1, keepdims=True)
+        center = inputs - mean
         spread = jnp.mean(center * center, axis=1, keepdims=True)
         inverse = lax.rsqrt(spread + 1e-06)
-        mean = jnp.mean(inputs, axis=1, keepdims=True)
         for begin, out in ((mine, nown), (other, nsend.at[4])):
             part = states[rows, pl.ds(begin, HALF)].astype(F32)
             out[rows, :] = ((part - mean) * inverse).astype(BF16)
@@ -107,13 +121,13 @@
             jax.ShapeDtypeStruct((CLIP, HALF), BF16),
             jax.ShapeDtypeStruct((5, CLIP, HALF), BF16),
         ),
-        compiler_params=pltpu.CompilerParams(vmem_limit_bytes=VMEM_LIMIT),
-        cost_estimate=pl.CostEstimate(flops=0, bytes_accessed=14000000, transcendentals=0),
+        compiler_params=pltpu.CompilerParams(vmem_limit_bytes=60 * 1024 * 1024),
+        cost_estimate=SMALL,
         name="normalize",
     )(place, states, q, k, v, g)
 
 
-def lower_kernel(place, nown, npeer, own0, other0, own, other, weight, out):
+def lower_kernel(place, nown, npeer, own, other, weight, out0, out1):
     core, y = place[2], place[1]
     for clip in range(2):
         totals = [jnp.zeros((CLIP, RANK), F32) for _ in range(2)]
@@ -123,48 +137,49 @@
                 rows = nown[:, pl.ds(start, SHARD)]
             else:
                 rows = npeer[0, :, pl.ds(start, SHARD)]
-            totals[0] += dot(rows, own[step - 1] if step else own0[0], 1, 0)
-            totals[1] += dot(rows, other[step - 1] if step else other0[0], 1, 0)
-        out[clip, core, :CLIP] = totals[0]
-        out[clip, 1 - core, :CLIP] = totals[1]
-        out[clip, 0, CLIP:] = weight[...]
-        out[clip, 1, CLIP:] = weight[...]
+            totals[0] += dot(rows, own[step], 1, 0)
+            totals[1] += dot(rows, other[step], 1, 0)
+        out = (out0, out1)[clip]
+        out[core, :CLIP] = totals[0]
+        out[1 - core, :CLIP] = totals[1]
+        out[0, CLIP:] = weight[...]
+        out[1, CLIP:] = weight[...]
 
 
 def lower(place, nown, peer, *downs_and_weight):
     return pl.pallas_call(
         lower_kernel,
         grid=(1,),
-        out_shape=jax.ShapeDtypeStruct((2, 2, CLIP + 8, RANK), F32),
+        out_shape=[jax.ShapeDtypeStruct((2, CLIP + 8, RANK), F32)] * 2,
         in_specs=[
             pl.BlockSpec(memory_space=pltpu.SMEM),
             whole((CLIP, HALF)),
             pl.BlockSpec((1, CLIP, HALF), lambda i: (4, 0, 0)),
         ]
         + [whole(a.shape) for a in downs_and_weight],
-        out_specs=whole((2, 2, CLIP + 8, RANK)),
+        out_specs=[whole((2, CLIP + 8, RANK))] * 2,
         compiler_params=pltpu.CompilerParams(vmem_limit_bytes=VMEM_LIMIT),
         name="lower",
     )(place, nown, peer, *downs_and_weight)
 
 
-def attend_kernel(step, place, *refs):
-    q0, k0, v0, g0, q1, k1, v1, g1, up_own, up_other = refs[:10]
-    if step == 0:
-        low_mine, low_peer, gup, dlow, low, weights, ups, dqs, dvs = refs[10:]
+def attend_kernel(first, after, place, *refs):
+    q0, k0, v0, g0, q1, k1, v1, g1, up = refs[:9]
+    refs = refs[9 + after :]
+    if first:
+        mine0, mine1, peer0, peer1, gup, dlow0, dlow1, low, weights, ups, dqs, dvs = refs
         for j in range(2):
             for clip in range(2):
-                total = low_mine[clip, j, :CLIP] + low_peer[1 - clip, j, :CLIP]
+                total = (mine0, mine1)[clip][j, :CLIP] + (peer1, peer0)[clip][j, :CLIP]
                 low[j, clip * CLIP : (clip + 1) * CLIP] = total.astype(BF16)
-        weights[0] = low_mine[0, 0, CLIP:]
-        weights[1] = low_peer[0, 0, CLIP:]
+        weights[0] = mine0[0, CLIP:]
+        weights[1] = peer0[0, CLIP:]
     else:
-        low, weights, dlow_in, gup, dlow, ups, dqs, dvs = refs[10:]
+        low, weights, in0, in1, gup, dlow0, dlow1, ups, dqs, dvs = refs
     core = place[2]
     scale = 1.0 / math.sqrt(HEAD)
-    slot = 0 if up_own.shape[0] == 1 else step - 1
-    ups[core] = up_own[slot]
-    ups[1 - core] = up_other[slot]
+    ups[core] = up[0]
+    ups[1 - core] = up[1]
     for clip in range(2):
         rows = slice(clip * CLIP, (clip + 1) * CLIP)
         weight = weights[clip, :1]
@@ -191,25 +206,28 @@
         for clip in range(2):
             rows = slice(clip * CLIP, (clip + 1) * CLIP)
             total = dot(grads[rows], ups[j], 1, 1)
-            dlow[clip, j] = total if step == 0 else dlow_in[clip, j] + total
+            out = (dlow0, dlow1)[clip]
+            out[j] = total if first else (in0, in1)[clip][j] + total
         store_pieces(gup, j, dot(low[j], grads[...], 0, 0))
+
+
+def lane_blocks(rows):
+    return jnp.concatenate(
+        [rows[:, h * HEAD : (h + 1) * HEAD] for h in range(LOCAL_HEADS)], axis=0
+    )
 
 
 def store_pieces(out, j, total):
     for piece in range(RANK // 8):
-        part = total[piece * 8 : (piece + 1) * 8]
-        part = jnp.concatenate(
-            [part[:, h * HEAD : (h + 1) * HEAD] for h in range(LOCAL_HEADS)], axis=0
-        )
         at = j * (RANK // 8) + piece
-        out[at // NZ, at % NZ] = part.astype(BF16)
+        out[at // NZ, at % NZ] = lane_blocks(total[piece * 8 : (piece + 1) * 8]).astype(BF16)
 
 
 PIECES = (4, NZ, 40, 128)
-LOWS = (2, 2, CLIP, RANK)
-
-
-def attend(step, place, arrays, peer, up_own, up_other, *lows):
+LOWS = (2, CLIP, RANK)
+
+
+def attend(step, after, place, arrays, peer, ups, *lows):
     def shard(place):
         return lax.rem(place[1] + step, NY)
 
@@ -218,20 +236,23 @@
         pl.BlockSpec((1, CLIP, SHARD), lambda i, place, n=n: (n, 0, shard(place)))
         for n in range(4)
     ]
-    out_shape = [jax.ShapeDtypeStruct(PIECES, BF16), jax.ShapeDtypeStruct(LOWS, F32)]
-    if step == 0:
+    out_shape = [jax.ShapeDtypeStruct(PIECES, BF16)] + [jax.ShapeDtypeStruct(LOWS, F32)] * 2
+    first = step == 0
+    if first:
         out_shape += [
             jax.ShapeDtypeStruct((2, 2 * CLIP, RANK), BF16),
             jax.ShapeDtypeStruct((2, 8, RANK), F32),
         ]
     return pl.pallas_call(
-        functools.partial(attend_kernel, step),
+        functools.partial(attend_kernel, first, len(after)),
         grid_spec=pltpu.PrefetchScalarGridSpec(
             num_scalar_prefetch=1,
             grid=(1,),
             in_specs=[own_spec] * 4
             + peer_specs
-            + [whole(a.shape) for a in (up_own, up_other, *lows)],
+            + [whole((2, RANK, SHARD))]
+            + [pl.BlockSpec(memory_space=pl.ANY)] * len(after)
+            + [whole(a.shape) for a in lows],
             out_specs=[whole(a.shape) for a in out_shape],
             scratch_shapes=[
                 pltpu.VMEM((2, RANK, SHARD), BF16),
@@ -241,83 +262,118 @@
         ),
         out_shape=out_shape,
         compiler_params=pltpu.CompilerParams(vmem_limit_bytes=24 * 1024 * 1024),
-        cost_estimate=pl.CostEstimate(
-            flops=4000000000, bytes_accessed=3000000, transcendentals=400000
-        ),
+        cost_estimate=SMALL,
         name="attend",
-    )(place, *arrays, peer, peer, peer, peer, up_own, up_other, *lows)
-
-
-def down_kernel(place, n0, n1, mine, peer, *refs):
-    outs, dlow = refs[:NY], refs[NY]
+    )(place, *arrays, peer, peer, peer, peer, ups[step], *after, *lows)
+
+
+def down_kernel(after, place, n0, n1, mine0, mine1, peer0, peer1, *refs):
+    *outs, dlow, totals = refs[after:]
 
     @pl.when(pl.program_id(0) == 0)
     def _():
         for j in range(2):
             for clip in range(2):
-                total = mine[clip, j] + peer[1 - clip, j]
+                total = (mine0, mine1)[clip][j] + (peer1, peer0)[clip][j]
                 dlow[j * RANK : (j + 1) * RANK, clip * CLIP : (clip + 1) * CLIP] = total.astype(
                     BF16
                 ).T
 
     normed = jnp.concatenate([n0[...], n1[0]], axis=0)
-    total = dot(dlow[...], normed, 1, 0)
-    for step in range(NY):
-
-        @pl.when(pl.program_id(0) == step)
-        def _(out=outs[step]):
-            for j in range(2):
-                store_pieces(out, j, total[j * RANK : (j + 1) * RANK])
-
-
-def down_grads(place, nown, peer, mine, theirs):
-    def shard(i, place):
-        return lax.rem(place[1] + i, NY)
-
-    return pl.pallas_call(
-        down_kernel,
+    totals[...] = dot(dlow[...], normed, 1, 0)
+    for step, out in enumerate(outs):
+        first = lax.rem(place[3] + step, NX) * (2 * RANK // NX)
+        for z in range(NZ):
+            rows = totals[pl.ds(pl.multiple_of(first + z * 8, 8), 8), :]
+            out[0, z] = lane_blocks(rows).astype(BF16)
+
+
+def down_grads(place, nown, peer, dlows, *after):
+    return pl.pallas_call(
+        functools.partial(down_kernel, len(after)),
         grid_spec=pltpu.PrefetchScalarGridSpec(
             num_scalar_prefetch=1,
             grid=(NY,),
             in_specs=[
-                pl.BlockSpec((CLIP, SHARD), lambda i, place: (0, shard(i, place))),
-                pl.BlockSpec((1, CLIP, SHARD), lambda i, place: (4, 0, shard(i, place))),
-                whole(LOWS),
-                whole(LOWS),
+                pl.BlockSpec((CLIP, SHARD), lambda i, place: (0, lax.rem(place[1] + i, NY))),
+                pl.BlockSpec(
+                    (1, CLIP, SHARD), lambda i, place: (4, 0, lax.rem(place[1] + i, NY))
+                ),
+            ]
+            + [whole(LOWS)] * 4
+            + [pl.BlockSpec(memory_space=pl.ANY)] * len(after),
+            out_specs=[pl.BlockSpec((1, *PIECES[1:]), lambda i, place: (i, 0, 0, 0))] * NX,
+            scratch_shapes=[
+                pltpu.VMEM((2 * RANK, 2 * CLIP), BF16),
+                pltpu.VMEM((2 * RANK, SHARD), F32),
             ],
-            out_specs=[whole(PIECES)] * NY,
-            scratch_shapes=[pltpu.VMEM((2 * RANK, 2 * CLIP), BF16)],
         ),
-        out_shape=[jax.ShapeDtypeStruct(PIECES, BF16)] * NY,
+        out_shape=[jax.ShapeDtypeStruct((NY, *PIECES[1:]), BF16)] * NX,
         compiler_params=pltpu.CompilerParams(vmem_limit_bytes=24 * 1024 * 1024),
-        cost_estimate=pl.CostEstimate(
-            flops=3000000000, bytes_accessed=5000000, transcendentals=0
-        ),
+        cost_estimate=SMALL,
         name="down_grads",
-    )(place, nown, peer, mine, theirs)
+    )(place, nown, peer, *dlows, *after)
 
 
 def sum_y_kernel(place, *refs):
-    ups, downs, outs = refs[:4], refs[4:8], refs[8:]
+    parts, outs = refs[:4], refs[4:]
     x = place[3]
     for quarter in range(4):
         source = lax.rem(quarter + x, 4)
         for z in range(NZ):
-            up = sum(r[source, z].astype(F32) for r in ups)
-            down = sum(r[source, z].astype(F32) for r in downs)
-            outs[quarter][z] = jnp.concatenate([up, down], axis=0).astype(BF16)
-
-
-def sum_y(place, ups, downs):
+            total = sum(r[source, z].astype(F32) for r in parts)
+            outs[quarter][z] = total.astype(BF16)
+
+
+def sum_y(place, parts):
     return pl.pallas_call(
         sum_y_kernel,
-        out_shape=[jax.ShapeDtypeStruct((NZ, 80, 128), BF16)] * 4,
+        out_shape=[jax.ShapeDtypeStruct(PIECES[1:], BF16)] * 4,
         in_specs=[pl.BlockSpec(memory_space=pltpu.SMEM)]
-        + [pl.BlockSpec(memory_space=pltpu.VMEM)] * 8,
+        + [pl.BlockSpec(memory_space=pltpu.VMEM)] * 4,
         out_specs=[pl.BlockSpec(memory_space=pltpu.VMEM)] * 4,
         compiler_params=pltpu.CompilerParams(vmem_limit_bytes=VMEM_LIMIT),
+        cost_estimate=SMALL,
         name="sum_y",
-    )(place, *ups, *downs)
+    )(place, *parts)
+
+
+def sum_x_kernel(*refs):
+    parts, outs = refs[:4], refs[4:]
+    for step in range(NY):
+        outs[step][...] = sum(r[step].astype(F32) for r in parts).astype(BF16)
+
+
+def sum_x(parts):
+    return pl.pallas_call(
+        sum_x_kernel,
+        out_shape=[jax.ShapeDtypeStruct(PIECES[1:], BF16)] * NY,
+        in_specs=[pl.BlockSpec(memory_space=pltpu.VMEM)] * 4,
+        out_specs=[pl.BlockSpec(memory_space=pltpu.VMEM)] * NY,
+        compiler_params=pltpu.CompilerParams(vmem_limit_bytes=VMEM_LIMIT),
+        cost_estimate=SMALL,
+        name="sum_x",
+    )(*parts)
+
+
+def join_kernel(*refs):
+    ups, downs, out = refs[:4], refs[4:8], refs[8]
+    for z in range(NZ):
+        up = sum(r[z].astype(F32) for r in ups)
+        down = sum(r[z].astype(F32) for r in downs)
+        out[z] = jnp.concatenate([up, down], axis=0).astype(BF16)
+
+
+def join(ups, downs):
+    return pl.pallas_call(
+        join_kernel,
+        out_shape=jax.ShapeDtypeStruct((NZ, 80, 128), BF16),
+        in_specs=[pl.BlockSpec(memory_space=pltpu.VMEM)] * 8,
+        out_specs=pl.BlockSpec(memory_space=pltpu.VMEM),
+        compiler_params=pltpu.CompilerParams(vmem_limit_bytes=VMEM_LIMIT),
+        cost_estimate=SMALL,
+        name="join",
+    )(*ups, *downs)
 
 
 def finish_kernel(factor, place, own, first, second, first_peer, second_peer, down, up, flat):
@@ -369,12 +425,6 @@
     return own, other
 
 
-def gather(part):
-    first = cross_x(part[None])
-    rest = cross_x(jnp.stack([send_y(part, -step) for step in range(1, NY)]))
-    return first, rest
-
-
 def local(states, steps, q, k, v, g, down_maps, up_maps):
     dp, fsdp = lax.axis_index("dp"), lax.axis_index("fsdp")
     core, x_lo, y = dp % 2, fsdp // NY, fsdp % NY
@@ -385,30 +435,30 @@
 
     down_part = lax.dynamic_index_in_dim(down_maps, core, 0, keepdims=False)
     up_part = lax.dynamic_index_in_dim(up_maps, core, 0, keepdims=False)
-    down_first, down_rest = gather(down_part)
     nown, nsend = normalize(place, states, q, k, v, g)
+    downs = [send_y(down_part, -step) for step in range(1, NY)]
+    up = jnp.stack(cross_x(up_part))
+    nsend, up, *downs = lax.optimization_barrier((nsend, up, *downs))
+    downs = cross_x(jnp.stack([down_part, *downs]))
+    ups = [up] + [send_y(up, -step) for step in range(1, NY)]
     peer = swap_cores(nsend)
-    up_first, up_rest = gather(up_part)
-
-    low_mine = lower(place, nown, peer, *down_first, *down_rest, weight)
-    low_peer = swap_cores(low_mine)
-    rows = (place, (q, k, v, g), peer)
-    gup, dlow, low, weights = attend(0, *rows, *up_first, low_mine, low_peer)
-    ups = [gup]
-    for step in range(1, NY):
-        gup, dlow = attend(step, *rows, *up_rest, low, weights, dlow)
-        ups.append(send_y(gup, step))
-    downs = down_grads(place, nown, peer, dlow, swap_cores(dlow))
-    downs = [downs[0]] + [send_y(downs[step], step) for step in range(1, NY)]
-
-    quarters = sum_y(place, ups, downs)
-    parts = [
-        quarters[0],
-        send(quarters[1], lambda x, y, z, c: (x + 1, y, z, 1 - c)),
-        send(quarters[2], lambda x, y, z, c: (x + 2, y, z, c)),
-        send(quarters[3], lambda x, y, z, c: (x - 1, y, z, 1 - c)),
-    ]
-    eighths = sum(part.astype(F32) for part in parts).astype(BF16)
+
+    lows = lower(place, nown, peer, *downs, weight)
+    lows = [*lows, *(swap_cores(part) for part in lows)]
+    rows = (place, (q, k, v, g), peer, ups)
+    gups = [None] * NY
+    gups[0], *dlow, low, weights = attend(0, (), *rows, *lows)
+    gup, *dlow = attend(1, (), *rows, low, weights, *dlow)
+    gups[1] = send_y(gup, 1)
+    gup, *dlow = attend(3, (), *rows, low, weights, *dlow)
+    gups[3] = send_y(gup, 3)
+    gup, *dlow = attend(2, (), *rows, low, weights, *dlow)
+    gups[2] = send_y(gup, 2)
+    dlows = [*dlow, *(swap_cores(part) for part in dlow)]
+    gdowns = scatter_x(down_grads(place, nown, peer, dlows, gups[1]))
+    ups = scatter_x(sum_y(place, gups))
+    downs = scatter_y(sum_x(gdowns))
+    eighths = join(ups, downs)
     eighths = exchange_z(eighths)
     piece = jnp.sum(eighths.astype(F32), axis=0).astype(BF16)
     quarter = exchange_z(jnp.broadcast_to(piece, (NZ, 80, 128)))

time: 169 us -> 134 us (0.79)
  waiting for transfers between devices: 56.8 us -> 29.5 us
  local copies, waits for them, and re-layouts: 7.86 us -> 1.08 us
  Pallas kernels: 32.9 us -> 28.9 us
  starting transfers between devices: 41.8 us -> 45.5 us
    ppermute x30 -> x31, waiting for transfers between devices: 56.8 us -> 29.5 us  [send(): return lax.ppermute(value, AXES, permutation(target))]
    unnamed x22 -> x14, local copies, waits for them, and re-layouts: 7.77 us -> 0.04 us
    pallas_call x7 -> x9, Pallas kernels: 26.1 us -> 19 us  [the longest x4 13.6 us: attend(): pl.pallas_call(functools.partial(attend_kernel, first, len(after)), grid_...]
    ppermute x30 -> x31, starting transfers between devices: 41.8 us -> 45.5 us  [send(): return lax.ppermute(value, AXES, permutation(target))]
    pallas_call x1, Pallas kernels: 5 us -> 8.17 us  [normalize(): pl.pallas_call(normalize_kernel, grid_spec=pltpu.PrefetchScalarGridSpec(n...]
  transfers between devices with their start and end apart: 30 -> 31, of which waited for: 17 -> 15; matrix products, arithmetic and copies ran while one was open for 0% -> 1% of each run, Pallas kernels for 5% -> 20%
where the time goes in v2:
time: 134 us
  starting transfers between devices  45.5 us (34%)
  waiting for transfers between devices  29.5 us (22%)
  Pallas kernels  28.9 us (22%)
  blocking collectives  26.9 us (20%)
  between operations  1.6 us (1%)
    ppermute x31, starting transfers between devices, send(): return lax.ppermute(value, AXES, permutation(target))  45.5 us
    ppermute x31, waiting for transfers between devices, send(): return lax.ppermute(value, AXES, permutation(target))  29.5 us
    all_to_all x2, blocking collectives, exchange_z(): lax.all_to_all(value, AXES, 0, 0, axis_index_groups=Z_GROUPS, tiled=True)  26.9 us
    pallas_call x4, Pallas kernels, attend(): pl.pallas_call(functools.partial(attend_kernel, first, len(after)), grid_...  13.6 us
    pallas_call x1, Pallas kernels, normalize(): pl.pallas_call(normalize_kernel, grid_spec=pltpu.PrefetchScalarGridSpec(n...  8.17 us
    pallas_call x1, Pallas kernels, down_grads(): pl.pallas_call(functools.partial(down_kernel, len(after)), grid_spec=pltp...  2.69 us
  transfers between devices with their start and end apart: 31, of which 15 were waited for; matrix products, arithmetic and copies ran while one was open for 1% of the time, Pallas kernels for 20%

profile of v2, /device:TPU:1, one launch (start us, length us, event | category | flops | bytes accessed | tf_op | source)
XLA Modules:
  0.0 134.1 jit_solution(18015284570239175795)
XLA Ops:
  0.7 1.0 dynamic-slice_bitcast_fusion
  1.6 3.3 %collective-permute-start.1 = (bf16[128,640]{1,0:T(8,128)(2,1)S(1)}, bf16[128,640]{1,0:T(8,128)(2,1)S(1)}, u32[]{:S(2)}, u32[]{:S(2)}) collective-permute-start(bf16[128,640]{1,0:T(8,128)(2,1)S(1)} %dynamic-slice_bitcast_fusion), channel_id=1, source_target_pairs={{0,140},{8,0},{16,156},{24,16},{32,172},{40,32},{48,188},{56,48},{... | collective-permute-start | bytes 491528 | tf_op jit(solution)/shard_map/ppermute | solution.py:46
  4.9 1.9 %collective-permute-start = (bf16[128,640]{1,0:T(8,128)(2,1)S(1)}, bf16[128,640]{1,0:T(8,128)(2,1)S(1)}, u32[]{:S(2)}, u32[]{:S(2)}) collective-permute-start(bf16[128,640]{1,0:T(8,128)(2,1)S(1)} %dynamic-slice_bitcast_fusion), channel_id=1, source_target_pairs={{0,0},{8,12},{16,16},{24,28},{32,32},{40,44},{48,48},{56,60},{64,6... | collective-permute-start | bytes 491528 | tf_op jit(solution)/shard_map/ppermute | solution.py:46
  6.8 2.3 %collective-permute-start.2 = (bf16[640,128]{1,0:T(8,128)(2,1)S(1)}, bf16[640,128]{1,0:T(8,128)(2,1)S(1)}, u32[]{:S(2)}, u32[]{:S(2)}) collective-permute-start(bf16[640,128]{1,0:T(8,128)(2,1)S(1)} %fusion), channel_id=1, source_target_pairs={{0,3},{8,11},{16,19},{24,27},{32,35},{40,43},{48,51},{56,59},{64,6... | collective-permute-start | bytes 491528 | tf_op jit(solution)/shard_map/ppermute | solution.py:46
  9.1 0.3 collective-permute-start.3
  9.5 0.7 collective-permute-start.4
  10.2 0.6 pad_add_fusion.place
  10.7 8.2 %normalize.1 = (bf16[192,2560]{1,0:T(8,128)(2,1)}, bf16[5,192,2560]{2,1,0:T(8,128)(2,1)}) custom-call(s32[4]{0:T(128)} %pad_add_fusion.place, bf16[192,5120]{1,0:T(8,128)(2,1)} %states.1, bf16[192,5120]{1,0:T(8,128)(2,1)} %refs_0_.7, bf16[192,5120]{1,0:T(8,128)(2,1)} %refs_1_.7, bf16[192,5120]{1,0:T(8,128)(2,1)} %refs_2_.7, bf16[192,5120]{1,0:T(8,128)(2,1)} %refs_3_.7), custom_call_target="tpu_custom_call" | custom-call | flops 1000 | bytes 1000 | tf_op jit(solution)/shard_map/normalize/pallas_call | solution.py:109
  19.0 1.3 collective-permute-done.4
  20.3 0.5 collective-permute-start.5
  20.9 2.1 %collective-permute-start.6 = (bf16[4,640,128]{2,1,0:T(8,128)(2,1)S(1)}, bf16[4,640,128]{2,1,0:T(8,128)(2,1)S(1)}, u32[]{:S(2)}, u32[]{:S(2)}) collective-permute-start(bf16[4,640,128]{2,1,0:T(8,128)(2,1)S(1)} %pad_maximum_fusion), channel_id=1, source_target_pairs={{0,0},{8,12},{16,16},{24,28},{32,32},{40,44},{48,48},{56,60},{64,6... | collective-permute-start | bytes 1966088 | tf_op jit(solution)/shard_map/ppermute | solution.py:46
  23.0 1.6 %collective-permute-start.10 = (bf16[2,128,640]{2,1,0:T(8,128)(2,1)S(1)}, bf16[2,128,640]{2,1,0:T(8,128)(2,1)S(1)}, u32[]{:S(2)}, u32[]{:S(2)}) collective-permute-start(bf16[2,128,640]{2,1,0:T(8,128)(2,1)S(1)} %pad_maximum_fusion.1.refs_8_), channel_id=1, source_target_pairs={{0,3},{8,11},{16,19},{24,27},{32,35},{40,43},{48,51},{56,59},{64,6... | collective-permute-start | bytes 983048 | tf_op jit(solution)/shard_map/ppermute | solution.py:46
  25.3 8.3 %collective-permute-done.6.own = bf16[4,640,128]{2,1,0:T(8,128)(2,1)S(1)} collective-permute-done((bf16[4,640,128]{2,1,0:T(8,128)(2,1)S(1)}, bf16[4,640,128]{2,1,0:T(8,128)(2,1)S(1)}, u32[]{:S(2)}, u32[]{:S(2)}) %collective-permute-start.6) | collective-permute-done | bytes 655392 | tf_op jit(solution)/shard_map/ppermute | solution.py:46
  33.6 1.7 %lower.1 = (f32[2,200,128]{2,1,0:T(8,128)S(1)}, f32[2,200,128]{2,1,0:T(8,128)S(1)}) custom-call(s32[4]{0:T(128)S(1)} %copy-done.6, bf16[192,2560]{1,0:T(8,128)(2,1)S(1)} %copy-done.5, bf16[5,192,2560]{2,1,0:T(8,128)(2,1)S(1)} %collective-permute-done.5.npeer.refs_4_.refs_5_.refs_6_.refs_7_.n1, bf16[4,640,128]{2,1,0:T(8,128)(2,1)S(1)} %collective-permute-done.6.own, ...), custom_call_target="tpu_custom_call" | custom-call | tf_op jit(solution)/shard_map/lower/pallas_call | solution.py:150
  35.4 0.6 collective-permute-start.8
  36.1 0.6 collective-permute-start.13
  36.7 1.8 %collective-permute-start.12 = (bf16[2,128,640]{2,1,0:T(8,128)(2,1)S(1)}, bf16[2,128,640]{2,1,0:T(8,128)(2,1)S(1)}, u32[]{:S(2)}, u32[]{:S(2)}) collective-permute-start(bf16[2,128,640]{2,1,0:T(8,128)(2,1)S(1)} %pad_maximum_fusion.1.refs_8_), channel_id=1, source_target_pairs={{0,2},{8,10},{16,18},{24,26},{32,34},{40,42},{48,50},{56,58},{64,6... | collective-permute-start | bytes 983048 | tf_op jit(solution)/shard_map/ppermute | solution.py:46
  38.5 3.4 %attend.4 = (bf16[4,8,40,128]{3,2,1,0:T(8,128)(2,1)S(1)}, f32[2,192,128]{2,1,0:T(8,128)S(1)}, f32[2,192,128]{2,1,0:T(8,128)S(1)}, bf16[2,384,128]{2,1,0:T(8,128)(2,1)S(1)}, f32[2,8,128]{2,1,0:T(8,128)S(1)}) custom-call(s32[4]{0:T(128)S(1)} %copy-done.6, bf16[192,5120]{1,0:T(8,128)(2,1)S(1)} %copy-done.1, bf16[192,5120]{1,0:T(8,128)(2,1)S(1)} %copy-done.2, ...), custom_call_target="tpu_custom_call" | custom-call | flops 1000 | bytes 1000 | tf_op jit(solution)/shard_map/attend/pallas_call | solution.py:246
  41.9 3.4 %attend.5 = (bf16[4,8,40,128]{3,2,1,0:T(8,128)(2,1)S(1)}, f32[2,192,128]{2,1,0:T(8,128)S(1)}, f32[2,192,128]{2,1,0:T(8,128)S(1)}) custom-call(s32[4]{0:T(128)S(1)} %copy-done.6, bf16[192,5120]{1,0:T(8,128)(2,1)S(1)} %copy-done.1, bf16[192,5120]{1,0:T(8,128)(2,1)S(1)} %copy-done.2, bf16[192,5120]{1,0:T(8,128)(2,1)S(1)} %copy-done.3, ...), custom_call_target="tpu_custom_call" | custom-call | flops 1000 | bytes 1000 | tf_op jit(solution)/shard_map/attend/pallas_call | solution.py:246
  45.3 1.0 collective-permute-start.11
  46.3 3.4 %attend.6 = (bf16[4,8,40,128]{3,2,1,0:T(8,128)(2,1)S(1)}, f32[2,192,128]{2,1,0:T(8,128)S(1)}, f32[2,192,128]{2,1,0:T(8,128)S(1)}) custom-call(s32[4]{0:T(128)S(1)} %copy-done.6, bf16[192,5120]{1,0:T(8,128)(2,1)S(1)} %copy-done.1, bf16[192,5120]{1,0:T(8,128)(2,1)S(1)} %copy-done.2, bf16[192,5120]{1,0:T(8,128)(2,1)S(1)} %copy-done.3, ...), custom_call_target="tpu_custom_call" | custom-call | flops 1000 | bytes 1000 | tf_op jit(solution)/shard_map/attend/pallas_call | solution.py:246
  49.7 3.4 %collective-permute-done.12.refs_8_ = bf16[2,128,640]{2,1,0:T(8,128)(2,1)S(1)} collective-permute-done((bf16[2,128,640]{2,1,0:T(8,128)(2,1)S(1)}, bf16[2,128,640]{2,1,0:T(8,128)(2,1)S(1)}, u32[]{:S(2)}, u32[]{:S(2)}) %collective-permute-start.12) | collective-permute-done | bytes 327712 | tf_op jit(solution)/shard_map/ppermute | solution.py:46
  53.1 3.4 %attend.7 = (bf16[4,8,40,128]{3,2,1,0:T(8,128)(2,1)S(1)}, f32[2,192,128]{2,1,0:T(8,128)S(1)}, f32[2,192,128]{2,1,0:T(8,128)S(1)}) custom-call(s32[4]{0:T(128)S(1)} %copy-done.6, bf16[192,5120]{1,0:T(8,128)(2,1)S(1)} %copy-done.1, bf16[192,5120]{1,0:T(8,128)(2,1)S(1)} %copy-done.2, bf16[192,5120]{1,0:T(8,128)(2,1)S(1)} %copy-done.3, ...), custom_call_target="tpu_custom_call" | custom-call | flops 1000 | bytes 1000 | tf_op jit(solution)/shard_map/attend/pallas_call | solution.py:246
  56.5 5.2 %collective-permute-start.19 = (f32[2,192,128]{2,1,0:T(8,128)S(1)}, f32[2,192,128]{2,1,0:T(8,128)S(1)}, u32[]{:S(2)}, u32[]{:S(2)}) collective-permute-start(f32[2,192,128]{2,1,0:T(8,128)S(1)} %get-tuple-element.64.mine0), channel_id=1, source_target_pairs={{0,8},{8,0},{16,24},{24,16},{32,40},{40,32},{48,56},{56,48},{64,72... | collective-permute-start | bytes 589832 | tf_op jit(solution)/shard_map/ppermute | solution.py:46
  61.8 1.0 collective-permute-done.19.peer0
  62.7 0.4 collective-permute-done.20.peer1
  63.1 2.7 %down_grads.1 = (bf16[4,8,40,128]{3,2,1,0:T(8,128)(2,1)S(1)}, bf16[4,8,40,128]{3,2,1,0:T(8,128)(2,1)S(1)}, bf16[4,8,40,128]{3,2,1,0:T(8,128)(2,1)S(1)}, bf16[4,8,40,128]{3,2,1,0:T(8,128)(2,1)S(1)}) custom-call(s32[4]{0:T(128)S(1)} %copy-done.6, bf16[192,2560]{1,0:T(8,128)(2,1)S(1)} %copy-done.5, ...), custom_call_target="tpu_custom_call" | custom-call | flops 1000 | bytes 1000 | tf_op jit(solution)/shard_map/down_grads/pallas_call | solution.py:292
  65.9 4.8 %collective-permute-start.22 = (bf16[4,8,40,128]{3,2,1,0:T(8,128)(2,1)S(1)}, bf16[4,8,40,128]{3,2,1,0:T(8,128)(2,1)S(1)}, u32[]{:S(2)}, u32[]{:S(2)}) collective-permute-start(bf16[4,8,40,128]{3,2,1,0:T(8,128)(2,1)S(1)} %get-tuple-element.68), channel_id=1, source_target_pairs={{0,128},{8,136},{16,144},{24,152},{32,160},{40,168},{48,176},{56,1... | collective-permute-start | bytes 983048 | tf_op jit(solution)/shard_map/ppermute | solution.py:46
  70.7 1.5 %collective-permute-done.14.refs_2_ = bf16[4,8,40,128]{3,2,1,0:T(8,128)(2,1)S(1)} collective-permute-done((bf16[4,8,40,128]{3,2,1,0:T(8,128)(2,1)S(1)}, bf16[4,8,40,128]{3,2,1,0:T(8,128)(2,1)S(1)}, u32[]{:S(2)}, u32[]{:S(2)}) %collective-permute-start.14) | collective-permute-done | bytes 327712 | tf_op jit(solution)/shard_map/ppermute | solution.py:46
  72.2 3.5 %collective-permute-done.15.refs_3_ = bf16[4,8,40,128]{3,2,1,0:T(8,128)(2,1)S(1)} collective-permute-done((bf16[4,8,40,128]{3,2,1,0:T(8,128)(2,1)S(1)}, bf16[4,8,40,128]{3,2,1,0:T(8,128)(2,1)S(1)}, u32[]{:S(2)}, u32[]{:S(2)}) %collective-permute-start.15) | collective-permute-done | bytes 327712 | tf_op jit(solution)/shard_map/ppermute | solution.py:46
  75.6 0.7 sum_y.1
  76.4 6.1 %collective-permute-start.17 = (bf16[8,40,128]{2,1,0:T(8,128)(2,1)S(1)}, bf16[8,40,128]{2,1,0:T(8,128)(2,1)S(1)}, u32[]{:S(2)}, u32[]{:S(2)}) collective-permute-start(bf16[8,40,128]{2,1,0:T(8,128)(2,1)S(1)} %get-tuple-element.62), channel_id=1, source_target_pairs={{0,128},{8,136},{16,144},{24,152},{32,160},{40,168},{48,176},{56,1... | collective-permute-start | bytes 245768 | tf_op jit(solution)/shard_map/ppermute | solution.py:46
  82.5 3.2 %collective-permute-done.22.refs_2_ = bf16[4,8,40,128]{3,2,1,0:T(8,128)(2,1)S(1)} collective-permute-done((bf16[4,8,40,128]{3,2,1,0:T(8,128)(2,1)S(1)}, bf16[4,8,40,128]{3,2,1,0:T(8,128)(2,1)S(1)}, u32[]{:S(2)}, u32[]{:S(2)}) %collective-permute-start.22) | collective-permute-done | bytes 327712 | tf_op jit(solution)/shard_map/ppermute | solution.py:46
  85.7 0.4 collective-permute-done.23.refs_3_
  86.2 0.7 collective-permute-start.24
  86.9 3.0 %collective-permute-start.25 = (bf16[8,40,128]{2,1,0:T(8,128)(2,1)S(1)}, bf16[8,40,128]{2,1,0:T(8,128)(2,1)S(1)}, u32[]{:S(2)}, u32[]{:S(2)}) collective-permute-start(bf16[8,40,128]{2,1,0:T(8,128)(2,1)S(1)} %get-tuple-element.72), channel_id=1, source_target_pairs={{0,2},{8,10},{16,18},{24,26},{32,34},{40,42},{48,50},{56,58},{64,6... | collective-permute-start | bytes 245768 | tf_op jit(solution)/shard_map/ppermute | solution.py:46
  89.9 0.6 collective-permute-start.26
  90.5 0.3 collective-permute-done.24.refs_5_
  90.8 3.4 %collective-permute-done.25.refs_6_ = bf16[8,40,128]{2,1,0:T(8,128)(2,1)S(1)} collective-permute-done((bf16[8,40,128]{2,1,0:T(8,128)(2,1)S(1)}, bf16[8,40,128]{2,1,0:T(8,128)(2,1)S(1)}, u32[]{:S(2)}, u32[]{:S(2)}) %collective-permute-start.25) | collective-permute-done | bytes 81952 | tf_op jit(solution)/shard_map/ppermute | solution.py:46
  94.3 16.1 %all_to_all.10 = bf16[8,80,128]{2,1,0:T(8,128)(2,1)S(1)} all-to-all(bf16[8,80,128]{2,1,0:T(8,128)(2,1)S(1)} %join.1), channel_id=1, replica_groups={{0,16,32,48,64,80,96,112},{8,24,40,56,72,88,104,120},{1,17,33,49,65,81,..., dimensions={0} | all-to-all | bytes 327680 | tf_op jit(solution)/shard_map/all_to_all | solution.py:79
  110.5 10.8 %all_to_all.11.own = bf16[8,80,128]{2,1,0:T(8,128)(2,1)S(1)} all-to-all(bf16[8,80,128]{2,1,0:T(8,128)(2,1)S(1)} %broadcast_in_dim.7), channel_id=1, replica_groups={{0,16,32,48,64,80,96,112},{8,24,40,56,72,88,104,120},{1,17,33,49,65,81,..., dimensions={0} | all-to-all | bytes 327680 | tf_op jit(solution)/shard_map/all_to_all | solution.py:79
  121.3 3.5 %collective-permute-start.27 = (bf16[8,80,128]{2,1,0:T(8,128)(2,1)S(1)}, bf16[8,80,128]{2,1,0:T(8,128)(2,1)S(1)}, u32[]{:S(2)}, u32[]{:S(2)}) collective-permute-start(bf16[8,80,128]{2,1,0:T(8,128)(2,1)S(1)} %all_to_all.11.own), channel_id=1, source_target_pairs={{0,136},{8,4},{16,152},{24,20},{32,168},{40,36},{48,184},{56,52},{... | collective-permute-start | bytes 491528 | tf_op jit(solution)/shard_map/ppermute | solution.py:46
  124.7 2.2 %collective-permute-start.28 = (bf16[8,80,128]{2,1,0:T(8,128)(2,1)S(1)}, bf16[8,80,128]{2,1,0:T(8,128)(2,1)S(1)}, u32[]{:S(2)}, u32[]{:S(2)}) collective-permute-start(bf16[8,80,128]{2,1,0:T(8,128)(2,1)S(1)} %all_to_all.11.own), channel_id=1, source_target_pairs={{0,8},{8,132},{16,24},{24,148},{32,40},{40,164},{48,56},{56,180},{... | collective-permute-start | bytes 491528 | tf_op jit(solution)/shard_map/ppermute | solution.py:46
  126.9 1.5 %collective-permute-done.27.first = bf16[8,80,128]{2,1,0:T(8,128)(2,1)S(1)} collective-permute-done((bf16[8,80,128]{2,1,0:T(8,128)(2,1)S(1)}, bf16[8,80,128]{2,1,0:T(8,128)(2,1)S(1)}, u32[]{:S(2)}, u32[]{:S(2)}) %collective-permute-start.27) | collective-permute-done | bytes 163872 | tf_op jit(solution)/shard_map/ppermute | solution.py:46
  128.4 2.5 %collective-permute-start.29 = (bf16[8,80,128]{2,1,0:T(8,128)(2,1)S(1)}, bf16[8,80,128]{2,1,0:T(8,128)(2,1)S(1)}, u32[]{:S(2)}, u32[]{:S(2)}) collective-permute-start(bf16[8,80,128]{2,1,0:T(8,128)(2,1)S(1)} %collective-permute-done.27.first), channel_id=1, source_target_pairs={{0,8},{8,0},{16,24},{24,16},{32,40},{40,32},{48,56},{56,48},{64,72... | collective-permute-start | bytes 491528 | tf_op jit(solution)/shard_map/ppermute | solution.py:46
  130.9 1.0 collective-permute-done.29.first_peer
  132.0 0.4 collective-permute-done.30.second_peer
  132.3 1.7 %finish.1 = (f32[2,640,128]{2,1,0:T(8,128)}, f32[32,8,640]{2,1,0:T(8,128)}) custom-call(s32[4]{0:T(128)S(1)} %copy-done.6, bf16[8,80,128]{2,1,0:T(8,128)(2,1)S(1)} %all_to_all.11.own, bf16[8,80,128]{2,1,0:T(8,128)(2,1)S(1)} %collective-permute-done.27.first, bf16[8,80,128]{2,1,0:T(8,128)(2,1)S(1)} %collective-permute-done.28.second, ...), custom_call_target="tpu_custom_call" | custom-call | tf_op jit(solution)/shard_map/finish/pallas_call | solution.py:407
  (50 shorter events, 1.0 us)
Async XLA Ops:
  0.6 6.2 %copy-start = (bf16[2,640,128]{2,1,0:T(8,128)(2,1)S(1)}, bf16[2,640,128]{2,1,0:T(8,128)(2,1)}, u32[]{:S(2)}) copy-start(bf16[2,640,128]{2,1,0:T(8,128)(2,1)} %param.14) | copy-start | bytes 983044
  1.6 17.3 %collective-permute-start.1 = (bf16[128,640]{1,0:T(8,128)(2,1)S(1)}, bf16[128,640]{1,0:T(8,128)(2,1)S(1)}, u32[]{:S(2)}, u32[]{:S(2)}) collective-permute-start(bf16[128,640]{1,0:T(8,128)(2,1)S(1)} %dynamic-slice_bitcast_fusion), channel_id=1, source_target_pairs={{0,140},{8,0},{16,156},{24,16},{32,172},{40,32},{48,188},{56,48},{... | collective-permute-start | bytes 491528 | tf_op jit(solution)/shard_map/ppermute | solution.py:46
  4.9 14.0 %collective-permute-start = (bf16[128,640]{1,0:T(8,128)(2,1)S(1)}, bf16[128,640]{1,0:T(8,128)(2,1)S(1)}, u32[]{:S(2)}, u32[]{:S(2)}) collective-permute-start(bf16[128,640]{1,0:T(8,128)(2,1)S(1)} %dynamic-slice_bitcast_fusion), channel_id=1, source_target_pairs={{0,0},{8,12},{16,16},{24,28},{32,32},{40,44},{48,48},{56,60},{64,6... | collective-permute-start | bytes 491528 | tf_op jit(solution)/shard_map/ppermute | solution.py:46
  6.8 12.1 %collective-permute-start.2 = (bf16[640,128]{1,0:T(8,128)(2,1)S(1)}, bf16[640,128]{1,0:T(8,128)(2,1)S(1)}, u32[]{:S(2)}, u32[]{:S(2)}) collective-permute-start(bf16[640,128]{1,0:T(8,128)(2,1)S(1)} %fusion), channel_id=1, source_target_pairs={{0,3},{8,11},{16,19},{24,27},{32,35},{40,43},{48,51},{56,59},{64,6... | collective-permute-start | bytes 491528 | tf_op jit(solution)/shard_map/ppermute | solution.py:46
  9.1 9.9 %collective-permute-start.3 = (bf16[640,128]{1,0:T(8,128)(2,1)S(1)}, bf16[640,128]{1,0:T(8,128)(2,1)S(1)}, u32[]{:S(2)}, u32[]{:S(2)}) collective-permute-start(bf16[640,128]{1,0:T(8,128)(2,1)S(1)} %fusion), channel_id=1, source_target_pairs={{0,2},{8,10},{16,18},{24,26},{32,34},{40,42},{48,50},{56,58},{64,6... | collective-permute-start | bytes 491528 | tf_op jit(solution)/shard_map/ppermute | solution.py:46
  9.5 10.8 %collective-permute-start.4 = (bf16[640,128]{1,0:T(8,128)(2,1)S(1)}, bf16[640,128]{1,0:T(8,128)(2,1)S(1)}, u32[]{:S(2)}, u32[]{:S(2)}) collective-permute-start(bf16[640,128]{1,0:T(8,128)(2,1)S(1)} %fusion), channel_id=1, source_target_pairs={{0,1},{8,9},{16,17},{24,25},{32,33},{40,41},{48,49},{56,57},{64,65... | collective-permute-start | bytes 491528 | tf_op jit(solution)/shard_map/ppermute | solution.py:46
  18.9 14.6 %copy-start.5 = (bf16[192,2560]{1,0:T(8,128)(2,1)S(1)}, bf16[192,2560]{1,0:T(8,128)(2,1)}, u32[]{:S(2)}) copy-start(bf16[192,2560]{1,0:T(8,128)(2,1)} %get-tuple-element.42.nown.n0) | copy-start | bytes 2949124
  18.9 14.7 %copy-start.6 = (s32[4]{0:T(128)S(1)}, s32[4]{0:T(128)}, u32[]{:S(2)}) copy-start(s32[4]{0:T(128)} %pad_add_fusion.place) | copy-start | bytes 52
  20.3 13.3 %collective-permute-start.5 = (bf16[5,192,2560]{2,1,0:T(8,128)(2,1)}, bf16[5,192,2560]{2,1,0:T(8,128)(2,1)S(1)}, u32[]{:S(2)}, u32[]{:S(2)}) collective-permute-start(bf16[5,192,2560]{2,1,0:T(8,128)(2,1)} %get-tuple-element.40), channel_id=1, source_target_pairs={{0,8},{8,0},{16,24},{24,16},{32,40},{40,32},{48,56},{56,48},{64,72... | collective-permute-start | bytes 14745608 | tf_op jit(solution)/shard_map/ppermute | solution.py:46
  20.8 17.6 %copy-start.4 = (bf16[192,5120]{1,0:T(8,128)(2,1)S(1)}, bf16[192,5120]{1,0:T(8,128)(2,1)}, u32[]{:S(2)}) copy-start(bf16[192,5120]{1,0:T(8,128)(2,1)} %refs_3_.7) | copy-start | bytes 5898244
  20.9 12.7 %collective-permute-start.6 = (bf16[4,640,128]{2,1,0:T(8,128)(2,1)S(1)}, bf16[4,640,128]{2,1,0:T(8,128)(2,1)S(1)}, u32[]{:S(2)}, u32[]{:S(2)}) collective-permute-start(bf16[4,640,128]{2,1,0:T(8,128)(2,1)S(1)} %pad_maximum_fusion), channel_id=1, source_target_pairs={{0,0},{8,12},{16,16},{24,28},{32,32},{40,44},{48,48},{56,60},{64,6... | collective-permute-start | bytes 1966088 | tf_op jit(solution)/shard_map/ppermute | solution.py:46
  22.9 10.6 %collective-permute-start.7 = (bf16[4,640,128]{2,1,0:T(8,128)(2,1)S(1)}, bf16[4,640,128]{2,1,0:T(8,128)(2,1)S(1)}, u32[]{:S(2)}, u32[]{:S(2)}) collective-permute-start(bf16[4,640,128]{2,1,0:T(8,128)(2,1)S(1)} %pad_maximum_fusion), channel_id=1, source_target_pairs={{0,140},{8,0},{16,156},{24,16},{32,172},{40,32},{48,188},{56,48},{... | collective-permute-start | bytes 1966088 | tf_op jit(solution)/shard_map/ppermute | solution.py:46
  23.0 18.9 %collective-permute-start.10 = (bf16[2,128,640]{2,1,0:T(8,128)(2,1)S(1)}, bf16[2,128,640]{2,1,0:T(8,128)(2,1)S(1)}, u32[]{:S(2)}, u32[]{:S(2)}) collective-permute-start(bf16[2,128,640]{2,1,0:T(8,128)(2,1)S(1)} %pad_maximum_fusion.1.refs_8_), channel_id=1, source_target_pairs={{0,3},{8,11},{16,19},{24,27},{32,35},{40,43},{48,51},{56,59},{64,6... | collective-permute-start | bytes 983048 | tf_op jit(solution)/shard_map/ppermute | solution.py:46
  33.6 4.8 %copy-start.1 = (bf16[192,5120]{1,0:T(8,128)(2,1)S(1)}, bf16[192,5120]{1,0:T(8,128)(2,1)}, u32[]{:S(2)}) copy-start(bf16[192,5120]{1,0:T(8,128)(2,1)} %refs_0_.7) | copy-start | bytes 5898244
  33.6 4.8 %copy-start.2 = (bf16[192,5120]{1,0:T(8,128)(2,1)S(1)}, bf16[192,5120]{1,0:T(8,128)(2,1)}, u32[]{:S(2)}) copy-start(bf16[192,5120]{1,0:T(8,128)(2,1)} %refs_1_.7) | copy-start | bytes 5898244
  33.6 4.8 %copy-start.3 = (bf16[192,5120]{1,0:T(8,128)(2,1)S(1)}, bf16[192,5120]{1,0:T(8,128)(2,1)}, u32[]{:S(2)}) copy-start(bf16[192,5120]{1,0:T(8,128)(2,1)} %refs_2_.7) | copy-start | bytes 5898244
  35.4 3.0 %collective-permute-start.8 = (f32[2,200,128]{2,1,0:T(8,128)S(1)}, f32[2,200,128]{2,1,0:T(8,128)S(1)}, u32[]{:S(2)}, u32[]{:S(2)}) collective-permute-start(f32[2,200,128]{2,1,0:T(8,128)S(1)} %get-tuple-element.46.refs_9_), channel_id=1, source_target_pairs={{0,8},{8,0},{16,24},{24,16},{32,40},{40,32},{48,56},{56,48},{64,72... | collective-permute-start | bytes 614408 | tf_op jit(solution)/shard_map/ppermute | solution.py:46
  36.0 2.4 %collective-permute-start.9 = (f32[2,200,128]{2,1,0:T(8,128)S(1)}, f32[2,200,128]{2,1,0:T(8,128)S(1)}, u32[]{:S(2)}, u32[]{:S(2)}) collective-permute-start(f32[2,200,128]{2,1,0:T(8,128)S(1)} %get-tuple-element.47.refs_10_), channel_id=1, source_target_pairs={{0,8},{8,0},{16,24},{24,16},{32,40},{40,32},{48,56},{56,48},{64,72... | collective-permute-start | bytes 614408 | tf_op jit(solution)/shard_map/ppermute | solution.py:46
  36.1 10.2 %collective-permute-start.13 = (bf16[2,128,640]{2,1,0:T(8,128)(2,1)S(1)}, bf16[2,128,640]{2,1,0:T(8,128)(2,1)S(1)}, u32[]{:S(2)}, u32[]{:S(2)}) collective-permute-start(bf16[2,128,640]{2,1,0:T(8,128)(2,1)S(1)} %pad_maximum_fusion.1.refs_8_), channel_id=1, source_target_pairs={{0,1},{8,9},{16,17},{24,25},{32,33},{40,41},{48,49},{56,57},{64,65... | collective-permute-start | bytes 983048 | tf_op jit(solution)/shard_map/ppermute | solution.py:46
  36.7 16.5 %collective-permute-start.12 = (bf16[2,128,640]{2,1,0:T(8,128)(2,1)S(1)}, bf16[2,128,640]{2,1,0:T(8,128)(2,1)S(1)}, u32[]{:S(2)}, u32[]{:S(2)}) collective-permute-start(bf16[2,128,640]{2,1,0:T(8,128)(2,1)S(1)} %pad_maximum_fusion.1.refs_8_), channel_id=1, source_target_pairs={{0,2},{8,10},{16,18},{24,26},{32,34},{40,42},{48,50},{56,58},{64,6... | collective-permute-start | bytes 983048 | tf_op jit(solution)/shard_map/ppermute | solution.py:46
  45.3 17.8 %collective-permute-start.11 = (bf16[4,8,40,128]{3,2,1,0:T(8,128)(2,1)S(1)}, bf16[4,8,40,128]{3,2,1,0:T(8,128)(2,1)S(1)}, u32[]{:S(2)}, u32[]{:S(2)}) collective-permute-start(bf16[4,8,40,128]{3,2,1,0:T(8,128)(2,1)S(1)} %get-tuple-element.53), channel_id=1, source_target_pairs={{0,1},{8,9},{16,17},{24,25},{32,33},{40,41},{48,49},{56,57},{64,65... | collective-permute-start | bytes 983048 | tf_op jit(solution)/shard_map/ppermute | solution.py:46
  56.5 6.2 %collective-permute-start.19 = (f32[2,192,128]{2,1,0:T(8,128)S(1)}, f32[2,192,128]{2,1,0:T(8,128)S(1)}, u32[]{:S(2)}, u32[]{:S(2)}) collective-permute-start(f32[2,192,128]{2,1,0:T(8,128)S(1)} %get-tuple-element.64.mine0), channel_id=1, source_target_pairs={{0,8},{8,0},{16,24},{24,16},{32,40},{40,32},{48,56},{56,48},{64,72... | collective-permute-start | bytes 589832 | tf_op jit(solution)/shard_map/ppermute | solution.py:46
  61.7 1.4 %collective-permute-start.20 = (f32[2,192,128]{2,1,0:T(8,128)S(1)}, f32[2,192,128]{2,1,0:T(8,128)S(1)}, u32[]{:S(2)}, u32[]{:S(2)}) collective-permute-start(f32[2,192,128]{2,1,0:T(8,128)S(1)} %get-tuple-element.65.mine1), channel_id=1, source_target_pairs={{0,8},{8,0},{16,24},{24,16},{32,40},{40,32},{48,56},{56,48},{64,72... | collective-permute-start | bytes 589832 | tf_op jit(solution)/shard_map/ppermute | solution.py:46
  61.8 10.4 %collective-permute-start.14 = (bf16[4,8,40,128]{3,2,1,0:T(8,128)(2,1)S(1)}, bf16[4,8,40,128]{3,2,1,0:T(8,128)(2,1)S(1)}, u32[]{:S(2)}, u32[]{:S(2)}) collective-permute-start(bf16[4,8,40,128]{3,2,1,0:T(8,128)(2,1)S(1)} %get-tuple-element.58), channel_id=1, source_target_pairs={{0,2},{8,10},{16,18},{24,26},{32,34},{40,42},{48,50},{56,58},{64,6... | collective-permute-start | bytes 983048 | tf_op jit(solution)/shard_map/ppermute | solution.py:46
  61.8 13.8 %collective-permute-start.15 = (bf16[4,8,40,128]{3,2,1,0:T(8,128)(2,1)S(1)}, bf16[4,8,40,128]{3,2,1,0:T(8,128)(2,1)S(1)}, u32[]{:S(2)}, u32[]{:S(2)}) collective-permute-start(bf16[4,8,40,128]{3,2,1,0:T(8,128)(2,1)S(1)} %get-tuple-element.59), channel_id=1, source_target_pairs={{0,3},{8,11},{16,19},{24,27},{32,35},{40,43},{48,51},{56,59},{64,6... | collective-permute-start | bytes 983048 | tf_op jit(solution)/shard_map/ppermute | solution.py:46
  65.8 16.7 %collective-permute-start.21 = (bf16[4,8,40,128]{3,2,1,0:T(8,128)(2,1)S(1)}, bf16[4,8,40,128]{3,2,1,0:T(8,128)(2,1)S(1)}, u32[]{:S(2)}, u32[]{:S(2)}) collective-permute-start(bf16[4,8,40,128]{3,2,1,0:T(8,128)(2,1)S(1)} %get-tuple-element.67), channel_id=1, source_target_pairs={{0,12},{8,4},{16,28},{24,20},{32,44},{40,36},{48,60},{56,52},{64,7... | collective-permute-start | bytes 983048 | tf_op jit(solution)/shard_map/ppermute | solution.py:46
  65.9 19.8 %collective-permute-start.22 = (bf16[4,8,40,128]{3,2,1,0:T(8,128)(2,1)S(1)}, bf16[4,8,40,128]{3,2,1,0:T(8,128)(2,1)S(1)}, u32[]{:S(2)}, u32[]{:S(2)}) collective-permute-start(bf16[4,8,40,128]{3,2,1,0:T(8,128)(2,1)S(1)} %get-tuple-element.68), channel_id=1, source_target_pairs={{0,128},{8,136},{16,144},{24,152},{32,160},{40,168},{48,176},{56,1... | collective-permute-start | bytes 983048 | tf_op jit(solution)/shard_map/ppermute | solution.py:46
  70.7 15.4 %collective-permute-start.23 = (bf16[4,8,40,128]{3,2,1,0:T(8,128)(2,1)S(1)}, bf16[4,8,40,128]{3,2,1,0:T(8,128)(2,1)S(1)}, u32[]{:S(2)}, u32[]{:S(2)}) collective-permute-start(bf16[4,8,40,128]{3,2,1,0:T(8,128)(2,1)S(1)} %get-tuple-element.69), channel_id=1, source_target_pairs={{0,140},{8,132},{16,156},{24,148},{32,172},{40,164},{48,188},{56,1... | collective-permute-start | bytes 983048 | tf_op jit(solution)/shard_map/ppermute | solution.py:46
  76.3 13.5 %collective-permute-start.16 = (bf16[8,40,128]{2,1,0:T(8,128)(2,1)S(1)}, bf16[8,40,128]{2,1,0:T(8,128)(2,1)S(1)}, u32[]{:S(2)}, u32[]{:S(2)}) collective-permute-start(bf16[8,40,128]{2,1,0:T(8,128)(2,1)S(1)} %get-tuple-element.61), channel_id=1, source_target_pairs={{0,12},{8,4},{16,28},{24,20},{32,44},{40,36},{48,60},{56,52},{64,7... | collective-permute-start | bytes 245768 | tf_op jit(solution)/shard_map/ppermute | solution.py:46
  76.4 14.1 %collective-permute-start.17 = (bf16[8,40,128]{2,1,0:T(8,128)(2,1)S(1)}, bf16[8,40,128]{2,1,0:T(8,128)(2,1)S(1)}, u32[]{:S(2)}, u32[]{:S(2)}) collective-permute-start(bf16[8,40,128]{2,1,0:T(8,128)(2,1)S(1)} %get-tuple-element.62), channel_id=1, source_target_pairs={{0,128},{8,136},{16,144},{24,152},{32,160},{40,168},{48,176},{56,1... | collective-permute-start | bytes 245768 | tf_op jit(solution)/shard_map/ppermute | solution.py:46
  82.5 8.0 %collective-permute-start.18 = (bf16[8,40,128]{2,1,0:T(8,128)(2,1)S(1)}, bf16[8,40,128]{2,1,0:T(8,128)(2,1)S(1)}, u32[]{:S(2)}, u32[]{:S(2)}) collective-permute-start(bf16[8,40,128]{2,1,0:T(8,128)(2,1)S(1)} %get-tuple-element.63), channel_id=1, source_target_pairs={{0,140},{8,132},{16,156},{24,148},{32,172},{40,164},{48,188},{56,1... | collective-permute-start | bytes 245768 | tf_op jit(solution)/shard_map/ppermute | solution.py:46
  86.2 4.6 %collective-permute-start.24 = (bf16[8,40,128]{2,1,0:T(8,128)(2,1)S(1)}, bf16[8,40,128]{2,1,0:T(8,128)(2,1)S(1)}, u32[]{:S(2)}, u32[]{:S(2)}) collective-permute-start(bf16[8,40,128]{2,1,0:T(8,128)(2,1)S(1)} %get-tuple-element.71), channel_id=1, source_target_pairs={{0,1},{8,9},{16,17},{24,25},{32,33},{40,41},{48,49},{56,57},{64,65... | collective-permute-start | bytes 245768 | tf_op jit(solution)/shard_map/ppermute | solution.py:46
  86.9 7.2 %collective-permute-start.25 = (bf16[8,40,128]{2,1,0:T(8,128)(2,1)S(1)}, bf16[8,40,128]{2,1,0:T(8,128)(2,1)S(1)}, u32[]{:S(2)}, u32[]{:S(2)}) collective-permute-start(bf16[8,40,128]{2,1,0:T(8,128)(2,1)S(1)} %get-tuple-element.72), channel_id=1, source_target_pairs={{0,2},{8,10},{16,18},{24,26},{32,34},{40,42},{48,50},{56,58},{64,6... | collective-permute-start | bytes 245768 | tf_op jit(solution)/shard_map/ppermute | solution.py:46
  89.9 4.4 %collective-permute-start.26 = (bf16[8,40,128]{2,1,0:T(8,128)(2,1)S(1)}, bf16[8,40,128]{2,1,0:T(8,128)(2,1)S(1)}, u32[]{:S(2)}, u32[]{:S(2)}) collective-permute-start(bf16[8,40,128]{2,1,0:T(8,128)(2,1)S(1)} %get-tuple-element.73), channel_id=1, source_target_pairs={{0,3},{8,11},{16,19},{24,27},{32,35},{40,43},{48,51},{56,59},{64,6... | collective-permute-start | bytes 245768 | tf_op jit(solution)/shard_map/ppermute | solution.py:46
  121.3 7.2 %collective-permute-start.27 = (bf16[8,80,128]{2,1,0:T(8,128)(2,1)S(1)}, bf16[8,80,128]{2,1,0:T(8,128)(2,1)S(1)}, u32[]{:S(2)}, u32[]{:S(2)}) collective-permute-start(bf16[8,80,128]{2,1,0:T(8,128)(2,1)S(1)} %all_to_all.11.own), channel_id=1, source_target_pairs={{0,136},{8,4},{16,152},{24,20},{32,168},{40,36},{48,184},{56,52},{... | collective-permute-start | bytes 491528 | tf_op jit(solution)/shard_map/ppermute | solution.py:46
  124.7 6.2 %collective-permute-start.28 = (bf16[8,80,128]{2,1,0:T(8,128)(2,1)S(1)}, bf16[8,80,128]{2,1,0:T(8,128)(2,1)S(1)}, u32[]{:S(2)}, u32[]{:S(2)}) collective-permute-start(bf16[8,80,128]{2,1,0:T(8,128)(2,1)S(1)} %all_to_all.11.own), channel_id=1, source_target_pairs={{0,8},{8,132},{16,24},{24,148},{32,40},{40,164},{48,56},{56,180},{... | collective-permute-start | bytes 491528 | tf_op jit(solution)/shard_map/ppermute | solution.py:46
  128.4 3.5 %collective-permute-start.29 = (bf16[8,80,128]{2,1,0:T(8,128)(2,1)S(1)}, bf16[8,80,128]{2,1,0:T(8,128)(2,1)S(1)}, u32[]{:S(2)}, u32[]{:S(2)}) collective-permute-start(bf16[8,80,128]{2,1,0:T(8,128)(2,1)S(1)} %collective-permute-done.27.first), channel_id=1, source_target_pairs={{0,8},{8,0},{16,24},{24,16},{32,40},{40,32},{48,56},{56,48},{64,72... | collective-permute-start | bytes 491528 | tf_op jit(solution)/shard_map/ppermute | solution.py:46
  130.9 1.4 %collective-permute-start.30 = (bf16[8,80,128]{2,1,0:T(8,128)(2,1)S(1)}, bf16[8,80,128]{2,1,0:T(8,128)(2,1)S(1)}, u32[]{:S(2)}, u32[]{:S(2)}) collective-permute-start(bf16[8,80,128]{2,1,0:T(8,128)(2,1)S(1)} %collective-permute-done.28.second), channel_id=1, source_target_pairs={{0,8},{8,0},{16,24},{24,16},{32,40},{40,32},{48,56},{56,48},{64,72... | collective-permute-start | bytes 491528 | tf_op jit(solution)/shard_map/ppermute | solution.py:46

commit v3 on v2

v3 whole, which is shorter than its diff:
```python
import functools
import math

import jax
import jax.numpy as jnp
from jax import lax
from jax.experimental import pallas as pl
from jax.experimental.pallas import tpu as pltpu
from jax.sharding import PartitionSpec as P

HEADS = 40
NSTEPS = 1000
AXES = ("dp", "fsdp")
NX, NY, NZ, NC = 4, 4, 8, 2
BF16 = jnp.bfloat16
F32 = jnp.float32
NORM_CHUNKS = 4
LOG2E = math.log2(math.e)

CLIP = 192
WIDTH = 5120
HALF = WIDTH // 2
SHARD = 640
RANK = 128
HEAD = 128
LOCAL_HEADS = SHARD // HEAD
VMEM_LIMIT = 24 * 1024 * 1024
SMALL = pl.CostEstimate(flops=1000, bytes_accessed=1000, transcendentals=0)


def linear(x, y, z, c):
    x, y, z, c = x % NX, y % NY, z % NZ, c % NC
    return (((x // 2) * NZ + z) * NC + c) * 8 + (x % 2) * NY + y


def permutation(target):
    pairs = []
    for x in range(NX):
        for y in range(NY):
            for z in range(NZ):
                for c in range(NC):
                    pairs.append((linear(x, y, z, c), linear(*target(x, y, z, c))))
    return pairs


def send(value, target):
    return lax.ppermute(value, AXES, permutation(target))


def swap_cores(value):
    return send(value, lambda x, y, z, c: (x, y, z, 1 - c))


def send_y(value, step):
    return send(value, lambda x, y, z, c: (x, y + step, z, c))


Z_GROUPS = [
    [linear(x, y, z, c) for z in range(NZ)]
    for x in range(NX)
    for y in range(NY)
    for c in range(NC)
]


def scatter_x(parts):
    return [
        parts[0],
        send(parts[1], lambda x, y, z, c: (x + 1, y, z, 1 - c)),
        send(parts[2], lambda x, y, z, c: (x + 2, y, z, c)),
        send(parts[3], lambda x, y, z, c: (x - 1, y, z, 1 - c)),
    ]


def scatter_y(parts):
    return [parts[0]] + [send_y(parts[step], step) for step in range(1, NY)]


def exchange_z(value):
    return lax.all_to_all(value, AXES, 0, 0, axis_index_groups=Z_GROUPS, tiled=True)


def dot(a, b, ca, cb):
    return lax.dot_general(a, b, (((ca,), (cb,)), ((), ())), preferred_element_type=F32)


def whole(shape):
    return pl.BlockSpec(shape, lambda *_: (0,) * len(shape))


SCALARS = pl.BlockSpec(memory_space=pltpu.SMEM)
RESIDENT = pl.BlockSpec(memory_space=pltpu.VMEM)
ANYWHERE = pl.BlockSpec(memory_space=pl.ANY)


def call(kernel, name, out_shape, scratch, place, resident, after=()):
    outs = [jax.ShapeDtypeStruct(shape, dtype) for shape, dtype in out_shape]
    return pl.pallas_call(
        kernel,
        out_shape=outs,
        in_specs=[SCALARS] + [RESIDENT] * len(resident) + [ANYWHERE] * len(after),
        out_specs=[RESIDENT] * len(outs),
        scratch_shapes=[pltpu.VMEM(shape, dtype) for shape, dtype in scratch],
        compiler_params=pltpu.CompilerParams(vmem_limit_bytes=VMEM_LIMIT),
        cost_estimate=SMALL,
        name=name,
    )(place, *resident, *after)


def normalize_kernel(place, states, q, k, v, g, nown, nsend, held, sems):
    mine = pl.multiple_of(place[0] * HALF, HALF)
    other = pl.multiple_of((1 - place[0]) * HALF, HALF)
    size = CLIP // NORM_CHUNKS
    chunks = [
        pltpu.make_async_copy(
            states.at[pl.ds(n * size, size)], held.at[pl.ds(n * size, size)], sems.at[n]
        )
        for n in range(NORM_CHUNKS)
    ]
    copies = [
        pltpu.make_async_copy(
            src.at[:, pl.ds(other, HALF)], nsend.at[n], sems.at[NORM_CHUNKS + n]
        )
        for n, src in enumerate((q, k, v, g))
    ]
    for copy in chunks + copies:
        copy.start()

    def block(step, carry):
        rows = pl.ds(pl.multiple_of(step * 16, 16), 16)
        inputs = held[rows, :].astype(F32)
        mean = jnp.mean(inputs, axis=1, keepdims=True)
        center = inputs - mean
        spread = jnp.mean(center * center, axis=1, keepdims=True)
        inverse = lax.rsqrt(spread + 1e-06)
        for begin, out in ((mine, nown), (other, nsend.at[4])):
            part = held[rows, pl.ds(begin, HALF)].astype(F32)
            out[rows, :] = ((part - mean) * inverse).astype(BF16)
        return carry

    for n, copy in enumerate(chunks):
        copy.wait()
        lax.fori_loop(n * size // 16, (n + 1) * size // 16, block, 0)
    for copy in copies:
        copy.wait()


def normalize(place, *arrays):
    return pl.pallas_call(
        normalize_kernel,
        out_shape=[
            jax.ShapeDtypeStruct((CLIP, HALF), BF16),
            jax.ShapeDtypeStruct((5, CLIP, HALF), BF16),
        ],
        in_specs=[SCALARS] + [pl.BlockSpec(memory_space=pl.ANY)] * 5,
        out_specs=[RESIDENT] * 2,
        scratch_shapes=[
            pltpu.VMEM((CLIP, WIDTH), BF16),
            pltpu.SemaphoreType.DMA((NORM_CHUNKS + 4,)),
        ],
        compiler_params=pltpu.CompilerParams(vmem_limit_bytes=VMEM_LIMIT),
        cost_estimate=SMALL,
        name="normalize",
    )(place, *(pltpu.with_memory_space_constraint(array, pltpu.HBM) for array in arrays))


def lower_kernel(place, nown, npeer, own, other, weight, out0, out1):
    core, y = place[2], place[1]
    total = jnp.zeros((2 * CLIP, 2 * RANK), F32)
    for step in range(NY):
        at = pl.ds(pl.multiple_of(lax.rem(y + step, NY) * SHARD, SHARD), SHARD)
        rows = jnp.concatenate([nown[:, at], npeer[4, :, at]], axis=0)
        total += dot(rows, jnp.concatenate([own[step], other[step]], axis=1), 1, 0)
    for clip, out in enumerate((out0, out1)):
        out[core, :CLIP] = total[clip * CLIP : (clip + 1) * CLIP, :RANK]
        out[1 - core, :CLIP] = total[clip * CLIP : (clip + 1) * CLIP, RANK:]
        out[0, CLIP:] = weight[...]
        out[1, CLIP:] = weight[...]


def lower(place, *arrays):
    return call(lower_kernel, "lower", [((2, CLIP + 8, RANK), F32)] * 2, [], place, arrays)


def attend_kernel(steps, first, after, place, *refs):
    count = len(steps)
    own, peer, lows, given = refs[:4], refs[4], refs[5:9], refs[9 : 9 + count]
    refs = refs[9 + count + after :]
    gups, dlow0, dlow1, rest = refs[:count], refs[count], refs[count + 1], refs[count + 2 :]
    if first:
        mine0, mine1, peer0, peer1 = lows
        low, weights, ups, dqs, dvs = rest
        for j in range(2):
            for clip in range(2):
                total = (mine0, mine1)[clip][j, :CLIP] + (peer1, peer0)[clip][j, :CLIP]
                low[j, clip * CLIP : (clip + 1) * CLIP] = total.astype(BF16)
        weights[0] = mine0[0, CLIP:]
        weights[1] = peer0[0, CLIP:]
    else:
        low, weights, in0, in1 = lows
        ups, dqs, dvs = rest
    core = place[2]
    scale = 1.0 / math.sqrt(HEAD)
    clips = [slice(clip * CLIP, (clip + 1) * CLIP) for clip in range(2)]

    def load(n, clip):
        shard = lax.rem(place[1] + steps[n], NY) * SHARD
        if clip == 0:
            at = pl.ds(pl.multiple_of(place[0] * HALF + shard, SHARD), SHARD)
            q, k, v, g = (r[:, at] for r in own)
        else:
            at = pl.ds(pl.multiple_of(shard, SHARD), SHARD)
            q, k, v, g = (peer[m, :, at] for m in range(4))
        rows = clips[clip]
        query = (q.astype(F32) + dot(low[0, rows], ups[n, 0], 1, 0)).astype(BF16)
        value = (v.astype(F32) + dot(low[1, rows], ups[n, 1], 1, 0)).astype(BF16)
        for h in range(LOCAL_HEADS):
            cols = slice(h * HEAD, (h + 1) * HEAD)
            heads.append((n, clip, cols, query[:, cols], k[:, cols], value[:, cols], g[:, cols]))

    def products(head):
        query, key, value, grad = head[3:]
        return dot(key, query, 1, 1), dot(value, grad, 1, 1)

    def finish(head, probs, dscores):
        n, clip, cols, query, key, value, grad = head
        weight = weights[clip, :1]
        dvs[n, clips[clip], cols] = (dot(probs, grad, 1, 0) * weight).astype(BF16)
        dqs[n, clips[clip], cols] = (dot(dscores, key, 0, 0) * (weight * scale)).astype(BF16)

    def collect(n):
        for j, grads in enumerate((dqs, dvs)):
            for clip, out in enumerate((dlow0, dlow1)):
                total = dot(grads[n, clips[clip]], ups[n, j], 1, 1)
                if n == 0:
                    out[j] = total if first else (in0, in1)[clip][j] + total
                else:
                    out[j] += total
            store_pieces(gups[n], j, dot(low[j], grads[n], 0, 0))

    heads = []
    for n in range(count):
        ups[n, core] = given[n][0]
        ups[n, 1 - core] = given[n][1]
        for clip in range(2):
            load(n, clip)

    ready = products(heads[0])
    done = None
    for at, head in enumerate(heads):
        scores, dprobs = ready
        if at + 1 < len(heads):
            ready = products(heads[at + 1])
        if done is not None:
            finish(*done)
            if head[0] != done[0][0]:
                collect(done[0][0])
        top = jnp.max(scores, axis=0, keepdims=True)
        powers = jnp.exp2((scores - top) * (scale * LOG2E))
        probs = powers * (1.0 / jnp.sum(powers, axis=0, keepdims=True))
        inner = jnp.sum(probs * dprobs, axis=0, keepdims=True)
        done = (head, probs.astype(BF16), (probs * (dprobs - inner)).astype(BF16))
    finish(*done)
    collect(count - 1)


def lane_blocks(rows):
    return jnp.concatenate(
        [rows[:, h * HEAD : (h + 1) * HEAD] for h in range(LOCAL_HEADS)], axis=0
    )


def store_pieces(out, j, total):
    for piece in range(RANK // 8):
        at = j * (RANK // 8) + piece
        out[at // NZ, at % NZ] = lane_blocks(total[piece * 8 : (piece + 1) * 8]).astype(BF16)


PIECES = (4, NZ, 40, 128)
LOWS = (2, CLIP, RANK)


def attend(steps, after, place, arrays, peer, ups, *lows):
    first, count = lows[0].dtype == F32, len(steps)
    shapes = [(PIECES, BF16)] * count + [(LOWS, F32)] * 2
    if first:
        shapes += [((2, 2 * CLIP, RANK), BF16), ((2, 8, RANK), F32)]
    scratch = [((count, 2, RANK, SHARD), BF16)] + [((count, 2 * CLIP, SHARD), BF16)] * 2
    kernel = functools.partial(attend_kernel, steps, first, len(after))
    given = [ups[step] for step in steps]
    return call(
        kernel, "attend", shapes, scratch, place, (*arrays, peer, *lows, *given), after
    )


def down_kernel(after, place, nown, peer, mine0, mine1, peer0, peer1, *refs):
    *outs, dlow, totals = refs[after:]
    for j in range(2):
        for clip in range(2):
            total = (mine0, mine1)[clip][j] + (peer1, peer0)[clip][j]
            dlow[j * RANK : (j + 1) * RANK, clip * CLIP : (clip + 1) * CLIP] = total.astype(BF16).T
    for shift in range(NY):
        shard = pl.multiple_of(lax.rem(place[1] + shift, NY) * SHARD, SHARD)
        normed = jnp.concatenate([nown[:, pl.ds(shard, SHARD)], peer[4, :, pl.ds(shard, SHARD)]], axis=0)
        totals[shift] = dot(dlow[...], normed, 1, 0)
        for step, out in enumerate(outs):
            first = lax.rem(place[3] + step, NX) * (2 * RANK // NX)
            for z in range(NZ):
                rows = totals[shift, pl.ds(pl.multiple_of(first + z * 8, 8), 8), :]
                out[shift, z] = lane_blocks(rows).astype(BF16)


def down_grads(place, nown, peer, dlows, *after):
    shapes = [((NY, *PIECES[1:]), BF16)] * NX
    scratch = [((2 * RANK, 2 * CLIP), BF16), ((NY, 2 * RANK, SHARD), F32)]
    kernel = functools.partial(down_kernel, len(after))
    return call(kernel, "down_grads", shapes, scratch, place, (nown, peer, *dlows), after)


def sum_y_kernel(place, *refs):
    parts, outs = refs[:4], refs[4:]
    x = place[3]
    for quarter in range(4):
        source = lax.rem(quarter + x, 4)
        for z in range(NZ):
            total = sum(r[source, z].astype(F32) for r in parts)
            outs[quarter][z] = total.astype(BF16)


def sum_y(place, parts):
    return pl.pallas_call(
        sum_y_kernel,
        out_shape=[jax.ShapeDtypeStruct(PIECES[1:], BF16)] * 4,
        in_specs=[pl.BlockSpec(memory_space=pltpu.SMEM)]
        + [pl.BlockSpec(memory_space=pltpu.VMEM)] * 4,
        out_specs=[pl.BlockSpec(memory_space=pltpu.VMEM)] * 4,
        compiler_params=pltpu.CompilerParams(vmem_limit_bytes=VMEM_LIMIT),
        cost_estimate=SMALL,
        name="sum_y",
    )(place, *parts)


def sum_x_kernel(*refs):
    parts, outs = refs[:4], refs[4:]
    for step in range(NY):
        outs[step][...] = sum(r[step].astype(F32) for r in parts).astype(BF16)


def sum_x(parts):
    return pl.pallas_call(
        sum_x_kernel,
        out_shape=[jax.ShapeDtypeStruct(PIECES[1:], BF16)] * NY,
        in_specs=[pl.BlockSpec(memory_space=pltpu.VMEM)] * 4,
        out_specs=[pl.BlockSpec(memory_space=pltpu.VMEM)] * NY,
        compiler_params=pltpu.CompilerParams(vmem_limit_bytes=VMEM_LIMIT),
        cost_estimate=SMALL,
        name="sum_x",
    )(*parts)


def join_kernel(*refs):
    ups, downs, out = refs[:4], refs[4:8], refs[8]
    for z in range(NZ):
        up = sum(r[z].astype(F32) for r in ups)
        down = sum(r[z].astype(F32) for r in downs)
        out[z] = jnp.concatenate([up, down], axis=0).astype(BF16)


def join(ups, downs):
    return pl.pallas_call(
        join_kernel,
        out_shape=jax.ShapeDtypeStruct((NZ, 80, 128), BF16),
        in_specs=[pl.BlockSpec(memory_space=pltpu.VMEM)] * 8,
        out_specs=pl.BlockSpec(memory_space=pltpu.VMEM),
        compiler_params=pltpu.CompilerParams(vmem_limit_bytes=VMEM_LIMIT),
        cost_estimate=SMALL,
        name="join",
    )(*ups, *downs)


def finish_kernel(factor, place, own, first, second, first_peer, second_peer, down, up, flat):
    core, x = place[2], place[3]

    def write(step, ref):
        quarter = lax.rem(x + step, 4)
        for z in range(NZ):
            part = ref[z].astype(F32) * factor
            for out, begin in ((up, 0), (flat, 40)):
                out[quarter * NZ + z] = jnp.concatenate(
                    [part[begin + h * 8 : begin + (h + 1) * 8] for h in range(LOCAL_HEADS)], axis=1
                )

    @pl.when(core == 0)
    def _():
        for step, ref in enumerate((own, second, first_peer, first)):
            write(step, ref)

    @pl.when(core == 1)
    def _():
        for step, ref in enumerate((second, second_peer, first, first_peer)):
            write(step, ref)

    for j in range(2):
        rows = flat[j * 2 * NZ : (j + 1) * 2 * NZ].reshape(RANK, SHARD)
        down[j] = rows.T


def finish(factor, place, *parts):
    return pl.pallas_call(
        functools.partial(finish_kernel, factor),
        out_shape=(
            jax.ShapeDtypeStruct((2, SHARD, RANK), F32),
            jax.ShapeDtypeStruct((4 * NZ, 8, SHARD), F32),
        ),
        in_specs=[pl.BlockSpec(memory_space=pltpu.SMEM)]
        + [pl.BlockSpec(memory_space=pltpu.VMEM)] * 5,
        out_specs=(pl.BlockSpec(memory_space=pltpu.VMEM),) * 2,
        scratch_shapes=[pltpu.VMEM((4 * NZ, 8, SHARD), F32)],
        compiler_params=pltpu.CompilerParams(vmem_limit_bytes=VMEM_LIMIT),
        name="finish",
    )(place, *parts)


def cross_x(part):
    other = send(part, lambda x, y, z, c: (x - 1, y, z, 1) if c == 0 else (x, y, z, 0))
    own = send(part, lambda x, y, z, c: (x, y, z, 0) if c == 0 else (x + 1, y, z, 1))
    return own, other


def local(states, steps, q, k, v, g, down_maps, up_maps):
    dp, fsdp = lax.axis_index("dp"), lax.axis_index("fsdp")
    core, x_lo, y = dp % 2, fsdp // NY, fsdp % NY
    x = (dp // (2 * NZ)) * 2 + x_lo
    place = jnp.stack([x_lo ^ core, y, core, x]).astype(jnp.int32)
    weight = (steps[0].astype(F32) + 1.0) / NSTEPS
    weight = jnp.full((8, RANK), weight, F32)

    down_part = lax.dynamic_index_in_dim(down_maps, core, 0, keepdims=False)
    up_part = lax.dynamic_index_in_dim(up_maps, core, 0, keepdims=False)
    nown, nsend = normalize(place, states, q, k, v, g)
    downs = [send_y(down_part, -step) for step in range(1, NY)]
    up = jnp.stack(cross_x(up_part))
    nsend, up, *downs = lax.optimization_barrier((nsend, up, *downs))
    downs = cross_x(jnp.stack([down_part, *downs]))
    ups = [up] + [send_y(up, -step) for step in range(1, NY)]
    peer = swap_cores(nsend)

    lows = lower(place, nown, peer, *downs, weight)
    lows = [*lows, *(swap_cores(part) for part in lows)]
    rows = (place, (q, k, v, g), peer, ups)
    gups = [None] * NY
    gups[1], gups[3], *dlow, low, weights = attend((1, 3), (), *rows, *lows)
    gups[1], gups[3] = send_y(gups[1], 1), send_y(gups[3], 3)
    gups[2], gups[0], *dlow = attend((2, 0), (), *rows, low, weights, *dlow)
    gups[2] = send_y(gups[2], 2)
    dlows = [*dlow, *(swap_cores(part) for part in dlow)]
    gdowns = scatter_x(down_grads(place, nown, peer, dlows, gups[1], gups[3]))
    ups = scatter_x(sum_y(place, gups))
    downs = scatter_y(sum_x(gdowns))
    eighths = join(ups, downs)
    eighths = exchange_z(eighths)
    piece = jnp.sum(eighths.astype(F32), axis=0).astype(BF16)
    quarter = exchange_z(jnp.broadcast_to(piece, (NZ, 80, 128)))

    first = send(
        quarter, lambda x, y, z, c: (x + 2, y, z, 1) if c == 0 else (x + 1, y, z, 0)
    )
    second = send(
        quarter, lambda x, y, z, c: (x, y, z, 1) if c == 0 else (x - 1, y, z, 0)
    )
    first_peer = swap_cores(first)
    second_peer = swap_cores(second)
    data_count = lax.axis_size("dp") * lax.axis_size("fsdp")
    factor = 1.0 / math.sqrt(CLIP * data_count)
    grad_down, grad_up = finish(
        factor, place, quarter, first, second, first_peer, second_peer
    )
    return (grad_down, grad_up.reshape(2, RANK, SHARD))


def solution(mesh):
    in_specs = (
        P(("dp", "fsdp"), None),
        P(("dp", "fsdp")),
        P(("dp", "fsdp"), None),
        P(("dp", "fsdp"), None),
        P(("dp", "fsdp"), None),
        P(("dp", "fsdp"), None),
        P(None, "fsdp", None),
        P(None, None, "fsdp"),
    )
    out_specs = (P(None, "fsdp", None), P(None, None, "fsdp"))
    return jax.shard_map(local, mesh=mesh, in_specs=in_specs, out_specs=out_specs, check_vma=False)
```

time: 134 us -> 125 us (0.933)
  Pallas kernels: 28.9 us -> 21.3 us
  starting transfers between devices: 45.5 us -> 40.3 us
  waiting for transfers between devices: 29.5 us -> 33 us
    pallas_call x7 -> x5, Pallas kernels: 26.2 us -> 18.6 us  [the longest x4 13.6 us: call(): pl.pallas_call(kernel, out_shape=outs, in_specs=[SCALARS] + [RESIDENT] *...]
    ppermute x31, starting transfers between devices: 45.5 us -> 40.3 us  [send(): return lax.ppermute(value, AXES, permutation(target))]
    ppermute x31, waiting for transfers between devices: 29.5 us -> 33 us  [send(): return lax.ppermute(value, AXES, permutation(target))]
  transfers between devices with their start and end apart: 31 -> 31, of which waited for: 15 -> 17; matrix products, arithmetic and copies ran while one was open for 1% -> 0% of each run, Pallas kernels for 20% -> 16%
where the time goes in v3:
time: 125 us
  starting transfers between devices  40.3 us (32%)
  waiting for transfers between devices  33 us (26%)
  blocking collectives  27.1 us (22%)
  Pallas kernels  21.3 us (17%)
  between operations  1.54 us (1%)
    ppermute x31, starting transfers between devices, send(): return lax.ppermute(value, AXES, permutation(target))  40.3 us
    ppermute x31, waiting for transfers between devices, send(): return lax.ppermute(value, AXES, permutation(target))  33 us
    all_to_all x2, blocking collectives, exchange_z(): lax.all_to_all(value, AXES, 0, 0, axis_index_groups=Z_GROUPS, tiled=True)  27.1 us
    pallas_call x4, Pallas kernels, call(): pl.pallas_call(kernel, out_shape=outs, in_specs=[SCALARS] + [RESIDENT] *...  13.6 us
    pallas_call x1, Pallas kernels, normalize(): pl.pallas_call(normalize_kernel, out_shape=[jax.ShapeDtypeStruct((CLIP, H...  5.02 us
  transfers between devices with their start and end apart: 31, of which 17 were waited for; matrix products, arithmetic and copies ran while one was open for 0% of the time, Pallas kernels for 16%

profile of v3, /device:TPU:1, one launch (start us, length us, event | category | flops | bytes accessed | tf_op | source)
XLA Modules:
  0.0 124.6 jit_solution(11996917106995963747)
XLA Ops:
  0.7 1.0 dynamic-slice_bitcast_fusion
  1.6 3.3 %collective-permute-start.1 = (bf16[128,640]{1,0:T(8,128)(2,1)S(1)}, bf16[128,640]{1,0:T(8,128)(2,1)S(1)}, u32[]{:S(2)}, u32[]{:S(2)}) collective-permute-start(bf16[128,640]{1,0:T(8,128)(2,1)S(1)} %dynamic-slice_bitcast_fusion), channel_id=1, source_target_pairs={{0,140},{8,0},{16,156},{24,16},{32,172},{40,32},{48,188},{56,48},{... | collective-permute-start | bytes 491528 | tf_op jit(solution)/shard_map/ppermute | solution.py:47
  4.9 1.9 %collective-permute-start = (bf16[128,640]{1,0:T(8,128)(2,1)S(1)}, bf16[128,640]{1,0:T(8,128)(2,1)S(1)}, u32[]{:S(2)}, u32[]{:S(2)}) collective-permute-start(bf16[128,640]{1,0:T(8,128)(2,1)S(1)} %dynamic-slice_bitcast_fusion), channel_id=1, source_target_pairs={{0,0},{8,12},{16,16},{24,28},{32,32},{40,44},{48,48},{56,60},{64,6... | collective-permute-start | bytes 491528 | tf_op jit(solution)/shard_map/ppermute | solution.py:47
  6.8 2.3 %collective-permute-start.2 = (bf16[640,128]{1,0:T(8,128)(2,1)S(1)}, bf16[640,128]{1,0:T(8,128)(2,1)S(1)}, u32[]{:S(2)}, u32[]{:S(2)}) collective-permute-start(bf16[640,128]{1,0:T(8,128)(2,1)S(1)} %fusion), channel_id=1, source_target_pairs={{0,3},{8,11},{16,19},{24,27},{32,35},{40,43},{48,51},{56,59},{64,6... | collective-permute-start | bytes 491528 | tf_op jit(solution)/shard_map/ppermute | solution.py:47
  9.1 0.3 collective-permute-start.3
  9.5 0.7 collective-permute-start.4
  10.2 5.0 %normalize.1 = (bf16[192,2560]{1,0:T(8,128)(2,1)S(1)}, bf16[5,192,2560]{2,1,0:T(8,128)(2,1)S(1)}) custom-call(s32[4]{0:T(128)S(1)} %pad_add_fusion.place, bf16[192,5120]{1,0:T(8,128)(2,1)} %states.1, bf16[192,5120]{1,0:T(8,128)(2,1)} %refs_0_.3, bf16[192,5120]{1,0:T(8,128)(2,1)} %refs_1_.3, bf16[192,5120]{1,0:T(8,128)(2,1)} %refs_2_.3, bf16[192,5120]{1,0:T(8,128)(2,1)} %refs_3_.3), custom_call_target="tpu_custom_call" | custom-call | flops 1000 | bytes 1000 | tf_op jit(solution)/shard_map/normalize/pallas_call | solution.py:149
  15.3 1.0 collective-permute-done.2
  16.5 3.8 %collective-permute-done.4 = bf16[640,128]{1,0:T(8,128)(2,1)S(1)} collective-permute-done((bf16[640,128]{1,0:T(8,128)(2,1)S(1)}, bf16[640,128]{1,0:T(8,128)(2,1)S(1)}, u32[]{:S(2)}, u32[]{:S(2)}) %collective-permute-start.4) | collective-permute-done | bytes 163872 | tf_op jit(solution)/shard_map/ppermute | solution.py:47
  20.3 0.5 collective-permute-start.5
  20.9 2.1 %collective-permute-start.6 = (bf16[4,640,128]{2,1,0:T(8,128)(2,1)S(1)}, bf16[4,640,128]{2,1,0:T(8,128)(2,1)S(1)}, u32[]{:S(2)}, u32[]{:S(2)}) collective-permute-start(bf16[4,640,128]{2,1,0:T(8,128)(2,1)S(1)} %pad_maximum_fusion), channel_id=1, source_target_pairs={{0,0},{8,12},{16,16},{24,28},{32,32},{40,44},{48,48},{56,60},{64,6... | collective-permute-start | bytes 1966088 | tf_op jit(solution)/shard_map/ppermute | solution.py:47
  23.0 0.4 collective-permute-start.10
  23.4 1.1 collective-permute-start.11
  25.2 8.7 %collective-permute-done.6.own = bf16[4,640,128]{2,1,0:T(8,128)(2,1)S(1)} collective-permute-done((bf16[4,640,128]{2,1,0:T(8,128)(2,1)S(1)}, bf16[4,640,128]{2,1,0:T(8,128)(2,1)S(1)}, u32[]{:S(2)}, u32[]{:S(2)}) %collective-permute-start.6) | collective-permute-done | bytes 655392 | tf_op jit(solution)/shard_map/ppermute | solution.py:47
  33.9 1.3 %lower.1 = (f32[2,200,128]{2,1,0:T(8,128)S(1)}, f32[2,200,128]{2,1,0:T(8,128)S(1)}) custom-call(s32[4]{0:T(128)S(1)} %pad_add_fusion.place, bf16[192,2560]{1,0:T(8,128)(2,1)S(1)} %get-tuple-element.37.nown, bf16[5,192,2560]{2,1,0:T(8,128)(2,1)S(1)} %collective-permute-done.5.npeer.refs_4_.peer, bf16[4,640,128]{2,1,0:T(8,128)(2,1)S(1)} %collective-permute-done.6.own, ...), custom_call_target="tpu_custom_call" | custom-call | flops 1000 | bytes 1000 | tf_op jit(solution)/shard_map/lower/pallas_call | solution.py:98
  35.2 0.3 collective-permute-start.8
  35.5 0.3 collective-permute-start.9
  36.0 0.8 collective-permute-done.8.refs_7_
  36.8 0.3 collective-permute-done.9.refs_8_
  37.1 5.3 %attend.2 = (bf16[4,8,40,128]{3,2,1,0:T(8,128)(2,1)S(1)}, bf16[4,8,40,128]{3,2,1,0:T(8,128)(2,1)S(1)}, f32[2,192,128]{2,1,0:T(8,128)S(1)}, f32[2,192,128]{2,1,0:...) custom-call(s32[4]{0:T(128)S(1)} %pad_add_fusion.place, bf16[192,5120]{1,0:T(8,128)(2,1)S(1)} %copy-done.1, ...), custom_call_target="tpu_custom_call" | custom-call | flops 1000 | bytes 1000 | tf_op jit(solution)/shard_map/attend/pallas_call | solution.py:98
  42.3 0.3 collective-permute-start.13
  42.6 2.7 %collective-permute-start.15 = (bf16[4,8,40,128]{3,2,1,0:T(8,128)(2,1)S(1)}, bf16[4,8,40,128]{3,2,1,0:T(8,128)(2,1)S(1)}, u32[]{:S(2)}, u32[]{:S(2)}) collective-permute-start(bf16[4,8,40,128]{3,2,1,0:T(8,128)(2,1)S(1)} %get-tuple-element.51), channel_id=1, source_target_pairs={{0,3},{8,11},{16,19},{24,27},{32,35},{40,43},{48,51},{56,59},{64,6... | collective-permute-start | bytes 983048 | tf_op jit(solution)/shard_map/ppermute | solution.py:47
  45.3 1.1 collective-permute-done.12.refs_9_
  46.4 5.2 %attend.3 = (bf16[4,8,40,128]{3,2,1,0:T(8,128)(2,1)S(1)}, bf16[4,8,40,128]{3,2,1,0:T(8,128)(2,1)S(1)}, f32[2,192,128]{2,1,0:T(8,128)S(1)}, f32[2,192,128]{2,1,0:T(8,128)S(1)}) custom-call(s32[4]{0:T(128)S(1)} %pad_add_fusion.place, bf16[192,5120]{1,0:T(8,128)(2,1)S(1)} %copy-done.1, bf16[192,5120]{1,0:T(8,128)(2,1)S(1)} %copy-done.2, ...), custom_call_target="tpu_custom_call" | custom-call | flops 1000 | bytes 1000 | tf_op jit(solution)/shard_map/attend/pallas_call | solution.py:98
  51.6 1.8 %collective-permute-start.19 = (f32[2,192,128]{2,1,0:T(8,128)S(1)}, f32[2,192,128]{2,1,0:T(8,128)S(1)}, u32[]{:S(2)}, u32[]{:S(2)}) collective-permute-start(f32[2,192,128]{2,1,0:T(8,128)S(1)} %get-tuple-element.56.mine0), channel_id=1, source_target_pairs={{0,8},{8,0},{16,24},{24,16},{32,40},{40,32},{48,56},{56,48},{64,72... | collective-permute-start | bytes 589832 | tf_op jit(solution)/shard_map/ppermute | solution.py:47
  53.5 1.0 collective-permute-done.19.peer0
  54.5 0.4 collective-permute-done.20.peer1
  54.8 1.9 %down_grads.1 = (bf16[4,8,40,128]{3,2,1,0:T(8,128)(2,1)S(1)}, bf16[4,8,40,128]{3,2,1,0:T(8,128)(2,1)S(1)}, bf16[4,8,40,128]{3,2,1,0:T(8,128)(2,1)S(1)}, bf16[4,8,40,128]{3,2,1,0:T(8,128)(2,1)S(1)}) custom-call(s32[4]{0:T(128)S(1)} %pad_add_fusion.place, bf16[192,2560]{1,0:T(8,128)(2,1)S(1)} %get-tuple-element.37.nown, ...), custom_call_target="tpu_custom_call" | custom-call | flops 1000 | bytes 1000 | tf_op jit(solution)/shard_map/down_grads/pallas_call | solution.py:98
  56.8 4.3 %collective-permute-start.22 = (bf16[4,8,40,128]{3,2,1,0:T(8,128)(2,1)S(1)}, bf16[4,8,40,128]{3,2,1,0:T(8,128)(2,1)S(1)}, u32[]{:S(2)}, u32[]{:S(2)}) collective-permute-start(bf16[4,8,40,128]{3,2,1,0:T(8,128)(2,1)S(1)} %get-tuple-element.60), channel_id=1, source_target_pairs={{0,128},{8,136},{16,144},{24,152},{32,160},{40,168},{48,176},{56,1... | collective-permute-start | bytes 983048 | tf_op jit(solution)/shard_map/ppermute | solution.py:47
  61.1 2.8 %collective-permute-done.14.refs_2_ = bf16[4,8,40,128]{3,2,1,0:T(8,128)(2,1)S(1)} collective-permute-done((bf16[4,8,40,128]{3,2,1,0:T(8,128)(2,1)S(1)}, bf16[4,8,40,128]{3,2,1,0:T(8,128)(2,1)S(1)}, u32[]{:S(2)}, u32[]{:S(2)}) %collective-permute-start.14) | collective-permute-done | bytes 327712 | tf_op jit(solution)/shard_map/ppermute | solution.py:47
  63.9 0.7 sum_y.1
  64.6 1.0 collective-permute-start.16
  65.6 4.3 %collective-permute-start.17 = (bf16[8,40,128]{2,1,0:T(8,128)(2,1)S(1)}, bf16[8,40,128]{2,1,0:T(8,128)(2,1)S(1)}, u32[]{:S(2)}, u32[]{:S(2)}) collective-permute-start(bf16[8,40,128]{2,1,0:T(8,128)(2,1)S(1)} %get-tuple-element.54), channel_id=1, source_target_pairs={{0,128},{8,136},{16,144},{24,152},{32,160},{40,168},{48,176},{56,1... | collective-permute-start | bytes 245768 | tf_op jit(solution)/shard_map/ppermute | solution.py:47
  69.9 6.2 %collective-permute-done.22.refs_2_ = bf16[4,8,40,128]{3,2,1,0:T(8,128)(2,1)S(1)} collective-permute-done((bf16[4,8,40,128]{3,2,1,0:T(8,128)(2,1)S(1)}, bf16[4,8,40,128]{3,2,1,0:T(8,128)(2,1)S(1)}, u32[]{:S(2)}, u32[]{:S(2)}) %collective-permute-start.22) | collective-permute-done | bytes 327712 | tf_op jit(solution)/shard_map/ppermute | solution.py:47
  76.1 0.3 collective-permute-done.23.refs_3_
  76.7 2.9 %collective-permute-start.25 = (bf16[8,40,128]{2,1,0:T(8,128)(2,1)S(1)}, bf16[8,40,128]{2,1,0:T(8,128)(2,1)S(1)}, u32[]{:S(2)}, u32[]{:S(2)}) collective-permute-start(bf16[8,40,128]{2,1,0:T(8,128)(2,1)S(1)} %get-tuple-element.64), channel_id=1, source_target_pairs={{0,2},{8,10},{16,18},{24,26},{32,34},{40,42},{48,50},{56,58},{64,6... | collective-permute-start | bytes 245768 | tf_op jit(solution)/shard_map/ppermute | solution.py:47
  79.6 1.3 %collective-permute-start.26 = (bf16[8,40,128]{2,1,0:T(8,128)(2,1)S(1)}, bf16[8,40,128]{2,1,0:T(8,128)(2,1)S(1)}, u32[]{:S(2)}, u32[]{:S(2)}) collective-permute-start(bf16[8,40,128]{2,1,0:T(8,128)(2,1)S(1)} %get-tuple-element.65), channel_id=1, source_target_pairs={{0,3},{8,11},{16,19},{24,27},{32,35},{40,43},{48,51},{56,59},{64,6... | collective-permute-start | bytes 245768 | tf_op jit(solution)/shard_map/ppermute | solution.py:47
  80.9 0.3 collective-permute-done.24.refs_5_
  81.2 2.8 %collective-permute-done.25.refs_6_ = bf16[8,40,128]{2,1,0:T(8,128)(2,1)S(1)} collective-permute-done((bf16[8,40,128]{2,1,0:T(8,128)(2,1)S(1)}, bf16[8,40,128]{2,1,0:T(8,128)(2,1)S(1)}, u32[]{:S(2)}, u32[]{:S(2)}) %collective-permute-start.25) | collective-permute-done | bytes 81952 | tf_op jit(solution)/shard_map/ppermute | solution.py:47
  84.0 16.4 %all_to_all.10 = bf16[8,80,128]{2,1,0:T(8,128)(2,1)S(1)} all-to-all(bf16[8,80,128]{2,1,0:T(8,128)(2,1)S(1)} %join.1), channel_id=1, replica_groups={{0,16,32,48,64,80,96,112},{8,24,40,56,72,88,104,120},{1,17,33,49,65,81,..., dimensions={0} | all-to-all | bytes 327680 | tf_op jit(solution)/shard_map/all_to_all | solution.py:80
  100.5 10.8 %all_to_all.11.own = bf16[8,80,128]{2,1,0:T(8,128)(2,1)S(1)} all-to-all(bf16[8,80,128]{2,1,0:T(8,128)(2,1)S(1)} %broadcast_in_dim.7), channel_id=1, replica_groups={{0,16,32,48,64,80,96,112},{8,24,40,56,72,88,104,120},{1,17,33,49,65,81,..., dimensions={0} | all-to-all | bytes 327680 | tf_op jit(solution)/shard_map/all_to_all | solution.py:80
  111.2 3.8 %collective-permute-start.27 = (bf16[8,80,128]{2,1,0:T(8,128)(2,1)S(1)}, bf16[8,80,128]{2,1,0:T(8,128)(2,1)S(1)}, u32[]{:S(2)}, u32[]{:S(2)}) collective-permute-start(bf16[8,80,128]{2,1,0:T(8,128)(2,1)S(1)} %all_to_all.11.own), channel_id=1, source_target_pairs={{0,136},{8,4},{16,152},{24,20},{32,168},{40,36},{48,184},{56,52},{... | collective-permute-start | bytes 491528 | tf_op jit(solution)/shard_map/ppermute | solution.py:47
  115.1 2.0 %collective-permute-start.28 = (bf16[8,80,128]{2,1,0:T(8,128)(2,1)S(1)}, bf16[8,80,128]{2,1,0:T(8,128)(2,1)S(1)}, u32[]{:S(2)}, u32[]{:S(2)}) collective-permute-start(bf16[8,80,128]{2,1,0:T(8,128)(2,1)S(1)} %all_to_all.11.own), channel_id=1, source_target_pairs={{0,8},{8,132},{16,24},{24,148},{32,40},{40,164},{48,56},{56,180},{... | collective-permute-start | bytes 491528 | tf_op jit(solution)/shard_map/ppermute | solution.py:47
  117.1 2.0 %collective-permute-done.27.first = bf16[8,80,128]{2,1,0:T(8,128)(2,1)S(1)} collective-permute-done((bf16[8,80,128]{2,1,0:T(8,128)(2,1)S(1)}, bf16[8,80,128]{2,1,0:T(8,128)(2,1)S(1)}, u32[]{:S(2)}, u32[]{:S(2)}) %collective-permute-start.27) | collective-permute-done | bytes 163872 | tf_op jit(solution)/shard_map/ppermute | solution.py:47
  119.1 2.4 %collective-permute-start.29 = (bf16[8,80,128]{2,1,0:T(8,128)(2,1)S(1)}, bf16[8,80,128]{2,1,0:T(8,128)(2,1)S(1)}, u32[]{:S(2)}, u32[]{:S(2)}) collective-permute-start(bf16[8,80,128]{2,1,0:T(8,128)(2,1)S(1)} %collective-permute-done.27.first), channel_id=1, source_target_pairs={{0,8},{8,0},{16,24},{24,16},{32,40},{40,32},{48,56},{56,48},{64,72... | collective-permute-start | bytes 491528 | tf_op jit(solution)/shard_map/ppermute | solution.py:47
  121.5 1.0 collective-permute-done.29.first_peer
  122.5 0.4 collective-permute-done.30.second_peer
  122.9 1.7 %finish.1 = (f32[2,640,128]{2,1,0:T(8,128)}, f32[32,8,640]{2,1,0:T(8,128)}) custom-call(s32[4]{0:T(128)S(1)} %pad_add_fusion.place, bf16[8,80,128]{2,1,0:T(8,128)(2,1)S(1)} %all_to_all.11.own, bf16[8,80,128]{2,1,0:T(8,128)(2,1)S(1)} %collective-permute-done.27.first, bf16[8,80,128]{2,1,0:T(8,128)(2,1)S(1)} %collective-permute-done.28.second, ...), custom_call_target="tpu_custom_call" | custom-call | tf_op jit(solution)/shard_map/finish/pallas_call | solution.py:409
  (44 shorter events, 1.3 us)
Async XLA Ops:
  0.6 6.2 %copy-start = (bf16[2,640,128]{2,1,0:T(8,128)(2,1)S(1)}, bf16[2,640,128]{2,1,0:T(8,128)(2,1)}, u32[]{:S(2)}) copy-start(bf16[2,640,128]{2,1,0:T(8,128)(2,1)} %param.14) | copy-start | bytes 983044
  1.6 13.6 %collective-permute-start.1 = (bf16[128,640]{1,0:T(8,128)(2,1)S(1)}, bf16[128,640]{1,0:T(8,128)(2,1)S(1)}, u32[]{:S(2)}, u32[]{:S(2)}) collective-permute-start(bf16[128,640]{1,0:T(8,128)(2,1)S(1)} %dynamic-slice_bitcast_fusion), channel_id=1, source_target_pairs={{0,140},{8,0},{16,156},{24,16},{32,172},{40,32},{48,188},{56,48},{... | collective-permute-start | bytes 491528 | tf_op jit(solution)/shard_map/ppermute | solution.py:47
  4.9 10.4 %collective-permute-start = (bf16[128,640]{1,0:T(8,128)(2,1)S(1)}, bf16[128,640]{1,0:T(8,128)(2,1)S(1)}, u32[]{:S(2)}, u32[]{:S(2)}) collective-permute-start(bf16[128,640]{1,0:T(8,128)(2,1)S(1)} %dynamic-slice_bitcast_fusion), channel_id=1, source_target_pairs={{0,0},{8,12},{16,16},{24,28},{32,32},{40,44},{48,48},{56,60},{64,6... | collective-permute-start | bytes 491528 | tf_op jit(solution)/shard_map/ppermute | solution.py:47
  6.8 9.4 %collective-permute-start.2 = (bf16[640,128]{1,0:T(8,128)(2,1)S(1)}, bf16[640,128]{1,0:T(8,128)(2,1)S(1)}, u32[]{:S(2)}, u32[]{:S(2)}) collective-permute-start(bf16[640,128]{1,0:T(8,128)(2,1)S(1)} %fusion), channel_id=1, source_target_pairs={{0,3},{8,11},{16,19},{24,27},{32,35},{40,43},{48,51},{56,59},{64,6... | collective-permute-start | bytes 491528 | tf_op jit(solution)/shard_map/ppermute | solution.py:47
  9.1 7.3 %collective-permute-start.3 = (bf16[640,128]{1,0:T(8,128)(2,1)S(1)}, bf16[640,128]{1,0:T(8,128)(2,1)S(1)}, u32[]{:S(2)}, u32[]{:S(2)}) collective-permute-start(bf16[640,128]{1,0:T(8,128)(2,1)S(1)} %fusion), channel_id=1, source_target_pairs={{0,2},{8,10},{16,18},{24,26},{32,34},{40,42},{48,50},{56,58},{64,6... | collective-permute-start | bytes 491528 | tf_op jit(solution)/shard_map/ppermute | solution.py:47
  9.5 10.8 %collective-permute-start.4 = (bf16[640,128]{1,0:T(8,128)(2,1)S(1)}, bf16[640,128]{1,0:T(8,128)(2,1)S(1)}, u32[]{:S(2)}, u32[]{:S(2)}) collective-permute-start(bf16[640,128]{1,0:T(8,128)(2,1)S(1)} %fusion), channel_id=1, source_target_pairs={{0,1},{8,9},{16,17},{24,25},{32,33},{40,41},{48,49},{56,57},{64,65... | collective-permute-start | bytes 491528 | tf_op jit(solution)/shard_map/ppermute | solution.py:47
  20.3 13.6 %collective-permute-start.5 = (bf16[5,192,2560]{2,1,0:T(8,128)(2,1)S(1)}, bf16[5,192,2560]{2,1,0:T(8,128)(2,1)S(1)}, u32[]{:S(2)}, u32[]{:S(2)}) collective-permute-start(bf16[5,192,2560]{2,1,0:T(8,128)(2,1)S(1)} %get-tuple-element.36), channel_id=1, source_target_pairs={{0,8},{8,0},{16,24},{24,16},{32,40},{40,32},{48,56},{56,48},{64,72... | collective-permute-start | bytes 14745608 | tf_op jit(solution)/shard_map/ppermute | solution.py:47
  20.8 16.3 %copy-start.4 = (bf16[192,5120]{1,0:T(8,128)(2,1)S(1)}, bf16[192,5120]{1,0:T(8,128)(2,1)}, u32[]{:S(2)}) copy-start(bf16[192,5120]{1,0:T(8,128)(2,1)} %refs_3_.3) | copy-start | bytes 5898244
  20.9 13.0 %collective-permute-start.6 = (bf16[4,640,128]{2,1,0:T(8,128)(2,1)S(1)}, bf16[4,640,128]{2,1,0:T(8,128)(2,1)S(1)}, u32[]{:S(2)}, u32[]{:S(2)}) collective-permute-start(bf16[4,640,128]{2,1,0:T(8,128)(2,1)S(1)} %pad_maximum_fusion), channel_id=1, source_target_pairs={{0,0},{8,12},{16,16},{24,28},{32,32},{40,44},{48,48},{56,60},{64,6... | collective-permute-start | bytes 1966088 | tf_op jit(solution)/shard_map/ppermute | solution.py:47
  22.9 10.9 %collective-permute-start.7 = (bf16[4,640,128]{2,1,0:T(8,128)(2,1)S(1)}, bf16[4,640,128]{2,1,0:T(8,128)(2,1)S(1)}, u32[]{:S(2)}, u32[]{:S(2)}) collective-permute-start(bf16[4,640,128]{2,1,0:T(8,128)(2,1)S(1)} %pad_maximum_fusion), channel_id=1, source_target_pairs={{0,140},{8,0},{16,156},{24,16},{32,172},{40,32},{48,188},{56,48},{... | collective-permute-start | bytes 1966088 | tf_op jit(solution)/shard_map/ppermute | solution.py:47
  23.0 13.0 %collective-permute-start.10 = (bf16[2,128,640]{2,1,0:T(8,128)(2,1)S(1)}, bf16[2,128,640]{2,1,0:T(8,128)(2,1)S(1)}, u32[]{:S(2)}, u32[]{:S(2)}) collective-permute-start(bf16[2,128,640]{2,1,0:T(8,128)(2,1)S(1)} %pad_maximum_fusion.1.refs_10_), channel_id=1, source_target_pairs={{0,3},{8,11},{16,19},{24,27},{32,35},{40,43},{48,51},{56,59},{64,6... | collective-permute-start | bytes 983048 | tf_op jit(solution)/shard_map/ppermute | solution.py:47
  23.4 12.6 %collective-permute-start.11 = (bf16[2,128,640]{2,1,0:T(8,128)(2,1)S(1)}, bf16[2,128,640]{2,1,0:T(8,128)(2,1)S(1)}, u32[]{:S(2)}, u32[]{:S(2)}) collective-permute-start(bf16[2,128,640]{2,1,0:T(8,128)(2,1)S(1)} %pad_maximum_fusion.1.refs_10_), channel_id=1, source_target_pairs={{0,1},{8,9},{16,17},{24,25},{32,33},{40,41},{48,49},{56,57},{64,65... | collective-permute-start | bytes 983048 | tf_op jit(solution)/shard_map/ppermute | solution.py:47
  33.9 3.2 %copy-start.1 = (bf16[192,5120]{1,0:T(8,128)(2,1)S(1)}, bf16[192,5120]{1,0:T(8,128)(2,1)}, u32[]{:S(2)}) copy-start(bf16[192,5120]{1,0:T(8,128)(2,1)} %refs_0_.3) | copy-start | bytes 5898244
  33.9 3.2 %copy-start.2 = (bf16[192,5120]{1,0:T(8,128)(2,1)S(1)}, bf16[192,5120]{1,0:T(8,128)(2,1)}, u32[]{:S(2)}) copy-start(bf16[192,5120]{1,0:T(8,128)(2,1)} %refs_1_.3) | copy-start | bytes 5898244
  33.9 3.2 %copy-start.3 = (bf16[192,5120]{1,0:T(8,128)(2,1)S(1)}, bf16[192,5120]{1,0:T(8,128)(2,1)}, u32[]{:S(2)}) copy-start(bf16[192,5120]{1,0:T(8,128)(2,1)} %refs_2_.3) | copy-start | bytes 5898244
  35.2 1.5 %collective-permute-start.8 = (f32[2,200,128]{2,1,0:T(8,128)S(1)}, f32[2,200,128]{2,1,0:T(8,128)S(1)}, u32[]{:S(2)}, u32[]{:S(2)}) collective-permute-start(f32[2,200,128]{2,1,0:T(8,128)S(1)} %get-tuple-element.41.refs_5_), channel_id=1, source_target_pairs={{0,8},{8,0},{16,24},{24,16},{32,40},{40,32},{48,56},{56,48},{64,72... | collective-permute-start | bytes 614408 | tf_op jit(solution)/shard_map/ppermute | solution.py:47
  35.5 1.5 %collective-permute-start.9 = (f32[2,200,128]{2,1,0:T(8,128)S(1)}, f32[2,200,128]{2,1,0:T(8,128)S(1)}, u32[]{:S(2)}, u32[]{:S(2)}) collective-permute-start(f32[2,200,128]{2,1,0:T(8,128)S(1)} %get-tuple-element.42.refs_6_), channel_id=1, source_target_pairs={{0,8},{8,0},{16,24},{24,16},{32,40},{40,32},{48,56},{56,48},{64,72... | collective-permute-start | bytes 614408 | tf_op jit(solution)/shard_map/ppermute | solution.py:47
  35.8 10.6 %collective-permute-start.12 = (bf16[2,128,640]{2,1,0:T(8,128)(2,1)S(1)}, bf16[2,128,640]{2,1,0:T(8,128)(2,1)S(1)}, u32[]{:S(2)}, u32[]{:S(2)}) collective-permute-start(bf16[2,128,640]{2,1,0:T(8,128)(2,1)S(1)} %pad_maximum_fusion.1.refs_10_), channel_id=1, source_target_pairs={{0,2},{8,10},{16,18},{24,26},{32,34},{40,42},{48,50},{56,58},{64,6... | collective-permute-start | bytes 983048 | tf_op jit(solution)/shard_map/ppermute | solution.py:47
  42.3 12.5 %collective-permute-start.13 = (bf16[4,8,40,128]{3,2,1,0:T(8,128)(2,1)S(1)}, bf16[4,8,40,128]{3,2,1,0:T(8,128)(2,1)S(1)}, u32[]{:S(2)}, u32[]{:S(2)}) collective-permute-start(bf16[4,8,40,128]{3,2,1,0:T(8,128)(2,1)S(1)} %get-tuple-element.49), channel_id=1, source_target_pairs={{0,1},{8,9},{16,17},{24,25},{32,33},{40,41},{48,49},{56,57},{64,65... | collective-permute-start | bytes 983048 | tf_op jit(solution)/shard_map/ppermute | solution.py:47
  42.6 12.2 %collective-permute-start.15 = (bf16[4,8,40,128]{3,2,1,0:T(8,128)(2,1)S(1)}, bf16[4,8,40,128]{3,2,1,0:T(8,128)(2,1)S(1)}, u32[]{:S(2)}, u32[]{:S(2)}) collective-permute-start(bf16[4,8,40,128]{3,2,1,0:T(8,128)(2,1)S(1)} %get-tuple-element.51), channel_id=1, source_target_pairs={{0,3},{8,11},{16,19},{24,27},{32,35},{40,43},{48,51},{56,59},{64,6... | collective-permute-start | bytes 983048 | tf_op jit(solution)/shard_map/ppermute | solution.py:47
  51.6 2.9 %collective-permute-start.19 = (f32[2,192,128]{2,1,0:T(8,128)S(1)}, f32[2,192,128]{2,1,0:T(8,128)S(1)}, u32[]{:S(2)}, u32[]{:S(2)}) collective-permute-start(f32[2,192,128]{2,1,0:T(8,128)S(1)} %get-tuple-element.56.mine0), channel_id=1, source_target_pairs={{0,8},{8,0},{16,24},{24,16},{32,40},{40,32},{48,56},{56,48},{64,72... | collective-permute-start | bytes 589832 | tf_op jit(solution)/shard_map/ppermute | solution.py:47
  53.4 1.4 %collective-permute-start.20 = (f32[2,192,128]{2,1,0:T(8,128)S(1)}, f32[2,192,128]{2,1,0:T(8,128)S(1)}, u32[]{:S(2)}, u32[]{:S(2)}) collective-permute-start(f32[2,192,128]{2,1,0:T(8,128)S(1)} %get-tuple-element.57.mine1), channel_id=1, source_target_pairs={{0,8},{8,0},{16,24},{24,16},{32,40},{40,32},{48,56},{56,48},{64,72... | collective-permute-start | bytes 589832 | tf_op jit(solution)/shard_map/ppermute | solution.py:47
  53.5 10.4 %collective-permute-start.14 = (bf16[4,8,40,128]{3,2,1,0:T(8,128)(2,1)S(1)}, bf16[4,8,40,128]{3,2,1,0:T(8,128)(2,1)S(1)}, u32[]{:S(2)}, u32[]{:S(2)}) collective-permute-start(bf16[4,8,40,128]{3,2,1,0:T(8,128)(2,1)S(1)} %get-tuple-element.50), channel_id=1, source_target_pairs={{0,2},{8,10},{16,18},{24,26},{32,34},{40,42},{48,50},{56,58},{64,6... | collective-permute-start | bytes 983048 | tf_op jit(solution)/shard_map/ppermute | solution.py:47
  56.7 13.2 %collective-permute-start.21 = (bf16[4,8,40,128]{3,2,1,0:T(8,128)(2,1)S(1)}, bf16[4,8,40,128]{3,2,1,0:T(8,128)(2,1)S(1)}, u32[]{:S(2)}, u32[]{:S(2)}) collective-permute-start(bf16[4,8,40,128]{3,2,1,0:T(8,128)(2,1)S(1)} %get-tuple-element.59), channel_id=1, source_target_pairs={{0,12},{8,4},{16,28},{24,20},{32,44},{40,36},{48,60},{56,52},{64,7... | collective-permute-start | bytes 983048 | tf_op jit(solution)/shard_map/ppermute | solution.py:47
  56.8 19.3 %collective-permute-start.22 = (bf16[4,8,40,128]{3,2,1,0:T(8,128)(2,1)S(1)}, bf16[4,8,40,128]{3,2,1,0:T(8,128)(2,1)S(1)}, u32[]{:S(2)}, u32[]{:S(2)}) collective-permute-start(bf16[4,8,40,128]{3,2,1,0:T(8,128)(2,1)S(1)} %get-tuple-element.60), channel_id=1, source_target_pairs={{0,128},{8,136},{16,144},{24,152},{32,160},{40,168},{48,176},{56,1... | collective-permute-start | bytes 983048 | tf_op jit(solution)/shard_map/ppermute | solution.py:47
  61.1 15.4 %collective-permute-start.23 = (bf16[4,8,40,128]{3,2,1,0:T(8,128)(2,1)S(1)}, bf16[4,8,40,128]{3,2,1,0:T(8,128)(2,1)S(1)}, u32[]{:S(2)}, u32[]{:S(2)}) collective-permute-start(bf16[4,8,40,128]{3,2,1,0:T(8,128)(2,1)S(1)} %get-tuple-element.61), channel_id=1, source_target_pairs={{0,140},{8,132},{16,156},{24,148},{32,172},{40,164},{48,188},{56,1... | collective-permute-start | bytes 983048 | tf_op jit(solution)/shard_map/ppermute | solution.py:47
  64.6 15.0 %collective-permute-start.16 = (bf16[8,40,128]{2,1,0:T(8,128)(2,1)S(1)}, bf16[8,40,128]{2,1,0:T(8,128)(2,1)S(1)}, u32[]{:S(2)}, u32[]{:S(2)}) collective-permute-start(bf16[8,40,128]{2,1,0:T(8,128)(2,1)S(1)} %get-tuple-element.53), channel_id=1, source_target_pairs={{0,12},{8,4},{16,28},{24,20},{32,44},{40,36},{48,60},{56,52},{64,7... | collective-permute-start | bytes 245768 | tf_op jit(solution)/shard_map/ppermute | solution.py:47
  65.6 15.2 %collective-permute-start.17 = (bf16[8,40,128]{2,1,0:T(8,128)(2,1)S(1)}, bf16[8,40,128]{2,1,0:T(8,128)(2,1)S(1)}, u32[]{:S(2)}, u32[]{:S(2)}) collective-permute-start(bf16[8,40,128]{2,1,0:T(8,128)(2,1)S(1)} %get-tuple-element.54), channel_id=1, source_target_pairs={{0,128},{8,136},{16,144},{24,152},{32,160},{40,168},{48,176},{56,1... | collective-permute-start | bytes 245768 | tf_op jit(solution)/shard_map/ppermute | solution.py:47
  69.9 10.9 %collective-permute-start.18 = (bf16[8,40,128]{2,1,0:T(8,128)(2,1)S(1)}, bf16[8,40,128]{2,1,0:T(8,128)(2,1)S(1)}, u32[]{:S(2)}, u32[]{:S(2)}) collective-permute-start(bf16[8,40,128]{2,1,0:T(8,128)(2,1)S(1)} %get-tuple-element.55), channel_id=1, source_target_pairs={{0,140},{8,132},{16,156},{24,148},{32,172},{40,164},{48,188},{56,1... | collective-permute-start | bytes 245768 | tf_op jit(solution)/shard_map/ppermute | solution.py:47
  76.6 4.6 %collective-permute-start.24 = (bf16[8,40,128]{2,1,0:T(8,128)(2,1)S(1)}, bf16[8,40,128]{2,1,0:T(8,128)(2,1)S(1)}, u32[]{:S(2)}, u32[]{:S(2)}) collective-permute-start(bf16[8,40,128]{2,1,0:T(8,128)(2,1)S(1)} %get-tuple-element.63), channel_id=1, source_target_pairs={{0,1},{8,9},{16,17},{24,25},{32,33},{40,41},{48,49},{56,57},{64,65... | collective-permute-start | bytes 245768 | tf_op jit(solution)/shard_map/ppermute | solution.py:47
  76.7 7.3 %collective-permute-start.25 = (bf16[8,40,128]{2,1,0:T(8,128)(2,1)S(1)}, bf16[8,40,128]{2,1,0:T(8,128)(2,1)S(1)}, u32[]{:S(2)}, u32[]{:S(2)}) collective-permute-start(bf16[8,40,128]{2,1,0:T(8,128)(2,1)S(1)} %get-tuple-element.64), channel_id=1, source_target_pairs={{0,2},{8,10},{16,18},{24,26},{32,34},{40,42},{48,50},{56,58},{64,6... | collective-permute-start | bytes 245768 | tf_op jit(solution)/shard_map/ppermute | solution.py:47
  79.6 4.4 %collective-permute-start.26 = (bf16[8,40,128]{2,1,0:T(8,128)(2,1)S(1)}, bf16[8,40,128]{2,1,0:T(8,128)(2,1)S(1)}, u32[]{:S(2)}, u32[]{:S(2)}) collective-permute-start(bf16[8,40,128]{2,1,0:T(8,128)(2,1)S(1)} %get-tuple-element.65), channel_id=1, source_target_pairs={{0,3},{8,11},{16,19},{24,27},{32,35},{40,43},{48,51},{56,59},{64,6... | collective-permute-start | bytes 245768 | tf_op jit(solution)/shard_map/ppermute | solution.py:47
  111.2 7.8 %collective-permute-start.27 = (bf16[8,80,128]{2,1,0:T(8,128)(2,1)S(1)}, bf16[8,80,128]{2,1,0:T(8,128)(2,1)S(1)}, u32[]{:S(2)}, u32[]{:S(2)}) collective-permute-start(bf16[8,80,128]{2,1,0:T(8,128)(2,1)S(1)} %all_to_all.11.own), channel_id=1, source_target_pairs={{0,136},{8,4},{16,152},{24,20},{32,168},{40,36},{48,184},{56,52},{... | collective-permute-start | bytes 491528 | tf_op jit(solution)/shard_map/ppermute | solution.py:47
  115.1 6.4 %collective-permute-start.28 = (bf16[8,80,128]{2,1,0:T(8,128)(2,1)S(1)}, bf16[8,80,128]{2,1,0:T(8,128)(2,1)S(1)}, u32[]{:S(2)}, u32[]{:S(2)}) collective-permute-start(bf16[8,80,128]{2,1,0:T(8,128)(2,1)S(1)} %all_to_all.11.own), channel_id=1, source_target_pairs={{0,8},{8,132},{16,24},{24,148},{32,40},{40,164},{48,56},{56,180},{... | collective-permute-start | bytes 491528 | tf_op jit(solution)/shard_map/ppermute | solution.py:47
  119.1 3.4 %collective-permute-start.29 = (bf16[8,80,128]{2,1,0:T(8,128)(2,1)S(1)}, bf16[8,80,128]{2,1,0:T(8,128)(2,1)S(1)}, u32[]{:S(2)}, u32[]{:S(2)}) collective-permute-start(bf16[8,80,128]{2,1,0:T(8,128)(2,1)S(1)} %collective-permute-done.27.first), channel_id=1, source_target_pairs={{0,8},{8,0},{16,24},{24,16},{32,40},{40,32},{48,56},{56,48},{64,72... | collective-permute-start | bytes 491528 | tf_op jit(solution)/shard_map/ppermute | solution.py:47
  121.5 1.4 %collective-permute-start.30 = (bf16[8,80,128]{2,1,0:T(8,128)(2,1)S(1)}, bf16[8,80,128]{2,1,0:T(8,128)(2,1)S(1)}, u32[]{:S(2)}, u32[]{:S(2)}) collective-permute-start(bf16[8,80,128]{2,1,0:T(8,128)(2,1)S(1)} %collective-permute-done.28.second), channel_id=1, source_target_pairs={{0,8},{8,0},{16,24},{24,16},{32,40},{40,32},{48,56},{56,48},{64,72... | collective-permute-start | bytes 491528 | tf_op jit(solution)/shard_map/ppermute | solution.py:47

commit v4 on v3

--- a/solution.py
+++ b/solution.py
@@ -449,12 +449,12 @@
     lows = [*lows, *(swap_cores(part) for part in lows)]
     rows = (place, (q, k, v, g), peer, ups)
     gups = [None] * NY
-    gups[1], gups[3], *dlow, low, weights = attend((1, 3), (), *rows, *lows)
+    gups[1], gups[3], gups[0], *dlow, low, weights = attend((1, 3, 0), (), *rows, *lows)
     gups[1], gups[3] = send_y(gups[1], 1), send_y(gups[3], 3)
-    gups[2], gups[0], *dlow = attend((2, 0), (), *rows, low, weights, *dlow)
+    gups[2], *dlow = attend((2,), (), *rows, low, weights, *dlow)
     gups[2] = send_y(gups[2], 2)
     dlows = [*dlow, *(swap_cores(part) for part in dlow)]
-    gdowns = scatter_x(down_grads(place, nown, peer, dlows, gups[1], gups[3]))
+    gdowns = scatter_x(down_grads(place, nown, peer, dlows))
     ups = scatter_x(sum_y(place, gups))
     downs = scatter_y(sum_x(gdowns))
     eighths = join(ups, downs)

time: 125 us -> 122 us (0.976)
  waiting for transfers between devices: 33 us -> 26.6 us
  starting transfers between devices: 40.3 us -> 44.6 us
    ppermute x31, waiting for transfers between devices: 33 us -> 26.6 us  [send(): return lax.ppermute(value, AXES, permutation(target))]
    ppermute x31, starting transfers between devices: 40.3 us -> 44.6 us  [send(): return lax.ppermute(value, AXES, permutation(target))]
  transfers between devices with their start and end apart: 31 -> 31, of which waited for: 17 -> 16; matrix products, arithmetic and copies ran while one was open for 0% -> 0% of each run, Pallas kernels for 16% -> 16%
where the time goes in v4:
time: 122 us
  starting transfers between devices  44.6 us (37%)
  blocking collectives  26.8 us (22%)
  waiting for transfers between devices  26.6 us (22%)
  Pallas kernels  21.2 us (17%)
  between operations  1.53 us (1%)
    ppermute x31, starting transfers between devices, send(): return lax.ppermute(value, AXES, permutation(target))  44.6 us
    all_to_all x2, blocking collectives, exchange_z(): lax.all_to_all(value, AXES, 0, 0, axis_index_groups=Z_GROUPS, tiled=True)  26.8 us
    ppermute x31, waiting for transfers between devices, send(): return lax.ppermute(value, AXES, permutation(target))  26.6 us
    pallas_call x4, Pallas kernels, call(): pl.pallas_call(kernel, out_shape=outs, in_specs=[SCALARS] + [RESIDENT] *...  13.5 us
    pallas_call x1, Pallas kernels, normalize(): pl.pallas_call(normalize_kernel, out_shape=[jax.ShapeDtypeStruct((CLIP, H...  5.02 us
  transfers between devices with their start and end apart: 31, of which 16 were waited for; matrix products, arithmetic and copies ran while one was open for 0% of the time, Pallas kernels for 16%

profile of v4, /device:TPU:1, one launch (start us, length us, event | category | flops | bytes accessed | tf_op | source)
XLA Modules:
  0.0 122.1 jit_solution(16323077130707566539)
XLA Ops:
  0.7 1.0 dynamic-slice_bitcast_fusion
  1.6 3.3 %collective-permute-start.1 = (bf16[128,640]{1,0:T(8,128)(2,1)S(1)}, bf16[128,640]{1,0:T(8,128)(2,1)S(1)}, u32[]{:S(2)}, u32[]{:S(2)}) collective-permute-start(bf16[128,640]{1,0:T(8,128)(2,1)S(1)} %dynamic-slice_bitcast_fusion), channel_id=1, source_target_pairs={{0,140},{8,0},{16,156},{24,16},{32,172},{40,32},{48,188},{56,48},{... | collective-permute-start | bytes 491528 | tf_op jit(solution)/shard_map/ppermute | solution.py:47
  4.9 1.9 %collective-permute-start = (bf16[128,640]{1,0:T(8,128)(2,1)S(1)}, bf16[128,640]{1,0:T(8,128)(2,1)S(1)}, u32[]{:S(2)}, u32[]{:S(2)}) collective-permute-start(bf16[128,640]{1,0:T(8,128)(2,1)S(1)} %dynamic-slice_bitcast_fusion), channel_id=1, source_target_pairs={{0,0},{8,12},{16,16},{24,28},{32,32},{40,44},{48,48},{56,60},{64,6... | collective-permute-start | bytes 491528 | tf_op jit(solution)/shard_map/ppermute | solution.py:47
  6.8 2.3 %collective-permute-start.2 = (bf16[640,128]{1,0:T(8,128)(2,1)S(1)}, bf16[640,128]{1,0:T(8,128)(2,1)S(1)}, u32[]{:S(2)}, u32[]{:S(2)}) collective-permute-start(bf16[640,128]{1,0:T(8,128)(2,1)S(1)} %fusion), channel_id=1, source_target_pairs={{0,3},{8,11},{16,19},{24,27},{32,35},{40,43},{48,51},{56,59},{64,6... | collective-permute-start | bytes 491528 | tf_op jit(solution)/shard_map/ppermute | solution.py:47
  9.1 0.3 collective-permute-start.3
  9.5 0.7 collective-permute-start.4
  10.2 5.0 %normalize.1 = (bf16[192,2560]{1,0:T(8,128)(2,1)S(1)}, bf16[5,192,2560]{2,1,0:T(8,128)(2,1)S(1)}) custom-call(s32[4]{0:T(128)S(1)} %pad_add_fusion.place, bf16[192,5120]{1,0:T(8,128)(2,1)} %states.1, bf16[192,5120]{1,0:T(8,128)(2,1)} %refs_0_.3, bf16[192,5120]{1,0:T(8,128)(2,1)} %refs_1_.3, bf16[192,5120]{1,0:T(8,128)(2,1)} %refs_2_.3, bf16[192,5120]{1,0:T(8,128)(2,1)} %refs_3_.3), custom_call_target="tpu_custom_call" | custom-call | flops 1000 | bytes 1000 | tf_op jit(solution)/shard_map/normalize/pallas_call | solution.py:149
  15.3 1.0 collective-permute-done.2
  16.5 3.8 %collective-permute-done.4 = bf16[640,128]{1,0:T(8,128)(2,1)S(1)} collective-permute-done((bf16[640,128]{1,0:T(8,128)(2,1)S(1)}, bf16[640,128]{1,0:T(8,128)(2,1)S(1)}, u32[]{:S(2)}, u32[]{:S(2)}) %collective-permute-start.4) | collective-permute-done | bytes 163872 | tf_op jit(solution)/shard_map/ppermute | solution.py:47
  20.3 0.5 collective-permute-start.5
  20.9 2.1 %collective-permute-start.6 = (bf16[4,640,128]{2,1,0:T(8,128)(2,1)S(1)}, bf16[4,640,128]{2,1,0:T(8,128)(2,1)S(1)}, u32[]{:S(2)}, u32[]{:S(2)}) collective-permute-start(bf16[4,640,128]{2,1,0:T(8,128)(2,1)S(1)} %pad_maximum_fusion), channel_id=1, source_target_pairs={{0,0},{8,12},{16,16},{24,28},{32,32},{40,44},{48,48},{56,60},{64,6... | collective-permute-start | bytes 1966088 | tf_op jit(solution)/shard_map/ppermute | solution.py:47
  23.0 0.4 collective-permute-start.10
  23.4 1.1 collective-permute-start.11
  25.2 8.7 %collective-permute-done.6.own = bf16[4,640,128]{2,1,0:T(8,128)(2,1)S(1)} collective-permute-done((bf16[4,640,128]{2,1,0:T(8,128)(2,1)S(1)}, bf16[4,640,128]{2,1,0:T(8,128)(2,1)S(1)}, u32[]{:S(2)}, u32[]{:S(2)}) %collective-permute-start.6) | collective-permute-done | bytes 655392 | tf_op jit(solution)/shard_map/ppermute | solution.py:47
  33.9 1.3 %lower.1 = (f32[2,200,128]{2,1,0:T(8,128)S(1)}, f32[2,200,128]{2,1,0:T(8,128)S(1)}) custom-call(s32[4]{0:T(128)S(1)} %pad_add_fusion.place, bf16[192,2560]{1,0:T(8,128)(2,1)S(1)} %get-tuple-element.37.nown, bf16[5,192,2560]{2,1,0:T(8,128)(2,1)S(1)} %collective-permute-done.5.npeer.refs_4_.peer, bf16[4,640,128]{2,1,0:T(8,128)(2,1)S(1)} %collective-permute-done.6.own, ...), custom_call_target="tpu_custom_call" | custom-call | flops 1000 | bytes 1000 | tf_op jit(solution)/shard_map/lower/pallas_call | solution.py:98
  35.2 0.3 collective-permute-start.8
  35.5 0.3 collective-permute-start.9
  36.0 0.8 collective-permute-done.8.refs_7_
  36.8 0.3 collective-permute-done.9.refs_8_
  37.1 7.4 %attend.2 = (bf16[4,8,40,128]{3,2,1,0:T(8,128)(2,1)S(1)}, bf16[4,8,40,128]{3,2,1,0:T(8,128)(2,1)S(1)}, bf16[4,8,40,128]{3,2,1,0:T(8,128)(2,1)S(1)}, f32[2,192,12...) custom-call(s32[4]{0:T(128)S(1)} %pad_add_fusion.place, ...), custom_call_target="tpu_custom_call" | custom-call | flops 1000 | bytes 1000 | tf_op jit(solution)/shard_map/attend/pallas_call | solution.py:98
  44.6 1.8 %collective-permute-done.13.refs_9_ = bf16[2,128,640]{2,1,0:T(8,128)(2,1)S(1)} collective-permute-done((bf16[2,128,640]{2,1,0:T(8,128)(2,1)S(1)}, bf16[2,128,640]{2,1,0:T(8,128)(2,1)S(1)}, u32[]{:S(2)}, u32[]{:S(2)}) %collective-permute-start.13) | collective-permute-done | bytes 327712 | tf_op jit(solution)/shard_map/ppermute | solution.py:47
  46.4 3.0 %attend.3 = (bf16[4,8,40,128]{3,2,1,0:T(8,128)(2,1)S(1)}, f32[2,192,128]{2,1,0:T(8,128)S(1)}, f32[2,192,128]{2,1,0:T(8,128)S(1)}) custom-call(s32[4]{0:T(128)S(1)} %pad_add_fusion.place, bf16[192,5120]{1,0:T(8,128)(2,1)S(1)} %copy-done.1, bf16[192,5120]{1,0:T(8,128)(2,1)S(1)} %copy-done.2, bf16[192,5120]{1,0:T(8,128)(2,1)S(1)} %copy-done.3, ...), custom_call_target="tpu_custom_call" | custom-call | flops 1000 | bytes 1000 | tf_op jit(solution)/shard_map/attend/pallas_call | solution.py:98
  49.4 1.2 collective-permute-start.19
  50.6 0.2 collective-permute-start.14
  50.9 1.4 %collective-permute-start.15 = (bf16[4,8,40,128]{3,2,1,0:T(8,128)(2,1)S(1)}, bf16[4,8,40,128]{3,2,1,0:T(8,128)(2,1)S(1)}, u32[]{:S(2)}, u32[]{:S(2)}) collective-permute-start(bf16[4,8,40,128]{3,2,1,0:T(8,128)(2,1)S(1)} %get-tuple-element.51), channel_id=1, source_target_pairs={{0,3},{8,11},{16,19},{24,27},{32,35},{40,43},{48,51},{56,59},{64,6... | collective-permute-start | bytes 983048 | tf_op jit(solution)/shard_map/ppermute | solution.py:47
  52.3 1.9 %down_grads.1 = (bf16[4,8,40,128]{3,2,1,0:T(8,128)(2,1)S(1)}, bf16[4,8,40,128]{3,2,1,0:T(8,128)(2,1)S(1)}, bf16[4,8,40,128]{3,2,1,0:T(8,128)(2,1)S(1)}, bf16[4,8,40,128]{3,2,1,0:T(8,128)(2,1)S(1)}) custom-call(s32[4]{0:T(128)S(1)} %pad_add_fusion.place, bf16[192,2560]{1,0:T(8,128)(2,1)S(1)} %get-tuple-element.37.nown, ...), custom_call_target="tpu_custom_call" | custom-call | flops 1000 | bytes 1000 | tf_op jit(solution)/shard_map/down_grads/pallas_call | solution.py:98
  54.1 0.8 collective-permute-start.21
  55.0 4.3 %collective-permute-start.22 = (bf16[4,8,40,128]{3,2,1,0:T(8,128)(2,1)S(1)}, bf16[4,8,40,128]{3,2,1,0:T(8,128)(2,1)S(1)}, u32[]{:S(2)}, u32[]{:S(2)}) collective-permute-start(bf16[4,8,40,128]{3,2,1,0:T(8,128)(2,1)S(1)} %get-tuple-element.60), channel_id=1, source_target_pairs={{0,128},{8,136},{16,144},{24,152},{32,160},{40,168},{48,176},{56,1... | collective-permute-start | bytes 983048 | tf_op jit(solution)/shard_map/ppermute | solution.py:47
  59.3 6.6 %collective-permute-start.23 = (bf16[4,8,40,128]{3,2,1,0:T(8,128)(2,1)S(1)}, bf16[4,8,40,128]{3,2,1,0:T(8,128)(2,1)S(1)}, u32[]{:S(2)}, u32[]{:S(2)}) collective-permute-start(bf16[4,8,40,128]{3,2,1,0:T(8,128)(2,1)S(1)} %get-tuple-element.61), channel_id=1, source_target_pairs={{0,140},{8,132},{16,156},{24,148},{32,172},{40,164},{48,188},{56,1... | collective-permute-start | bytes 983048 | tf_op jit(solution)/shard_map/ppermute | solution.py:47
  65.8 0.2 collective-permute-done.15.refs_3_
  66.0 0.7 sum_y.1
  66.8 1.2 collective-permute-start.16
  67.9 4.3 %collective-permute-start.17 = (bf16[8,40,128]{2,1,0:T(8,128)(2,1)S(1)}, bf16[8,40,128]{2,1,0:T(8,128)(2,1)S(1)}, u32[]{:S(2)}, u32[]{:S(2)}) collective-permute-start(bf16[8,40,128]{2,1,0:T(8,128)(2,1)S(1)} %get-tuple-element.54), channel_id=1, source_target_pairs={{0,128},{8,136},{16,144},{24,152},{32,160},{40,168},{48,176},{56,1... | collective-permute-start | bytes 245768 | tf_op jit(solution)/shard_map/ppermute | solution.py:47
  72.2 2.1 %collective-permute-done.22.refs_2_ = bf16[4,8,40,128]{3,2,1,0:T(8,128)(2,1)S(1)} collective-permute-done((bf16[4,8,40,128]{3,2,1,0:T(8,128)(2,1)S(1)}, bf16[4,8,40,128]{3,2,1,0:T(8,128)(2,1)S(1)}, u32[]{:S(2)}, u32[]{:S(2)}) %collective-permute-start.22) | collective-permute-done | bytes 327712 | tf_op jit(solution)/shard_map/ppermute | solution.py:47
  74.3 0.3 collective-permute-done.23.refs_3_
  74.9 2.4 %collective-permute-start.25 = (bf16[8,40,128]{2,1,0:T(8,128)(2,1)S(1)}, bf16[8,40,128]{2,1,0:T(8,128)(2,1)S(1)}, u32[]{:S(2)}, u32[]{:S(2)}) collective-permute-start(bf16[8,40,128]{2,1,0:T(8,128)(2,1)S(1)} %get-tuple-element.64), channel_id=1, source_target_pairs={{0,2},{8,10},{16,18},{24,26},{32,34},{40,42},{48,50},{56,58},{64,6... | collective-permute-start | bytes 245768 | tf_op jit(solution)/shard_map/ppermute | solution.py:47
  77.2 0.9 collective-permute-start.26
  78.1 2.9 %collective-permute-done.24.refs_5_ = bf16[8,40,128]{2,1,0:T(8,128)(2,1)S(1)} collective-permute-done((bf16[8,40,128]{2,1,0:T(8,128)(2,1)S(1)}, bf16[8,40,128]{2,1,0:T(8,128)(2,1)S(1)}, u32[]{:S(2)}, u32[]{:S(2)}) %collective-permute-start.24) | collective-permute-done | bytes 81952 | tf_op jit(solution)/shard_map/ppermute | solution.py:47
  81.1 1.2 collective-permute-done.26.refs_7_
  82.4 16.1 %all_to_all.10 = bf16[8,80,128]{2,1,0:T(8,128)(2,1)S(1)} all-to-all(bf16[8,80,128]{2,1,0:T(8,128)(2,1)S(1)} %join.1), channel_id=1, replica_groups={{0,16,32,48,64,80,96,112},{8,24,40,56,72,88,104,120},{1,17,33,49,65,81,..., dimensions={0} | all-to-all | bytes 327680 | tf_op jit(solution)/shard_map/all_to_all | solution.py:80
  98.5 10.8 %all_to_all.11.own = bf16[8,80,128]{2,1,0:T(8,128)(2,1)S(1)} all-to-all(bf16[8,80,128]{2,1,0:T(8,128)(2,1)S(1)} %broadcast_in_dim.7), channel_id=1, replica_groups={{0,16,32,48,64,80,96,112},{8,24,40,56,72,88,104,120},{1,17,33,49,65,81,..., dimensions={0} | all-to-all | bytes 327680 | tf_op jit(solution)/shard_map/all_to_all | solution.py:80
  109.3 3.8 %collective-permute-start.27 = (bf16[8,80,128]{2,1,0:T(8,128)(2,1)S(1)}, bf16[8,80,128]{2,1,0:T(8,128)(2,1)S(1)}, u32[]{:S(2)}, u32[]{:S(2)}) collective-permute-start(bf16[8,80,128]{2,1,0:T(8,128)(2,1)S(1)} %all_to_all.11.own), channel_id=1, source_target_pairs={{0,136},{8,4},{16,152},{24,20},{32,168},{40,36},{48,184},{56,52},{... | collective-permute-start | bytes 491528 | tf_op jit(solution)/shard_map/ppermute | solution.py:47
  113.1 2.1 %collective-permute-start.28 = (bf16[8,80,128]{2,1,0:T(8,128)(2,1)S(1)}, bf16[8,80,128]{2,1,0:T(8,128)(2,1)S(1)}, u32[]{:S(2)}, u32[]{:S(2)}) collective-permute-start(bf16[8,80,128]{2,1,0:T(8,128)(2,1)S(1)} %all_to_all.11.own), channel_id=1, source_target_pairs={{0,8},{8,132},{16,24},{24,148},{32,40},{40,164},{48,56},{56,180},{... | collective-permute-start | bytes 491528 | tf_op jit(solution)/shard_map/ppermute | solution.py:47
  115.2 1.9 %collective-permute-done.27.first = bf16[8,80,128]{2,1,0:T(8,128)(2,1)S(1)} collective-permute-done((bf16[8,80,128]{2,1,0:T(8,128)(2,1)S(1)}, bf16[8,80,128]{2,1,0:T(8,128)(2,1)S(1)}, u32[]{:S(2)}, u32[]{:S(2)}) %collective-permute-start.27) | collective-permute-done | bytes 163872 | tf_op jit(solution)/shard_map/ppermute | solution.py:47
  117.1 1.9 %collective-permute-start.29 = (bf16[8,80,128]{2,1,0:T(8,128)(2,1)S(1)}, bf16[8,80,128]{2,1,0:T(8,128)(2,1)S(1)}, u32[]{:S(2)}, u32[]{:S(2)}) collective-permute-start(bf16[8,80,128]{2,1,0:T(8,128)(2,1)S(1)} %collective-permute-done.27.first), channel_id=1, source_target_pairs={{0,8},{8,0},{16,24},{24,16},{32,40},{40,32},{48,56},{56,48},{64,72... | collective-permute-start | bytes 491528 | tf_op jit(solution)/shard_map/ppermute | solution.py:47
  119.0 1.0 collective-permute-done.29.first_peer
  120.0 0.4 collective-permute-done.30.second_peer
  120.4 1.7 %finish.1 = (f32[2,640,128]{2,1,0:T(8,128)}, f32[32,8,640]{2,1,0:T(8,128)}) custom-call(s32[4]{0:T(128)S(1)} %pad_add_fusion.place, bf16[8,80,128]{2,1,0:T(8,128)(2,1)S(1)} %all_to_all.11.own, bf16[8,80,128]{2,1,0:T(8,128)(2,1)S(1)} %collective-permute-done.27.first, bf16[8,80,128]{2,1,0:T(8,128)(2,1)S(1)} %collective-permute-done.28.second, ...), custom_call_target="tpu_custom_call" | custom-call | tf_op jit(solution)/shard_map/finish/pallas_call | solution.py:409
  (44 shorter events, 1.4 us)
Async XLA Ops:
  0.6 6.2 %copy-start = (bf16[2,640,128]{2,1,0:T(8,128)(2,1)S(1)}, bf16[2,640,128]{2,1,0:T(8,128)(2,1)}, u32[]{:S(2)}) copy-start(bf16[2,640,128]{2,1,0:T(8,128)(2,1)} %param.14) | copy-start | bytes 983044
  1.6 13.6 %collective-permute-start.1 = (bf16[128,640]{1,0:T(8,128)(2,1)S(1)}, bf16[128,640]{1,0:T(8,128)(2,1)S(1)}, u32[]{:S(2)}, u32[]{:S(2)}) collective-permute-start(bf16[128,640]{1,0:T(8,128)(2,1)S(1)} %dynamic-slice_bitcast_fusion), channel_id=1, source_target_pairs={{0,140},{8,0},{16,156},{24,16},{32,172},{40,32},{48,188},{56,48},{... | collective-permute-start | bytes 491528 | tf_op jit(solution)/shard_map/ppermute | solution.py:47
  4.9 10.4 %collective-permute-start = (bf16[128,640]{1,0:T(8,128)(2,1)S(1)}, bf16[128,640]{1,0:T(8,128)(2,1)S(1)}, u32[]{:S(2)}, u32[]{:S(2)}) collective-permute-start(bf16[128,640]{1,0:T(8,128)(2,1)S(1)} %dynamic-slice_bitcast_fusion), channel_id=1, source_target_pairs={{0,0},{8,12},{16,16},{24,28},{32,32},{40,44},{48,48},{56,60},{64,6... | collective-permute-start | bytes 491528 | tf_op jit(solution)/shard_map/ppermute | solution.py:47
  6.8 9.4 %collective-permute-start.2 = (bf16[640,128]{1,0:T(8,128)(2,1)S(1)}, bf16[640,128]{1,0:T(8,128)(2,1)S(1)}, u32[]{:S(2)}, u32[]{:S(2)}) collective-permute-start(bf16[640,128]{1,0:T(8,128)(2,1)S(1)} %fusion), channel_id=1, source_target_pairs={{0,3},{8,11},{16,19},{24,27},{32,35},{40,43},{48,51},{56,59},{64,6... | collective-permute-start | bytes 491528 | tf_op jit(solution)/shard_map/ppermute | solution.py:47
  9.1 7.3 %collective-permute-start.3 = (bf16[640,128]{1,0:T(8,128)(2,1)S(1)}, bf16[640,128]{1,0:T(8,128)(2,1)S(1)}, u32[]{:S(2)}, u32[]{:S(2)}) collective-permute-start(bf16[640,128]{1,0:T(8,128)(2,1)S(1)} %fusion), channel_id=1, source_target_pairs={{0,2},{8,10},{16,18},{24,26},{32,34},{40,42},{48,50},{56,58},{64,6... | collective-permute-start | bytes 491528 | tf_op jit(solution)/shard_map/ppermute | solution.py:47
  9.5 10.8 %collective-permute-start.4 = (bf16[640,128]{1,0:T(8,128)(2,1)S(1)}, bf16[640,128]{1,0:T(8,128)(2,1)S(1)}, u32[]{:S(2)}, u32[]{:S(2)}) collective-permute-start(bf16[640,128]{1,0:T(8,128)(2,1)S(1)} %fusion), channel_id=1, source_target_pairs={{0,1},{8,9},{16,17},{24,25},{32,33},{40,41},{48,49},{56,57},{64,65... | collective-permute-start | bytes 491528 | tf_op jit(solution)/shard_map/ppermute | solution.py:47
  20.3 13.6 %collective-permute-start.5 = (bf16[5,192,2560]{2,1,0:T(8,128)(2,1)S(1)}, bf16[5,192,2560]{2,1,0:T(8,128)(2,1)S(1)}, u32[]{:S(2)}, u32[]{:S(2)}) collective-permute-start(bf16[5,192,2560]{2,1,0:T(8,128)(2,1)S(1)} %get-tuple-element.36), channel_id=1, source_target_pairs={{0,8},{8,0},{16,24},{24,16},{32,40},{40,32},{48,56},{56,48},{64,72... | collective-permute-start | bytes 14745608 | tf_op jit(solution)/shard_map/ppermute | solution.py:47
  20.8 16.3 %copy-start.4 = (bf16[192,5120]{1,0:T(8,128)(2,1)S(1)}, bf16[192,5120]{1,0:T(8,128)(2,1)}, u32[]{:S(2)}) copy-start(bf16[192,5120]{1,0:T(8,128)(2,1)} %refs_3_.3) | copy-start | bytes 5898244
  20.9 13.0 %collective-permute-start.6 = (bf16[4,640,128]{2,1,0:T(8,128)(2,1)S(1)}, bf16[4,640,128]{2,1,0:T(8,128)(2,1)S(1)}, u32[]{:S(2)}, u32[]{:S(2)}) collective-permute-start(bf16[4,640,128]{2,1,0:T(8,128)(2,1)S(1)} %pad_maximum_fusion), channel_id=1, source_target_pairs={{0,0},{8,12},{16,16},{24,28},{32,32},{40,44},{48,48},{56,60},{64,6... | collective-permute-start | bytes 1966088 | tf_op jit(solution)/shard_map/ppermute | solution.py:47
  22.9 10.9 %collective-permute-start.7 = (bf16[4,640,128]{2,1,0:T(8,128)(2,1)S(1)}, bf16[4,640,128]{2,1,0:T(8,128)(2,1)S(1)}, u32[]{:S(2)}, u32[]{:S(2)}) collective-permute-start(bf16[4,640,128]{2,1,0:T(8,128)(2,1)S(1)} %pad_maximum_fusion), channel_id=1, source_target_pairs={{0,140},{8,0},{16,156},{24,16},{32,172},{40,32},{48,188},{56,48},{... | collective-permute-start | bytes 1966088 | tf_op jit(solution)/shard_map/ppermute | solution.py:47
  23.0 13.0 %collective-permute-start.10 = (bf16[2,128,640]{2,1,0:T(8,128)(2,1)S(1)}, bf16[2,128,640]{2,1,0:T(8,128)(2,1)S(1)}, u32[]{:S(2)}, u32[]{:S(2)}) collective-permute-start(bf16[2,128,640]{2,1,0:T(8,128)(2,1)S(1)} %pad_maximum_fusion.1.refs_11_), channel_id=1, source_target_pairs={{0,3},{8,11},{16,19},{24,27},{32,35},{40,43},{48,51},{56,59},{64,6... | collective-permute-start | bytes 983048 | tf_op jit(solution)/shard_map/ppermute | solution.py:47
  23.4 12.6 %collective-permute-start.11 = (bf16[2,128,640]{2,1,0:T(8,128)(2,1)S(1)}, bf16[2,128,640]{2,1,0:T(8,128)(2,1)S(1)}, u32[]{:S(2)}, u32[]{:S(2)}) collective-permute-start(bf16[2,128,640]{2,1,0:T(8,128)(2,1)S(1)} %pad_maximum_fusion.1.refs_11_), channel_id=1, source_target_pairs={{0,1},{8,9},{16,17},{24,25},{32,33},{40,41},{48,49},{56,57},{64,65... | collective-permute-start | bytes 983048 | tf_op jit(solution)/shard_map/ppermute | solution.py:47
  33.9 3.2 %copy-start.1 = (bf16[192,5120]{1,0:T(8,128)(2,1)S(1)}, bf16[192,5120]{1,0:T(8,128)(2,1)}, u32[]{:S(2)}) copy-start(bf16[192,5120]{1,0:T(8,128)(2,1)} %refs_0_.3) | copy-start | bytes 5898244
  33.9 3.2 %copy-start.2 = (bf16[192,5120]{1,0:T(8,128)(2,1)S(1)}, bf16[192,5120]{1,0:T(8,128)(2,1)}, u32[]{:S(2)}) copy-start(bf16[192,5120]{1,0:T(8,128)(2,1)} %refs_1_.3) | copy-start | bytes 5898244
  33.9 3.2 %copy-start.3 = (bf16[192,5120]{1,0:T(8,128)(2,1)S(1)}, bf16[192,5120]{1,0:T(8,128)(2,1)}, u32[]{:S(2)}) copy-start(bf16[192,5120]{1,0:T(8,128)(2,1)} %refs_2_.3) | copy-start | bytes 5898244
  35.2 1.5 %collective-permute-start.8 = (f32[2,200,128]{2,1,0:T(8,128)S(1)}, f32[2,200,128]{2,1,0:T(8,128)S(1)}, u32[]{:S(2)}, u32[]{:S(2)}) collective-permute-start(f32[2,200,128]{2,1,0:T(8,128)S(1)} %get-tuple-element.41.refs_5_), channel_id=1, source_target_pairs={{0,8},{8,0},{16,24},{24,16},{32,40},{40,32},{48,56},{56,48},{64,72... | collective-permute-start | bytes 614408 | tf_op jit(solution)/shard_map/ppermute | solution.py:47
  35.5 1.5 %collective-permute-start.9 = (f32[2,200,128]{2,1,0:T(8,128)S(1)}, f32[2,200,128]{2,1,0:T(8,128)S(1)}, u32[]{:S(2)}, u32[]{:S(2)}) collective-permute-start(f32[2,200,128]{2,1,0:T(8,128)S(1)} %get-tuple-element.42.refs_6_), channel_id=1, source_target_pairs={{0,8},{8,0},{16,24},{24,16},{32,40},{40,32},{48,56},{56,48},{64,72... | collective-permute-start | bytes 614408 | tf_op jit(solution)/shard_map/ppermute | solution.py:47
  35.8 10.6 %collective-permute-start.13 = (bf16[2,128,640]{2,1,0:T(8,128)(2,1)S(1)}, bf16[2,128,640]{2,1,0:T(8,128)(2,1)S(1)}, u32[]{:S(2)}, u32[]{:S(2)}) collective-permute-start(bf16[2,128,640]{2,1,0:T(8,128)(2,1)S(1)} %pad_maximum_fusion.1.refs_11_), channel_id=1, source_target_pairs={{0,2},{8,10},{16,18},{24,26},{32,34},{40,42},{48,50},{56,58},{64,6... | collective-permute-start | bytes 983048 | tf_op jit(solution)/shard_map/ppermute | solution.py:47
  44.5 14.8 %collective-permute-start.12 = (bf16[4,8,40,128]{3,2,1,0:T(8,128)(2,1)S(1)}, bf16[4,8,40,128]{3,2,1,0:T(8,128)(2,1)S(1)}, u32[]{:S(2)}, u32[]{:S(2)}) collective-permute-start(bf16[4,8,40,128]{3,2,1,0:T(8,128)(2,1)S(1)} %get-tuple-element.45), channel_id=1, source_target_pairs={{0,1},{8,9},{16,17},{24,25},{32,33},{40,41},{48,49},{56,57},{64,65... | collective-permute-start | bytes 983048 | tf_op jit(solution)/shard_map/ppermute | solution.py:47
  49.4 2.9 %collective-permute-start.19 = (f32[2,192,128]{2,1,0:T(8,128)S(1)}, f32[2,192,128]{2,1,0:T(8,128)S(1)}, u32[]{:S(2)}, u32[]{:S(2)}) collective-permute-start(f32[2,192,128]{2,1,0:T(8,128)S(1)} %get-tuple-element.56.mine0), channel_id=1, source_target_pairs={{0,8},{8,0},{16,24},{24,16},{32,40},{40,32},{48,56},{56,48},{64,72... | collective-permute-start | bytes 589832 | tf_op jit(solution)/shard_map/ppermute | solution.py:47
  50.5 1.8 %collective-permute-start.20 = (f32[2,192,128]{2,1,0:T(8,128)S(1)}, f32[2,192,128]{2,1,0:T(8,128)S(1)}, u32[]{:S(2)}, u32[]{:S(2)}) collective-permute-start(f32[2,192,128]{2,1,0:T(8,128)S(1)} %get-tuple-element.57.mine1), channel_id=1, source_target_pairs={{0,8},{8,0},{16,24},{24,16},{32,40},{40,32},{48,56},{56,48},{64,72... | collective-permute-start | bytes 589832 | tf_op jit(solution)/shard_map/ppermute | solution.py:47
  50.6 15.2 %collective-permute-start.14 = (bf16[4,8,40,128]{3,2,1,0:T(8,128)(2,1)S(1)}, bf16[4,8,40,128]{3,2,1,0:T(8,128)(2,1)S(1)}, u32[]{:S(2)}, u32[]{:S(2)}) collective-permute-start(bf16[4,8,40,128]{3,2,1,0:T(8,128)(2,1)S(1)} %get-tuple-element.50), channel_id=1, source_target_pairs={{0,2},{8,10},{16,18},{24,26},{32,34},{40,42},{48,50},{56,58},{64,6... | collective-permute-start | bytes 983048 | tf_op jit(solution)/shard_map/ppermute | solution.py:47
  50.9 15.2 %collective-permute-start.15 = (bf16[4,8,40,128]{3,2,1,0:T(8,128)(2,1)S(1)}, bf16[4,8,40,128]{3,2,1,0:T(8,128)(2,1)S(1)}, u32[]{:S(2)}, u32[]{:S(2)}) collective-permute-start(bf16[4,8,40,128]{3,2,1,0:T(8,128)(2,1)S(1)} %get-tuple-element.51), channel_id=1, source_target_pairs={{0,3},{8,11},{16,19},{24,27},{32,35},{40,43},{48,51},{56,59},{64,6... | collective-permute-start | bytes 983048 | tf_op jit(solution)/shard_map/ppermute | solution.py:47
  54.1 18.1 %collective-permute-start.21 = (bf16[4,8,40,128]{3,2,1,0:T(8,128)(2,1)S(1)}, bf16[4,8,40,128]{3,2,1,0:T(8,128)(2,1)S(1)}, u32[]{:S(2)}, u32[]{:S(2)}) collective-permute-start(bf16[4,8,40,128]{3,2,1,0:T(8,128)(2,1)S(1)} %get-tuple-element.59), channel_id=1, source_target_pairs={{0,12},{8,4},{16,28},{24,20},{32,44},{40,36},{48,60},{56,52},{64,7... | collective-permute-start | bytes 983048 | tf_op jit(solution)/shard_map/ppermute | solution.py:47
  55.0 19.3 %collective-permute-start.22 = (bf16[4,8,40,128]{3,2,1,0:T(8,128)(2,1)S(1)}, bf16[4,8,40,128]{3,2,1,0:T(8,128)(2,1)S(1)}, u32[]{:S(2)}, u32[]{:S(2)}) collective-permute-start(bf16[4,8,40,128]{3,2,1,0:T(8,128)(2,1)S(1)} %get-tuple-element.60), channel_id=1, source_target_pairs={{0,128},{8,136},{16,144},{24,152},{32,160},{40,168},{48,176},{56,1... | collective-permute-start | bytes 983048 | tf_op jit(solution)/shard_map/ppermute | solution.py:47
  59.3 15.4 %collective-permute-start.23 = (bf16[4,8,40,128]{3,2,1,0:T(8,128)(2,1)S(1)}, bf16[4,8,40,128]{3,2,1,0:T(8,128)(2,1)S(1)}, u32[]{:S(2)}, u32[]{:S(2)}) collective-permute-start(bf16[4,8,40,128]{3,2,1,0:T(8,128)(2,1)S(1)} %get-tuple-element.61), channel_id=1, source_target_pairs={{0,140},{8,132},{16,156},{24,148},{32,172},{40,164},{48,188},{56,1... | collective-permute-start | bytes 983048 | tf_op jit(solution)/shard_map/ppermute | solution.py:47
  66.8 10.5 %collective-permute-start.16 = (bf16[8,40,128]{2,1,0:T(8,128)(2,1)S(1)}, bf16[8,40,128]{2,1,0:T(8,128)(2,1)S(1)}, u32[]{:S(2)}, u32[]{:S(2)}) collective-permute-start(bf16[8,40,128]{2,1,0:T(8,128)(2,1)S(1)} %get-tuple-element.53), channel_id=1, source_target_pairs={{0,12},{8,4},{16,28},{24,20},{32,44},{40,36},{48,60},{56,52},{64,7... | collective-permute-start | bytes 245768 | tf_op jit(solution)/shard_map/ppermute | solution.py:47
  67.9 10.2 %collective-permute-start.17 = (bf16[8,40,128]{2,1,0:T(8,128)(2,1)S(1)}, bf16[8,40,128]{2,1,0:T(8,128)(2,1)S(1)}, u32[]{:S(2)}, u32[]{:S(2)}) collective-permute-start(bf16[8,40,128]{2,1,0:T(8,128)(2,1)S(1)} %get-tuple-element.54), channel_id=1, source_target_pairs={{0,128},{8,136},{16,144},{24,152},{32,160},{40,168},{48,176},{56,1... | collective-permute-start | bytes 245768 | tf_op jit(solution)/shard_map/ppermute | solution.py:47
  72.2 5.9 %collective-permute-start.18 = (bf16[8,40,128]{2,1,0:T(8,128)(2,1)S(1)}, bf16[8,40,128]{2,1,0:T(8,128)(2,1)S(1)}, u32[]{:S(2)}, u32[]{:S(2)}) collective-permute-start(bf16[8,40,128]{2,1,0:T(8,128)(2,1)S(1)} %get-tuple-element.55), channel_id=1, source_target_pairs={{0,140},{8,132},{16,156},{24,148},{32,172},{40,164},{48,188},{56,1... | collective-permute-start | bytes 245768 | tf_op jit(solution)/shard_map/ppermute | solution.py:47
  74.8 6.2 %collective-permute-start.24 = (bf16[8,40,128]{2,1,0:T(8,128)(2,1)S(1)}, bf16[8,40,128]{2,1,0:T(8,128)(2,1)S(1)}, u32[]{:S(2)}, u32[]{:S(2)}) collective-permute-start(bf16[8,40,128]{2,1,0:T(8,128)(2,1)S(1)} %get-tuple-element.63), channel_id=1, source_target_pairs={{0,1},{8,9},{16,17},{24,25},{32,33},{40,41},{48,49},{56,57},{64,65... | collective-permute-start | bytes 245768 | tf_op jit(solution)/shard_map/ppermute | solution.py:47
  74.9 6.3 %collective-permute-start.25 = (bf16[8,40,128]{2,1,0:T(8,128)(2,1)S(1)}, bf16[8,40,128]{2,1,0:T(8,128)(2,1)S(1)}, u32[]{:S(2)}, u32[]{:S(2)}) collective-permute-start(bf16[8,40,128]{2,1,0:T(8,128)(2,1)S(1)} %get-tuple-element.64), channel_id=1, source_target_pairs={{0,2},{8,10},{16,18},{24,26},{32,34},{40,42},{48,50},{56,58},{64,6... | collective-permute-start | bytes 245768 | tf_op jit(solution)/shard_map/ppermute | solution.py:47
  77.2 5.1 %collective-permute-start.26 = (bf16[8,40,128]{2,1,0:T(8,128)(2,1)S(1)}, bf16[8,40,128]{2,1,0:T(8,128)(2,1)S(1)}, u32[]{:S(2)}, u32[]{:S(2)}) collective-permute-start(bf16[8,40,128]{2,1,0:T(8,128)(2,1)S(1)} %get-tuple-element.65), channel_id=1, source_target_pairs={{0,3},{8,11},{16,19},{24,27},{32,35},{40,43},{48,51},{56,59},{64,6... | collective-permute-start | bytes 245768 | tf_op jit(solution)/shard_map/ppermute | solution.py:47
  109.3 7.8 %collective-permute-start.27 = (bf16[8,80,128]{2,1,0:T(8,128)(2,1)S(1)}, bf16[8,80,128]{2,1,0:T(8,128)(2,1)S(1)}, u32[]{:S(2)}, u32[]{:S(2)}) collective-permute-start(bf16[8,80,128]{2,1,0:T(8,128)(2,1)S(1)} %all_to_all.11.own), channel_id=1, source_target_pairs={{0,136},{8,4},{16,152},{24,20},{32,168},{40,36},{48,184},{56,52},{... | collective-permute-start | bytes 491528 | tf_op jit(solution)/shard_map/ppermute | solution.py:47
  113.1 5.9 %collective-permute-start.28 = (bf16[8,80,128]{2,1,0:T(8,128)(2,1)S(1)}, bf16[8,80,128]{2,1,0:T(8,128)(2,1)S(1)}, u32[]{:S(2)}, u32[]{:S(2)}) collective-permute-start(bf16[8,80,128]{2,1,0:T(8,128)(2,1)S(1)} %all_to_all.11.own), channel_id=1, source_target_pairs={{0,8},{8,132},{16,24},{24,148},{32,40},{40,164},{48,56},{56,180},{... | collective-permute-start | bytes 491528 | tf_op jit(solution)/shard_map/ppermute | solution.py:47
  117.1 2.9 %collective-permute-start.29 = (bf16[8,80,128]{2,1,0:T(8,128)(2,1)S(1)}, bf16[8,80,128]{2,1,0:T(8,128)(2,1)S(1)}, u32[]{:S(2)}, u32[]{:S(2)}) collective-permute-start(bf16[8,80,128]{2,1,0:T(8,128)(2,1)S(1)} %collective-permute-done.27.first), channel_id=1, source_target_pairs={{0,8},{8,0},{16,24},{24,16},{32,40},{40,32},{48,56},{56,48},{64,72... | collective-permute-start | bytes 491528 | tf_op jit(solution)/shard_map/ppermute | solution.py:47
  119.0 1.4 %collective-permute-start.30 = (bf16[8,80,128]{2,1,0:T(8,128)(2,1)S(1)}, bf16[8,80,128]{2,1,0:T(8,128)(2,1)S(1)}, u32[]{:S(2)}, u32[]{:S(2)}) collective-permute-start(bf16[8,80,128]{2,1,0:T(8,128)(2,1)S(1)} %collective-permute-done.28.second), channel_id=1, source_target_pairs={{0,8},{8,0},{16,24},{24,16},{32,40},{40,32},{48,56},{56,48},{64,72... | collective-permute-start | bytes 491528 | tf_op jit(solution)/shard_map/ppermute | solution.py:47

commit v5 on v4

--- a/solution.py
+++ b/solution.py
@@ -64,16 +64,15 @@
 
 
 def scatter_x(parts):
-    return [
-        parts[0],
-        send(parts[1], lambda x, y, z, c: (x + 1, y, z, 1 - c)),
-        send(parts[2], lambda x, y, z, c: (x + 2, y, z, c)),
-        send(parts[3], lambda x, y, z, c: (x - 1, y, z, 1 - c)),
-    ]
+    across = send(parts[2], lambda x, y, z, c: (x + 2, y, z, c))
+    after = send(parts[1], lambda x, y, z, c: (x + 1, y, z, 1 - c))
+    before = send(parts[3], lambda x, y, z, c: (x - 1, y, z, 1 - c))
+    return [parts[0], across, after, before]
 
 
 def scatter_y(parts):
-    return [parts[0]] + [send_y(parts[step], step) for step in range(1, NY)]
+    across = send_y(parts[2], 2)
+    return [parts[0], across, send_y(parts[1], 1), send_y(parts[3], 3)]
 
 
 def exchange_z(value):

time: 122 us -> 122 us (level)
    ppermute x31, waiting for transfers between devices: 26.6 us -> 25.4 us  [send(): return lax.ppermute(value, AXES, permutation(target))]
  transfers between devices with their start and end apart: 31 -> 31, of which waited for: 16 -> 15; matrix products, arithmetic and copies ran while one was open for 0% -> 0% of each run, Pallas kernels for 16% -> 16%
where the time goes in v5:
time: 122 us
  starting transfers between devices  45.2 us (37%)
  blocking collectives  27.2 us (22%)
  waiting for transfers between devices  25.4 us (21%)
  Pallas kernels  21.2 us (17%)
  between operations  1.53 us (1%)
    ppermute x31, starting transfers between devices, send(): return lax.ppermute(value, AXES, permutation(target))  45.2 us
    all_to_all x2, blocking collectives, exchange_z(): lax.all_to_all(value, AXES, 0, 0, axis_index_groups=Z_GROUPS, tiled=True)  27.2 us
    ppermute x31, waiting for transfers between devices, send(): return lax.ppermute(value, AXES, permutation(target))  25.4 us
    pallas_call x4, Pallas kernels, call(): pl.pallas_call(kernel, out_shape=outs, in_specs=[SCALARS] + [RESIDENT] *...  13.5 us
    pallas_call x1, Pallas kernels, normalize(): pl.pallas_call(normalize_kernel, out_shape=[jax.ShapeDtypeStruct((CLIP, H...  5.02 us
  transfers between devices with their start and end apart: 31, of which 15 were waited for; matrix products, arithmetic and copies ran while one was open for 0% of the time, Pallas kernels for 16%

profile of v5, /device:TPU:1, one launch (start us, length us, event | category | flops | bytes accessed | tf_op | source)
XLA Modules:
  0.0 121.8 jit_solution(2090159502834786428)
XLA Ops:
  0.7 1.0 dynamic-slice_bitcast_fusion
  1.6 3.3 %collective-permute-start.1 = (bf16[128,640]{1,0:T(8,128)(2,1)S(1)}, bf16[128,640]{1,0:T(8,128)(2,1)S(1)}, u32[]{:S(2)}, u32[]{:S(2)}) collective-permute-start(bf16[128,640]{1,0:T(8,128)(2,1)S(1)} %dynamic-slice_bitcast_fusion), channel_id=1, source_target_pairs={{0,140},{8,0},{16,156},{24,16},{32,172},{40,32},{48,188},{56,48},{... | collective-permute-start | bytes 491528 | tf_op jit(solution)/shard_map/ppermute | solution.py:47
  4.9 1.9 %collective-permute-start = (bf16[128,640]{1,0:T(8,128)(2,1)S(1)}, bf16[128,640]{1,0:T(8,128)(2,1)S(1)}, u32[]{:S(2)}, u32[]{:S(2)}) collective-permute-start(bf16[128,640]{1,0:T(8,128)(2,1)S(1)} %dynamic-slice_bitcast_fusion), channel_id=1, source_target_pairs={{0,0},{8,12},{16,16},{24,28},{32,32},{40,44},{48,48},{56,60},{64,6... | collective-permute-start | bytes 491528 | tf_op jit(solution)/shard_map/ppermute | solution.py:47
  6.8 2.3 %collective-permute-start.2 = (bf16[640,128]{1,0:T(8,128)(2,1)S(1)}, bf16[640,128]{1,0:T(8,128)(2,1)S(1)}, u32[]{:S(2)}, u32[]{:S(2)}) collective-permute-start(bf16[640,128]{1,0:T(8,128)(2,1)S(1)} %fusion), channel_id=1, source_target_pairs={{0,3},{8,11},{16,19},{24,27},{32,35},{40,43},{48,51},{56,59},{64,6... | collective-permute-start | bytes 491528 | tf_op jit(solution)/shard_map/ppermute | solution.py:47
  9.1 0.3 collective-permute-start.3
  9.5 0.7 collective-permute-start.4
  10.2 5.0 %normalize.1 = (bf16[192,2560]{1,0:T(8,128)(2,1)S(1)}, bf16[5,192,2560]{2,1,0:T(8,128)(2,1)S(1)}) custom-call(s32[4]{0:T(128)S(1)} %pad_add_fusion.place, bf16[192,5120]{1,0:T(8,128)(2,1)} %states.1, bf16[192,5120]{1,0:T(8,128)(2,1)} %refs_0_.3, bf16[192,5120]{1,0:T(8,128)(2,1)} %refs_1_.3, bf16[192,5120]{1,0:T(8,128)(2,1)} %refs_2_.3, bf16[192,5120]{1,0:T(8,128)(2,1)} %refs_3_.3), custom_call_target="tpu_custom_call" | custom-call | flops 1000 | bytes 1000 | tf_op jit(solution)/shard_map/normalize/pallas_call | solution.py:148
  15.3 1.0 collective-permute-done.2
  16.5 3.8 %collective-permute-done.4 = bf16[640,128]{1,0:T(8,128)(2,1)S(1)} collective-permute-done((bf16[640,128]{1,0:T(8,128)(2,1)S(1)}, bf16[640,128]{1,0:T(8,128)(2,1)S(1)}, u32[]{:S(2)}, u32[]{:S(2)}) %collective-permute-start.4) | collective-permute-done | bytes 163872 | tf_op jit(solution)/shard_map/ppermute | solution.py:47
  20.3 0.5 collective-permute-start.5
  20.9 2.1 %collective-permute-start.6 = (bf16[4,640,128]{2,1,0:T(8,128)(2,1)S(1)}, bf16[4,640,128]{2,1,0:T(8,128)(2,1)S(1)}, u32[]{:S(2)}, u32[]{:S(2)}) collective-permute-start(bf16[4,640,128]{2,1,0:T(8,128)(2,1)S(1)} %pad_maximum_fusion), channel_id=1, source_target_pairs={{0,0},{8,12},{16,16},{24,28},{32,32},{40,44},{48,48},{56,60},{64,6... | collective-permute-start | bytes 1966088 | tf_op jit(solution)/shard_map/ppermute | solution.py:47
  23.0 0.4 collective-permute-start.10
  23.4 1.1 collective-permute-start.11
  25.2 8.7 %collective-permute-done.6.own = bf16[4,640,128]{2,1,0:T(8,128)(2,1)S(1)} collective-permute-done((bf16[4,640,128]{2,1,0:T(8,128)(2,1)S(1)}, bf16[4,640,128]{2,1,0:T(8,128)(2,1)S(1)}, u32[]{:S(2)}, u32[]{:S(2)}) %collective-permute-start.6) | collective-permute-done | bytes 655392 | tf_op jit(solution)/shard_map/ppermute | solution.py:47
  33.9 1.3 %lower.1 = (f32[2,200,128]{2,1,0:T(8,128)S(1)}, f32[2,200,128]{2,1,0:T(8,128)S(1)}) custom-call(s32[4]{0:T(128)S(1)} %pad_add_fusion.place, bf16[192,2560]{1,0:T(8,128)(2,1)S(1)} %get-tuple-element.37.nown, bf16[5,192,2560]{2,1,0:T(8,128)(2,1)S(1)} %collective-permute-done.5.npeer.refs_4_.peer, bf16[4,640,128]{2,1,0:T(8,128)(2,1)S(1)} %collective-permute-done.6.own, ...), custom_call_target="tpu_custom_call" | custom-call | flops 1000 | bytes 1000 | tf_op jit(solution)/shard_map/lower/pallas_call | solution.py:97
  35.2 0.3 collective-permute-start.8
  35.5 0.3 collective-permute-start.9
  36.0 0.8 collective-permute-done.8.refs_7_
  36.8 0.3 collective-permute-done.9.refs_8_
  37.1 7.4 %attend.2 = (bf16[4,8,40,128]{3,2,1,0:T(8,128)(2,1)S(1)}, bf16[4,8,40,128]{3,2,1,0:T(8,128)(2,1)S(1)}, bf16[4,8,40,128]{3,2,1,0:T(8,128)(2,1)S(1)}, f32[2,192,12...) custom-call(s32[4]{0:T(128)S(1)} %pad_add_fusion.place, ...), custom_call_target="tpu_custom_call" | custom-call | flops 1000 | bytes 1000 | tf_op jit(solution)/shard_map/attend/pallas_call | solution.py:97
  44.6 1.8 %collective-permute-done.13.refs_9_ = bf16[2,128,640]{2,1,0:T(8,128)(2,1)S(1)} collective-permute-done((bf16[2,128,640]{2,1,0:T(8,128)(2,1)S(1)}, bf16[2,128,640]{2,1,0:T(8,128)(2,1)S(1)}, u32[]{:S(2)}, u32[]{:S(2)}) %collective-permute-start.13) | collective-permute-done | bytes 327712 | tf_op jit(solution)/shard_map/ppermute | solution.py:47
  46.4 3.0 %attend.3 = (bf16[4,8,40,128]{3,2,1,0:T(8,128)(2,1)S(1)}, f32[2,192,128]{2,1,0:T(8,128)S(1)}, f32[2,192,128]{2,1,0:T(8,128)S(1)}) custom-call(s32[4]{0:T(128)S(1)} %pad_add_fusion.place, bf16[192,5120]{1,0:T(8,128)(2,1)S(1)} %copy-done.1, bf16[192,5120]{1,0:T(8,128)(2,1)S(1)} %copy-done.2, bf16[192,5120]{1,0:T(8,128)(2,1)S(1)} %copy-done.3, ...), custom_call_target="tpu_custom_call" | custom-call | flops 1000 | bytes 1000 | tf_op jit(solution)/shard_map/attend/pallas_call | solution.py:97
  49.4 1.2 collective-permute-start.19
  50.6 0.2 collective-permute-start.14
  50.9 1.4 %collective-permute-start.15 = (bf16[4,8,40,128]{3,2,1,0:T(8,128)(2,1)S(1)}, bf16[4,8,40,128]{3,2,1,0:T(8,128)(2,1)S(1)}, u32[]{:S(2)}, u32[]{:S(2)}) collective-permute-start(bf16[4,8,40,128]{3,2,1,0:T(8,128)(2,1)S(1)} %get-tuple-element.51), channel_id=1, source_target_pairs={{0,3},{8,11},{16,19},{24,27},{32,35},{40,43},{48,51},{56,59},{64,6... | collective-permute-start | bytes 983048 | tf_op jit(solution)/shard_map/ppermute | solution.py:47
  52.3 1.9 %down_grads.1 = (bf16[4,8,40,128]{3,2,1,0:T(8,128)(2,1)S(1)}, bf16[4,8,40,128]{3,2,1,0:T(8,128)(2,1)S(1)}, bf16[4,8,40,128]{3,2,1,0:T(8,128)(2,1)S(1)}, bf16[4,8,40,128]{3,2,1,0:T(8,128)(2,1)S(1)}) custom-call(s32[4]{0:T(128)S(1)} %pad_add_fusion.place, bf16[192,2560]{1,0:T(8,128)(2,1)S(1)} %get-tuple-element.37.nown, ...), custom_call_target="tpu_custom_call" | custom-call | flops 1000 | bytes 1000 | tf_op jit(solution)/shard_map/down_grads/pallas_call | solution.py:97
  54.1 1.5 %collective-permute-start.21 = (bf16[4,8,40,128]{3,2,1,0:T(8,128)(2,1)S(1)}, bf16[4,8,40,128]{3,2,1,0:T(8,128)(2,1)S(1)}, u32[]{:S(2)}, u32[]{:S(2)}) collective-permute-start(bf16[4,8,40,128]{3,2,1,0:T(8,128)(2,1)S(1)} %get-tuple-element.59), channel_id=1, source_target_pairs={{0,128},{8,136},{16,144},{24,152},{32,160},{40,168},{48,176},{56,1... | collective-permute-start | bytes 983048 | tf_op jit(solution)/shard_map/ppermute | solution.py:47
  55.7 3.3 %collective-permute-start.22 = (bf16[4,8,40,128]{3,2,1,0:T(8,128)(2,1)S(1)}, bf16[4,8,40,128]{3,2,1,0:T(8,128)(2,1)S(1)}, u32[]{:S(2)}, u32[]{:S(2)}) collective-permute-start(bf16[4,8,40,128]{3,2,1,0:T(8,128)(2,1)S(1)} %get-tuple-element.60), channel_id=1, source_target_pairs={{0,12},{8,4},{16,28},{24,20},{32,44},{40,36},{48,60},{56,52},{64,7... | collective-permute-start | bytes 983048 | tf_op jit(solution)/shard_map/ppermute | solution.py:47
  58.9 6.9 %collective-permute-start.23 = (bf16[4,8,40,128]{3,2,1,0:T(8,128)(2,1)S(1)}, bf16[4,8,40,128]{3,2,1,0:T(8,128)(2,1)S(1)}, u32[]{:S(2)}, u32[]{:S(2)}) collective-permute-start(bf16[4,8,40,128]{3,2,1,0:T(8,128)(2,1)S(1)} %get-tuple-element.61), channel_id=1, source_target_pairs={{0,140},{8,132},{16,156},{24,148},{32,172},{40,164},{48,188},{56,1... | collective-permute-start | bytes 983048 | tf_op jit(solution)/shard_map/ppermute | solution.py:47
  65.8 0.2 collective-permute-done.15.refs_3_
  66.0 0.7 sum_y.1
  66.8 1.6 %collective-permute-start.16 = (bf16[8,40,128]{2,1,0:T(8,128)(2,1)S(1)}, bf16[8,40,128]{2,1,0:T(8,128)(2,1)S(1)}, u32[]{:S(2)}, u32[]{:S(2)}) collective-permute-start(bf16[8,40,128]{2,1,0:T(8,128)(2,1)S(1)} %get-tuple-element.53), channel_id=1, source_target_pairs={{0,128},{8,136},{16,144},{24,152},{32,160},{40,168},{48,176},{56,1... | collective-permute-start | bytes 245768 | tf_op jit(solution)/shard_map/ppermute | solution.py:47
  68.3 3.5 %collective-permute-start.17 = (bf16[8,40,128]{2,1,0:T(8,128)(2,1)S(1)}, bf16[8,40,128]{2,1,0:T(8,128)(2,1)S(1)}, u32[]{:S(2)}, u32[]{:S(2)}) collective-permute-start(bf16[8,40,128]{2,1,0:T(8,128)(2,1)S(1)} %get-tuple-element.54), channel_id=1, source_target_pairs={{0,12},{8,4},{16,28},{24,20},{32,44},{40,36},{48,60},{56,52},{64,7... | collective-permute-start | bytes 245768 | tf_op jit(solution)/shard_map/ppermute | solution.py:47
  71.9 1.4 %collective-permute-done.22.refs_2_ = bf16[4,8,40,128]{3,2,1,0:T(8,128)(2,1)S(1)} collective-permute-done((bf16[4,8,40,128]{3,2,1,0:T(8,128)(2,1)S(1)}, bf16[4,8,40,128]{3,2,1,0:T(8,128)(2,1)S(1)}, u32[]{:S(2)}, u32[]{:S(2)}) %collective-permute-start.22) | collective-permute-done | bytes 327712 | tf_op jit(solution)/shard_map/ppermute | solution.py:47
  73.3 0.3 collective-permute-done.23.refs_3_
  73.8 1.9 %collective-permute-start.24 = (bf16[8,40,128]{2,1,0:T(8,128)(2,1)S(1)}, bf16[8,40,128]{2,1,0:T(8,128)(2,1)S(1)}, u32[]{:S(2)}, u32[]{:S(2)}) collective-permute-start(bf16[8,40,128]{2,1,0:T(8,128)(2,1)S(1)} %get-tuple-element.63), channel_id=1, source_target_pairs={{0,2},{8,10},{16,18},{24,26},{32,34},{40,42},{48,50},{56,58},{64,6... | collective-permute-start | bytes 245768 | tf_op jit(solution)/shard_map/ppermute | solution.py:47
  75.7 2.7 %collective-permute-start.26 = (bf16[8,40,128]{2,1,0:T(8,128)(2,1)S(1)}, bf16[8,40,128]{2,1,0:T(8,128)(2,1)S(1)}, u32[]{:S(2)}, u32[]{:S(2)}) collective-permute-start(bf16[8,40,128]{2,1,0:T(8,128)(2,1)S(1)} %get-tuple-element.65), channel_id=1, source_target_pairs={{0,3},{8,11},{16,19},{24,27},{32,35},{40,43},{48,51},{56,59},{64,6... | collective-permute-start | bytes 245768 | tf_op jit(solution)/shard_map/ppermute | solution.py:47
  78.4 0.9 collective-permute-done.24.refs_5_
  79.3 2.4 %collective-permute-done.25.refs_6_ = bf16[8,40,128]{2,1,0:T(8,128)(2,1)S(1)} collective-permute-done((bf16[8,40,128]{2,1,0:T(8,128)(2,1)S(1)}, bf16[8,40,128]{2,1,0:T(8,128)(2,1)S(1)}, u32[]{:S(2)}, u32[]{:S(2)}) %collective-permute-start.25) | collective-permute-done | bytes 81952 | tf_op jit(solution)/shard_map/ppermute | solution.py:47
  81.7 16.4 %all_to_all.10 = bf16[8,80,128]{2,1,0:T(8,128)(2,1)S(1)} all-to-all(bf16[8,80,128]{2,1,0:T(8,128)(2,1)S(1)} %join.1), channel_id=1, replica_groups={{0,16,32,48,64,80,96,112},{8,24,40,56,72,88,104,120},{1,17,33,49,65,81,..., dimensions={0} | all-to-all | bytes 327680 | tf_op jit(solution)/shard_map/all_to_all | solution.py:79
  98.2 10.8 %all_to_all.11.own = bf16[8,80,128]{2,1,0:T(8,128)(2,1)S(1)} all-to-all(bf16[8,80,128]{2,1,0:T(8,128)(2,1)S(1)} %broadcast_in_dim.7), channel_id=1, replica_groups={{0,16,32,48,64,80,96,112},{8,24,40,56,72,88,104,120},{1,17,33,49,65,81,..., dimensions={0} | all-to-all | bytes 327680 | tf_op jit(solution)/shard_map/all_to_all | solution.py:79
  108.9 3.1 %collective-permute-start.27 = (bf16[8,80,128]{2,1,0:T(8,128)(2,1)S(1)}, bf16[8,80,128]{2,1,0:T(8,128)(2,1)S(1)}, u32[]{:S(2)}, u32[]{:S(2)}) collective-permute-start(bf16[8,80,128]{2,1,0:T(8,128)(2,1)S(1)} %all_to_all.11.own), channel_id=1, source_target_pairs={{0,136},{8,4},{16,152},{24,20},{32,168},{40,36},{48,184},{56,52},{... | collective-permute-start | bytes 491528 | tf_op jit(solution)/shard_map/ppermute | solution.py:47
  112.0 1.9 %collective-permute-start.28 = (bf16[8,80,128]{2,1,0:T(8,128)(2,1)S(1)}, bf16[8,80,128]{2,1,0:T(8,128)(2,1)S(1)}, u32[]{:S(2)}, u32[]{:S(2)}) collective-permute-start(bf16[8,80,128]{2,1,0:T(8,128)(2,1)S(1)} %all_to_all.11.own), channel_id=1, source_target_pairs={{0,8},{8,132},{16,24},{24,148},{32,40},{40,164},{48,56},{56,180},{... | collective-permute-start | bytes 491528 | tf_op jit(solution)/shard_map/ppermute | solution.py:47
  114.0 2.3 %collective-permute-done.27.first = bf16[8,80,128]{2,1,0:T(8,128)(2,1)S(1)} collective-permute-done((bf16[8,80,128]{2,1,0:T(8,128)(2,1)S(1)}, bf16[8,80,128]{2,1,0:T(8,128)(2,1)S(1)}, u32[]{:S(2)}, u32[]{:S(2)}) %collective-permute-start.27) | collective-permute-done | bytes 163872 | tf_op jit(solution)/shard_map/ppermute | solution.py:47
  116.3 2.4 %collective-permute-start.29 = (bf16[8,80,128]{2,1,0:T(8,128)(2,1)S(1)}, bf16[8,80,128]{2,1,0:T(8,128)(2,1)S(1)}, u32[]{:S(2)}, u32[]{:S(2)}) collective-permute-start(bf16[8,80,128]{2,1,0:T(8,128)(2,1)S(1)} %collective-permute-done.27.first), channel_id=1, source_target_pairs={{0,8},{8,0},{16,24},{24,16},{32,40},{40,32},{48,56},{56,48},{64,72... | collective-permute-start | bytes 491528 | tf_op jit(solution)/shard_map/ppermute | solution.py:47
  118.7 1.0 collective-permute-done.29.first_peer
  119.7 0.4 collective-permute-done.30.second_peer
  120.0 1.7 %finish.1 = (f32[2,640,128]{2,1,0:T(8,128)}, f32[32,8,640]{2,1,0:T(8,128)}) custom-call(s32[4]{0:T(128)S(1)} %pad_add_fusion.place, bf16[8,80,128]{2,1,0:T(8,128)(2,1)S(1)} %all_to_all.11.own, bf16[8,80,128]{2,1,0:T(8,128)(2,1)S(1)} %collective-permute-done.27.first, bf16[8,80,128]{2,1,0:T(8,128)(2,1)S(1)} %collective-permute-done.28.second, ...), custom_call_target="tpu_custom_call" | custom-call | tf_op jit(solution)/shard_map/finish/pallas_call | solution.py:408
  (44 shorter events, 1.2 us)
Async XLA Ops:
  0.6 6.2 %copy-start = (bf16[2,640,128]{2,1,0:T(8,128)(2,1)S(1)}, bf16[2,640,128]{2,1,0:T(8,128)(2,1)}, u32[]{:S(2)}) copy-start(bf16[2,640,128]{2,1,0:T(8,128)(2,1)} %param.14) | copy-start | bytes 983044
  1.6 13.6 %collective-permute-start.1 = (bf16[128,640]{1,0:T(8,128)(2,1)S(1)}, bf16[128,640]{1,0:T(8,128)(2,1)S(1)}, u32[]{:S(2)}, u32[]{:S(2)}) collective-permute-start(bf16[128,640]{1,0:T(8,128)(2,1)S(1)} %dynamic-slice_bitcast_fusion), channel_id=1, source_target_pairs={{0,140},{8,0},{16,156},{24,16},{32,172},{40,32},{48,188},{56,48},{... | collective-permute-start | bytes 491528 | tf_op jit(solution)/shard_map/ppermute | solution.py:47
  4.9 10.4 %collective-permute-start = (bf16[128,640]{1,0:T(8,128)(2,1)S(1)}, bf16[128,640]{1,0:T(8,128)(2,1)S(1)}, u32[]{:S(2)}, u32[]{:S(2)}) collective-permute-start(bf16[128,640]{1,0:T(8,128)(2,1)S(1)} %dynamic-slice_bitcast_fusion), channel_id=1, source_target_pairs={{0,0},{8,12},{16,16},{24,28},{32,32},{40,44},{48,48},{56,60},{64,6... | collective-permute-start | bytes 491528 | tf_op jit(solution)/shard_map/ppermute | solution.py:47
  6.8 9.4 %collective-permute-start.2 = (bf16[640,128]{1,0:T(8,128)(2,1)S(1)}, bf16[640,128]{1,0:T(8,128)(2,1)S(1)}, u32[]{:S(2)}, u32[]{:S(2)}) collective-permute-start(bf16[640,128]{1,0:T(8,128)(2,1)S(1)} %fusion), channel_id=1, source_target_pairs={{0,3},{8,11},{16,19},{24,27},{32,35},{40,43},{48,51},{56,59},{64,6... | collective-permute-start | bytes 491528 | tf_op jit(solution)/shard_map/ppermute | solution.py:47
  9.1 7.3 %collective-permute-start.3 = (bf16[640,128]{1,0:T(8,128)(2,1)S(1)}, bf16[640,128]{1,0:T(8,128)(2,1)S(1)}, u32[]{:S(2)}, u32[]{:S(2)}) collective-permute-start(bf16[640,128]{1,0:T(8,128)(2,1)S(1)} %fusion), channel_id=1, source_target_pairs={{0,2},{8,10},{16,18},{24,26},{32,34},{40,42},{48,50},{56,58},{64,6... | collective-permute-start | bytes 491528 | tf_op jit(solution)/shard_map/ppermute | solution.py:47
  9.5 10.8 %collective-permute-start.4 = (bf16[640,128]{1,0:T(8,128)(2,1)S(1)}, bf16[640,128]{1,0:T(8,128)(2,1)S(1)}, u32[]{:S(2)}, u32[]{:S(2)}) collective-permute-start(bf16[640,128]{1,0:T(8,128)(2,1)S(1)} %fusion), channel_id=1, source_target_pairs={{0,1},{8,9},{16,17},{24,25},{32,33},{40,41},{48,49},{56,57},{64,65... | collective-permute-start | bytes 491528 | tf_op jit(solution)/shard_map/ppermute | solution.py:47
  20.3 13.6 %collective-permute-start.5 = (bf16[5,192,2560]{2,1,0:T(8,128)(2,1)S(1)}, bf16[5,192,2560]{2,1,0:T(8,128)(2,1)S(1)}, u32[]{:S(2)}, u32[]{:S(2)}) collective-permute-start(bf16[5,192,2560]{2,1,0:T(8,128)(2,1)S(1)} %get-tuple-element.36), channel_id=1, source_target_pairs={{0,8},{8,0},{16,24},{24,16},{32,40},{40,32},{48,56},{56,48},{64,72... | collective-permute-start | bytes 14745608 | tf_op jit(solution)/shard_map/ppermute | solution.py:47
  20.8 16.3 %copy-start.4 = (bf16[192,5120]{1,0:T(8,128)(2,1)S(1)}, bf16[192,5120]{1,0:T(8,128)(2,1)}, u32[]{:S(2)}) copy-start(bf16[192,5120]{1,0:T(8,128)(2,1)} %refs_3_.3) | copy-start | bytes 5898244
  20.9 13.0 %collective-permute-start.6 = (bf16[4,640,128]{2,1,0:T(8,128)(2,1)S(1)}, bf16[4,640,128]{2,1,0:T(8,128)(2,1)S(1)}, u32[]{:S(2)}, u32[]{:S(2)}) collective-permute-start(bf16[4,640,128]{2,1,0:T(8,128)(2,1)S(1)} %pad_maximum_fusion), channel_id=1, source_target_pairs={{0,0},{8,12},{16,16},{24,28},{32,32},{40,44},{48,48},{56,60},{64,6... | collective-permute-start | bytes 1966088 | tf_op jit(solution)/shard_map/ppermute | solution.py:47
  22.9 10.9 %collective-permute-start.7 = (bf16[4,640,128]{2,1,0:T(8,128)(2,1)S(1)}, bf16[4,640,128]{2,1,0:T(8,128)(2,1)S(1)}, u32[]{:S(2)}, u32[]{:S(2)}) collective-permute-start(bf16[4,640,128]{2,1,0:T(8,128)(2,1)S(1)} %pad_maximum_fusion), channel_id=1, source_target_pairs={{0,140},{8,0},{16,156},{24,16},{32,172},{40,32},{48,188},{56,48},{... | collective-permute-start | bytes 1966088 | tf_op jit(solution)/shard_map/ppermute | solution.py:47
  23.0 13.0 %collective-permute-start.10 = (bf16[2,128,640]{2,1,0:T(8,128)(2,1)S(1)}, bf16[2,128,640]{2,1,0:T(8,128)(2,1)S(1)}, u32[]{:S(2)}, u32[]{:S(2)}) collective-permute-start(bf16[2,128,640]{2,1,0:T(8,128)(2,1)S(1)} %pad_maximum_fusion.1.refs_11_), channel_id=1, source_target_pairs={{0,3},{8,11},{16,19},{24,27},{32,35},{40,43},{48,51},{56,59},{64,6... | collective-permute-start | bytes 983048 | tf_op jit(solution)/shard_map/ppermute | solution.py:47
  23.4 12.6 %collective-permute-start.11 = (bf16[2,128,640]{2,1,0:T(8,128)(2,1)S(1)}, bf16[2,128,640]{2,1,0:T(8,128)(2,1)S(1)}, u32[]{:S(2)}, u32[]{:S(2)}) collective-permute-start(bf16[2,128,640]{2,1,0:T(8,128)(2,1)S(1)} %pad_maximum_fusion.1.refs_11_), channel_id=1, source_target_pairs={{0,1},{8,9},{16,17},{24,25},{32,33},{40,41},{48,49},{56,57},{64,65... | collective-permute-start | bytes 983048 | tf_op jit(solution)/shard_map/ppermute | solution.py:47
  33.9 3.2 %copy-start.1 = (bf16[192,5120]{1,0:T(8,128)(2,1)S(1)}, bf16[192,5120]{1,0:T(8,128)(2,1)}, u32[]{:S(2)}) copy-start(bf16[192,5120]{1,0:T(8,128)(2,1)} %refs_0_.3) | copy-start | bytes 5898244
  33.9 3.2 %copy-start.2 = (bf16[192,5120]{1,0:T(8,128)(2,1)S(1)}, bf16[192,5120]{1,0:T(8,128)(2,1)}, u32[]{:S(2)}) copy-start(bf16[192,5120]{1,0:T(8,128)(2,1)} %refs_1_.3) | copy-start | bytes 5898244
  33.9 3.2 %copy-start.3 = (bf16[192,5120]{1,0:T(8,128)(2,1)S(1)}, bf16[192,5120]{1,0:T(8,128)(2,1)}, u32[]{:S(2)}) copy-start(bf16[192,5120]{1,0:T(8,128)(2,1)} %refs_2_.3) | copy-start | bytes 5898244
  35.2 1.5 %collective-permute-start.8 = (f32[2,200,128]{2,1,0:T(8,128)S(1)}, f32[2,200,128]{2,1,0:T(8,128)S(1)}, u32[]{:S(2)}, u32[]{:S(2)}) collective-permute-start(f32[2,200,128]{2,1,0:T(8,128)S(1)} %get-tuple-element.41.refs_5_), channel_id=1, source_target_pairs={{0,8},{8,0},{16,24},{24,16},{32,40},{40,32},{48,56},{56,48},{64,72... | collective-permute-start | bytes 614408 | tf_op jit(solution)/shard_map/ppermute | solution.py:47
  35.5 1.5 %collective-permute-start.9 = (f32[2,200,128]{2,1,0:T(8,128)S(1)}, f32[2,200,128]{2,1,0:T(8,128)S(1)}, u32[]{:S(2)}, u32[]{:S(2)}) collective-permute-start(f32[2,200,128]{2,1,0:T(8,128)S(1)} %get-tuple-element.42.refs_6_), channel_id=1, source_target_pairs={{0,8},{8,0},{16,24},{24,16},{32,40},{40,32},{48,56},{56,48},{64,72... | collective-permute-start | bytes 614408 | tf_op jit(solution)/shard_map/ppermute | solution.py:47
  35.8 10.6 %collective-permute-start.13 = (bf16[2,128,640]{2,1,0:T(8,128)(2,1)S(1)}, bf16[2,128,640]{2,1,0:T(8,128)(2,1)S(1)}, u32[]{:S(2)}, u32[]{:S(2)}) collective-permute-start(bf16[2,128,640]{2,1,0:T(8,128)(2,1)S(1)} %pad_maximum_fusion.1.refs_11_), channel_id=1, source_target_pairs={{0,2},{8,10},{16,18},{24,26},{32,34},{40,42},{48,50},{56,58},{64,6... | collective-permute-start | bytes 983048 | tf_op jit(solution)/shard_map/ppermute | solution.py:47
  44.5 14.5 %collective-permute-start.12 = (bf16[4,8,40,128]{3,2,1,0:T(8,128)(2,1)S(1)}, bf16[4,8,40,128]{3,2,1,0:T(8,128)(2,1)S(1)}, u32[]{:S(2)}, u32[]{:S(2)}) collective-permute-start(bf16[4,8,40,128]{3,2,1,0:T(8,128)(2,1)S(1)} %get-tuple-element.45), channel_id=1, source_target_pairs={{0,1},{8,9},{16,17},{24,25},{32,33},{40,41},{48,49},{56,57},{64,65... | collective-permute-start | bytes 983048 | tf_op jit(solution)/shard_map/ppermute | solution.py:47
  49.4 2.9 %collective-permute-start.19 = (f32[2,192,128]{2,1,0:T(8,128)S(1)}, f32[2,192,128]{2,1,0:T(8,128)S(1)}, u32[]{:S(2)}, u32[]{:S(2)}) collective-permute-start(f32[2,192,128]{2,1,0:T(8,128)S(1)} %get-tuple-element.56.mine0), channel_id=1, source_target_pairs={{0,8},{8,0},{16,24},{24,16},{32,40},{40,32},{48,56},{56,48},{64,72... | collective-permute-start | bytes 589832 | tf_op jit(solution)/shard_map/ppermute | solution.py:47
  50.5 1.8 %collective-permute-start.20 = (f32[2,192,128]{2,1,0:T(8,128)S(1)}, f32[2,192,128]{2,1,0:T(8,128)S(1)}, u32[]{:S(2)}, u32[]{:S(2)}) collective-permute-start(f32[2,192,128]{2,1,0:T(8,128)S(1)} %get-tuple-element.57.mine1), channel_id=1, source_target_pairs={{0,8},{8,0},{16,24},{24,16},{32,40},{40,32},{48,56},{56,48},{64,72... | collective-permute-start | bytes 589832 | tf_op jit(solution)/shard_map/ppermute | solution.py:47
  50.6 15.2 %collective-permute-start.14 = (bf16[4,8,40,128]{3,2,1,0:T(8,128)(2,1)S(1)}, bf16[4,8,40,128]{3,2,1,0:T(8,128)(2,1)S(1)}, u32[]{:S(2)}, u32[]{:S(2)}) collective-permute-start(bf16[4,8,40,128]{3,2,1,0:T(8,128)(2,1)S(1)} %get-tuple-element.50), channel_id=1, source_target_pairs={{0,2},{8,10},{16,18},{24,26},{32,34},{40,42},{48,50},{56,58},{64,6... | collective-permute-start | bytes 983048 | tf_op jit(solution)/shard_map/ppermute | solution.py:47
  50.9 15.2 %collective-permute-start.15 = (bf16[4,8,40,128]{3,2,1,0:T(8,128)(2,1)S(1)}, bf16[4,8,40,128]{3,2,1,0:T(8,128)(2,1)S(1)}, u32[]{:S(2)}, u32[]{:S(2)}) collective-permute-start(bf16[4,8,40,128]{3,2,1,0:T(8,128)(2,1)S(1)} %get-tuple-element.51), channel_id=1, source_target_pairs={{0,3},{8,11},{16,19},{24,27},{32,35},{40,43},{48,51},{56,59},{64,6... | collective-permute-start | bytes 983048 | tf_op jit(solution)/shard_map/ppermute | solution.py:47
  54.1 17.7 %collective-permute-start.21 = (bf16[4,8,40,128]{3,2,1,0:T(8,128)(2,1)S(1)}, bf16[4,8,40,128]{3,2,1,0:T(8,128)(2,1)S(1)}, u32[]{:S(2)}, u32[]{:S(2)}) collective-permute-start(bf16[4,8,40,128]{3,2,1,0:T(8,128)(2,1)S(1)} %get-tuple-element.59), channel_id=1, source_target_pairs={{0,128},{8,136},{16,144},{24,152},{32,160},{40,168},{48,176},{56,1... | collective-permute-start | bytes 983048 | tf_op jit(solution)/shard_map/ppermute | solution.py:47
  55.7 17.6 %collective-permute-start.22 = (bf16[4,8,40,128]{3,2,1,0:T(8,128)(2,1)S(1)}, bf16[4,8,40,128]{3,2,1,0:T(8,128)(2,1)S(1)}, u32[]{:S(2)}, u32[]{:S(2)}) collective-permute-start(bf16[4,8,40,128]{3,2,1,0:T(8,128)(2,1)S(1)} %get-tuple-element.60), channel_id=1, source_target_pairs={{0,12},{8,4},{16,28},{24,20},{32,44},{40,36},{48,60},{56,52},{64,7... | collective-permute-start | bytes 983048 | tf_op jit(solution)/shard_map/ppermute | solution.py:47
  58.9 14.7 %collective-permute-start.23 = (bf16[4,8,40,128]{3,2,1,0:T(8,128)(2,1)S(1)}, bf16[4,8,40,128]{3,2,1,0:T(8,128)(2,1)S(1)}, u32[]{:S(2)}, u32[]{:S(2)}) collective-permute-start(bf16[4,8,40,128]{3,2,1,0:T(8,128)(2,1)S(1)} %get-tuple-element.61), channel_id=1, source_target_pairs={{0,140},{8,132},{16,156},{24,148},{32,172},{40,164},{48,188},{56,1... | collective-permute-start | bytes 983048 | tf_op jit(solution)/shard_map/ppermute | solution.py:47
  66.8 9.0 %collective-permute-start.16 = (bf16[8,40,128]{2,1,0:T(8,128)(2,1)S(1)}, bf16[8,40,128]{2,1,0:T(8,128)(2,1)S(1)}, u32[]{:S(2)}, u32[]{:S(2)}) collective-permute-start(bf16[8,40,128]{2,1,0:T(8,128)(2,1)S(1)} %get-tuple-element.53), channel_id=1, source_target_pairs={{0,128},{8,136},{16,144},{24,152},{32,160},{40,168},{48,176},{56,1... | collective-permute-start | bytes 245768 | tf_op jit(solution)/shard_map/ppermute | solution.py:47
  68.3 10.1 %collective-permute-start.17 = (bf16[8,40,128]{2,1,0:T(8,128)(2,1)S(1)}, bf16[8,40,128]{2,1,0:T(8,128)(2,1)S(1)}, u32[]{:S(2)}, u32[]{:S(2)}) collective-permute-start(bf16[8,40,128]{2,1,0:T(8,128)(2,1)S(1)} %get-tuple-element.54), channel_id=1, source_target_pairs={{0,12},{8,4},{16,28},{24,20},{32,44},{40,36},{48,60},{56,52},{64,7... | collective-permute-start | bytes 245768 | tf_op jit(solution)/shard_map/ppermute | solution.py:47
  71.9 6.5 %collective-permute-start.18 = (bf16[8,40,128]{2,1,0:T(8,128)(2,1)S(1)}, bf16[8,40,128]{2,1,0:T(8,128)(2,1)S(1)}, u32[]{:S(2)}, u32[]{:S(2)}) collective-permute-start(bf16[8,40,128]{2,1,0:T(8,128)(2,1)S(1)} %get-tuple-element.55), channel_id=1, source_target_pairs={{0,140},{8,132},{16,156},{24,148},{32,172},{40,164},{48,188},{56,1... | collective-permute-start | bytes 245768 | tf_op jit(solution)/shard_map/ppermute | solution.py:47
  73.8 5.5 %collective-permute-start.24 = (bf16[8,40,128]{2,1,0:T(8,128)(2,1)S(1)}, bf16[8,40,128]{2,1,0:T(8,128)(2,1)S(1)}, u32[]{:S(2)}, u32[]{:S(2)}) collective-permute-start(bf16[8,40,128]{2,1,0:T(8,128)(2,1)S(1)} %get-tuple-element.63), channel_id=1, source_target_pairs={{0,2},{8,10},{16,18},{24,26},{32,34},{40,42},{48,50},{56,58},{64,6... | collective-permute-start | bytes 245768 | tf_op jit(solution)/shard_map/ppermute | solution.py:47
  75.7 5.9 %collective-permute-start.25 = (bf16[8,40,128]{2,1,0:T(8,128)(2,1)S(1)}, bf16[8,40,128]{2,1,0:T(8,128)(2,1)S(1)}, u32[]{:S(2)}, u32[]{:S(2)}) collective-permute-start(bf16[8,40,128]{2,1,0:T(8,128)(2,1)S(1)} %get-tuple-element.64), channel_id=1, source_target_pairs={{0,1},{8,9},{16,17},{24,25},{32,33},{40,41},{48,49},{56,57},{64,65... | collective-permute-start | bytes 245768 | tf_op jit(solution)/shard_map/ppermute | solution.py:47
  75.7 5.9 %collective-permute-start.26 = (bf16[8,40,128]{2,1,0:T(8,128)(2,1)S(1)}, bf16[8,40,128]{2,1,0:T(8,128)(2,1)S(1)}, u32[]{:S(2)}, u32[]{:S(2)}) collective-permute-start(bf16[8,40,128]{2,1,0:T(8,128)(2,1)S(1)} %get-tuple-element.65), channel_id=1, source_target_pairs={{0,3},{8,11},{16,19},{24,27},{32,35},{40,43},{48,51},{56,59},{64,6... | collective-permute-start | bytes 245768 | tf_op jit(solution)/shard_map/ppermute | solution.py:47
  108.9 7.3 %collective-permute-start.27 = (bf16[8,80,128]{2,1,0:T(8,128)(2,1)S(1)}, bf16[8,80,128]{2,1,0:T(8,128)(2,1)S(1)}, u32[]{:S(2)}, u32[]{:S(2)}) collective-permute-start(bf16[8,80,128]{2,1,0:T(8,128)(2,1)S(1)} %all_to_all.11.own), channel_id=1, source_target_pairs={{0,136},{8,4},{16,152},{24,20},{32,168},{40,36},{48,184},{56,52},{... | collective-permute-start | bytes 491528 | tf_op jit(solution)/shard_map/ppermute | solution.py:47
  112.0 6.6 %collective-permute-start.28 = (bf16[8,80,128]{2,1,0:T(8,128)(2,1)S(1)}, bf16[8,80,128]{2,1,0:T(8,128)(2,1)S(1)}, u32[]{:S(2)}, u32[]{:S(2)}) collective-permute-start(bf16[8,80,128]{2,1,0:T(8,128)(2,1)S(1)} %all_to_all.11.own), channel_id=1, source_target_pairs={{0,8},{8,132},{16,24},{24,148},{32,40},{40,164},{48,56},{56,180},{... | collective-permute-start | bytes 491528 | tf_op jit(solution)/shard_map/ppermute | solution.py:47
  116.3 3.4 %collective-permute-start.29 = (bf16[8,80,128]{2,1,0:T(8,128)(2,1)S(1)}, bf16[8,80,128]{2,1,0:T(8,128)(2,1)S(1)}, u32[]{:S(2)}, u32[]{:S(2)}) collective-permute-start(bf16[8,80,128]{2,1,0:T(8,128)(2,1)S(1)} %collective-permute-done.27.first), channel_id=1, source_target_pairs={{0,8},{8,0},{16,24},{24,16},{32,40},{40,32},{48,56},{56,48},{64,72... | collective-permute-start | bytes 491528 | tf_op jit(solution)/shard_map/ppermute | solution.py:47
  118.7 1.4 %collective-permute-start.30 = (bf16[8,80,128]{2,1,0:T(8,128)(2,1)S(1)}, bf16[8,80,128]{2,1,0:T(8,128)(2,1)S(1)}, u32[]{:S(2)}, u32[]{:S(2)}) collective-permute-start(bf16[8,80,128]{2,1,0:T(8,128)(2,1)S(1)} %collective-permute-done.28.second), channel_id=1, source_target_pairs={{0,8},{8,0},{16,24},{24,16},{32,40},{40,32},{48,56},{56,48},{64,72... | collective-permute-start | bytes 491528 | tf_op jit(solution)/shard_map/ppermute | solution.py:47

commit v6 on v5

--- a/solution.py
+++ b/solution.py
@@ -437,10 +437,10 @@
     down_part = lax.dynamic_index_in_dim(down_maps, core, 0, keepdims=False)
     up_part = lax.dynamic_index_in_dim(up_maps, core, 0, keepdims=False)
     nown, nsend = normalize(place, states, q, k, v, g)
-    downs = [send_y(down_part, -step) for step in range(1, NY)]
+    across, after, before = (send_y(down_part, -step) for step in (2, 1, 3))
     up = jnp.stack(cross_x(up_part))
-    nsend, up, *downs = lax.optimization_barrier((nsend, up, *downs))
-    downs = cross_x(jnp.stack([down_part, *downs]))
+    nsend, up, across, after, before = lax.optimization_barrier((nsend, up, across, after, before))
+    downs = cross_x(jnp.stack([down_part, after, across, before]))
     ups = [up] + [send_y(up, -step) for step in range(1, NY)]
     peer = swap_cores(nsend)
 

time: 122 us -> 122 us (level)
  waiting for transfers between devices: 25.4 us -> 20.1 us
  starting transfers between devices: 45.2 us -> 49.8 us
    ppermute x31, waiting for transfers between devices: 25.4 us -> 20.1 us  [send(): return lax.ppermute(value, AXES, permutation(target))]
    ppermute x31, starting transfers between devices: 45.2 us -> 49.8 us  [send(): return lax.ppermute(value, AXES, permutation(target))]
  transfers between devices with their start and end apart: 31 -> 31, of which waited for: 15 -> 11; matrix products, arithmetic and copies ran while one was open for 0% -> 0% of each run, Pallas kernels for 16% -> 16%
where the time goes in v6:
time: 122 us; the launch traced here: 121 us
  starting transfers between devices  49.8 us (41%)
  blocking collectives  27.4 us (22%)
  Pallas kernels  21.2 us (17%)
  waiting for transfers between devices  20.1 us (16%)
  between operations  1.56 us (1%)
    ppermute x31, starting transfers between devices, send(): return lax.ppermute(value, AXES, permutation(target))  49.8 us
    all_to_all x2, blocking collectives, exchange_z(): lax.all_to_all(value, AXES, 0, 0, axis_index_groups=Z_GROUPS, tiled=True)  27.4 us
    ppermute x31, waiting for transfers between devices, send(): return lax.ppermute(value, AXES, permutation(target))  20.1 us
    pallas_call x4, Pallas kernels, call(): pl.pallas_call(kernel, out_shape=outs, in_specs=[SCALARS] + [RESIDENT] *...  13.5 us
    pallas_call x1, Pallas kernels, normalize(): pl.pallas_call(normalize_kernel, out_shape=[jax.ShapeDtypeStruct((CLIP, H...  5.02 us
  transfers between devices with their start and end apart: 31, of which 11 were waited for; matrix products, arithmetic and copies ran while one was open for 0% of the time, Pallas kernels for 16%

profile of v6, /device:TPU:1, one launch (start us, length us, event | category | flops | bytes accessed | tf_op | source)
XLA Modules:
  0.0 121.3 jit_solution(932300672126285812)
XLA Ops:
  0.7 1.0 dynamic-slice_bitcast_fusion
  1.6 3.3 %collective-permute-start.1 = (bf16[128,640]{1,0:T(8,128)(2,1)S(1)}, bf16[128,640]{1,0:T(8,128)(2,1)S(1)}, u32[]{:S(2)}, u32[]{:S(2)}) collective-permute-start(bf16[128,640]{1,0:T(8,128)(2,1)S(1)} %dynamic-slice_bitcast_fusion), channel_id=1, source_target_pairs={{0,140},{8,0},{16,156},{24,16},{32,172},{40,32},{48,188},{56,48},{... | collective-permute-start | bytes 491528 | tf_op jit(solution)/shard_map/ppermute | solution.py:47
  4.9 1.9 %collective-permute-start = (bf16[128,640]{1,0:T(8,128)(2,1)S(1)}, bf16[128,640]{1,0:T(8,128)(2,1)S(1)}, u32[]{:S(2)}, u32[]{:S(2)}) collective-permute-start(bf16[128,640]{1,0:T(8,128)(2,1)S(1)} %dynamic-slice_bitcast_fusion), channel_id=1, source_target_pairs={{0,0},{8,12},{16,16},{24,28},{32,32},{40,44},{48,48},{56,60},{64,6... | collective-permute-start | bytes 491528 | tf_op jit(solution)/shard_map/ppermute | solution.py:47
  6.8 2.5 %collective-permute-start.2 = (bf16[640,128]{1,0:T(8,128)(2,1)S(1)}, bf16[640,128]{1,0:T(8,128)(2,1)S(1)}, u32[]{:S(2)}, u32[]{:S(2)}) collective-permute-start(bf16[640,128]{1,0:T(8,128)(2,1)S(1)} %fusion), channel_id=1, source_target_pairs={{0,2},{8,10},{16,18},{24,26},{32,34},{40,42},{48,50},{56,58},{64,6... | collective-permute-start | bytes 491528 | tf_op jit(solution)/shard_map/ppermute | solution.py:47
  9.3 0.8 collective-permute-start.3
  10.1 0.7 collective-permute-start.4
  10.9 5.0 %normalize.1 = (bf16[192,2560]{1,0:T(8,128)(2,1)S(1)}, bf16[5,192,2560]{2,1,0:T(8,128)(2,1)S(1)}) custom-call(s32[4]{0:T(128)S(1)} %pad_add_fusion.place, bf16[192,5120]{1,0:T(8,128)(2,1)} %states.1, bf16[192,5120]{1,0:T(8,128)(2,1)} %refs_0_.3, bf16[192,5120]{1,0:T(8,128)(2,1)} %refs_1_.3, bf16[192,5120]{1,0:T(8,128)(2,1)} %refs_2_.3, bf16[192,5120]{1,0:T(8,128)(2,1)} %refs_3_.3), custom_call_target="tpu_custom_call" | custom-call | flops 1000 | bytes 1000 | tf_op jit(solution)/shard_map/normalize/pallas_call | solution.py:148
  16.0 1.8 %collective-permute-done.3 = bf16[640,128]{1,0:T(8,128)(2,1)S(1)} collective-permute-done((bf16[640,128]{1,0:T(8,128)(2,1)S(1)}, bf16[640,128]{1,0:T(8,128)(2,1)S(1)}, u32[]{:S(2)}, u32[]{:S(2)}) %collective-permute-start.3) | collective-permute-done | bytes 163872 | tf_op jit(solution)/shard_map/ppermute | solution.py:47
  17.8 0.6 collective-permute-start.5
  18.5 2.1 %collective-permute-start.6 = (bf16[4,640,128]{2,1,0:T(8,128)(2,1)S(1)}, bf16[4,640,128]{2,1,0:T(8,128)(2,1)S(1)}, u32[]{:S(2)}, u32[]{:S(2)}) collective-permute-start(bf16[4,640,128]{2,1,0:T(8,128)(2,1)S(1)} %pad_maximum_fusion), channel_id=1, source_target_pairs={{0,0},{8,12},{16,16},{24,28},{32,32},{40,44},{48,48},{56,60},{64,6... | collective-permute-start | bytes 1966088 | tf_op jit(solution)/shard_map/ppermute | solution.py:47
  20.6 2.4 %collective-permute-start.10 = (bf16[2,128,640]{2,1,0:T(8,128)(2,1)S(1)}, bf16[2,128,640]{2,1,0:T(8,128)(2,1)S(1)}, u32[]{:S(2)}, u32[]{:S(2)}) collective-permute-start(bf16[2,128,640]{2,1,0:T(8,128)(2,1)S(1)} %pad_maximum_fusion.1.refs_11_), channel_id=1, source_target_pairs={{0,3},{8,11},{16,19},{24,27},{32,35},{40,43},{48,51},{56,59},{64,6... | collective-permute-start | bytes 983048 | tf_op jit(solution)/shard_map/ppermute | solution.py:47
  23.7 7.8 %collective-permute-done.6.own = bf16[4,640,128]{2,1,0:T(8,128)(2,1)S(1)} collective-permute-done((bf16[4,640,128]{2,1,0:T(8,128)(2,1)S(1)}, bf16[4,640,128]{2,1,0:T(8,128)(2,1)S(1)}, u32[]{:S(2)}, u32[]{:S(2)}) %collective-permute-start.6) | collective-permute-done | bytes 655392 | tf_op jit(solution)/shard_map/ppermute | solution.py:47
  31.6 1.3 %lower.1 = (f32[2,200,128]{2,1,0:T(8,128)S(1)}, f32[2,200,128]{2,1,0:T(8,128)S(1)}) custom-call(s32[4]{0:T(128)S(1)} %pad_add_fusion.place, bf16[192,2560]{1,0:T(8,128)(2,1)S(1)} %get-tuple-element.37.nown, bf16[5,192,2560]{2,1,0:T(8,128)(2,1)S(1)} %collective-permute-done.5.npeer.refs_4_.peer, bf16[4,640,128]{2,1,0:T(8,128)(2,1)S(1)} %collective-permute-done.6.own, ...), custom_call_target="tpu_custom_call" | custom-call | flops 1000 | bytes 1000 | tf_op jit(solution)/shard_map/lower/pallas_call | solution.py:97
  32.9 0.3 collective-permute-start.8
  33.2 0.3 collective-permute-start.9
  33.5 2.4 %collective-permute-start.13 = (bf16[2,128,640]{2,1,0:T(8,128)(2,1)S(1)}, bf16[2,128,640]{2,1,0:T(8,128)(2,1)S(1)}, u32[]{:S(2)}, u32[]{:S(2)}) collective-permute-start(bf16[2,128,640]{2,1,0:T(8,128)(2,1)S(1)} %pad_maximum_fusion.1.refs_11_), channel_id=1, source_target_pairs={{0,2},{8,10},{16,18},{24,26},{32,34},{40,42},{48,50},{56,58},{64,6... | collective-permute-start | bytes 983048 | tf_op jit(solution)/shard_map/ppermute | solution.py:47
  35.9 7.4 %attend.2 = (bf16[4,8,40,128]{3,2,1,0:T(8,128)(2,1)S(1)}, bf16[4,8,40,128]{3,2,1,0:T(8,128)(2,1)S(1)}, bf16[4,8,40,128]{3,2,1,0:T(8,128)(2,1)S(1)}, f32[2,192,12...) custom-call(s32[4]{0:T(128)S(1)} %pad_add_fusion.place, ...), custom_call_target="tpu_custom_call" | custom-call | flops 1000 | bytes 1000 | tf_op jit(solution)/shard_map/attend/pallas_call | solution.py:97
  43.3 0.5 collective-permute-start.12
  43.8 0.2 collective-permute-done.13.refs_9_
  44.1 3.0 %attend.3 = (bf16[4,8,40,128]{3,2,1,0:T(8,128)(2,1)S(1)}, f32[2,192,128]{2,1,0:T(8,128)S(1)}, f32[2,192,128]{2,1,0:T(8,128)S(1)}) custom-call(s32[4]{0:T(128)S(1)} %pad_add_fusion.place, bf16[192,5120]{1,0:T(8,128)(2,1)S(1)} %copy-done.1, bf16[192,5120]{1,0:T(8,128)(2,1)S(1)} %copy-done.2, bf16[192,5120]{1,0:T(8,128)(2,1)S(1)} %copy-done.3, ...), custom_call_target="tpu_custom_call" | custom-call | flops 1000 | bytes 1000 | tf_op jit(solution)/shard_map/attend/pallas_call | solution.py:97
  47.0 1.2 collective-permute-start.19
  48.2 0.1 collective-permute-start.20
  48.3 2.4 %collective-permute-start.14 = (bf16[4,8,40,128]{3,2,1,0:T(8,128)(2,1)S(1)}, bf16[4,8,40,128]{3,2,1,0:T(8,128)(2,1)S(1)}, u32[]{:S(2)}, u32[]{:S(2)}) collective-permute-start(bf16[4,8,40,128]{3,2,1,0:T(8,128)(2,1)S(1)} %get-tuple-element.50), channel_id=1, source_target_pairs={{0,2},{8,10},{16,18},{24,26},{32,34},{40,42},{48,50},{56,58},{64,6... | collective-permute-start | bytes 983048 | tf_op jit(solution)/shard_map/ppermute | solution.py:47
  50.7 0.9 collective-permute-start.15
  51.6 1.9 %down_grads.1 = (bf16[4,8,40,128]{3,2,1,0:T(8,128)(2,1)S(1)}, bf16[4,8,40,128]{3,2,1,0:T(8,128)(2,1)S(1)}, bf16[4,8,40,128]{3,2,1,0:T(8,128)(2,1)S(1)}, bf16[4,8,40,128]{3,2,1,0:T(8,128)(2,1)S(1)}) custom-call(s32[4]{0:T(128)S(1)} %pad_add_fusion.place, bf16[192,2560]{1,0:T(8,128)(2,1)S(1)} %get-tuple-element.37.nown, ...), custom_call_target="tpu_custom_call" | custom-call | flops 1000 | bytes 1000 | tf_op jit(solution)/shard_map/down_grads/pallas_call | solution.py:97
  53.5 1.4 %collective-permute-start.21 = (bf16[4,8,40,128]{3,2,1,0:T(8,128)(2,1)S(1)}, bf16[4,8,40,128]{3,2,1,0:T(8,128)(2,1)S(1)}, u32[]{:S(2)}, u32[]{:S(2)}) collective-permute-start(bf16[4,8,40,128]{3,2,1,0:T(8,128)(2,1)S(1)} %get-tuple-element.59), channel_id=1, source_target_pairs={{0,128},{8,136},{16,144},{24,152},{32,160},{40,168},{48,176},{56,1... | collective-permute-start | bytes 983048 | tf_op jit(solution)/shard_map/ppermute | solution.py:47
  54.9 3.6 %collective-permute-start.22 = (bf16[4,8,40,128]{3,2,1,0:T(8,128)(2,1)S(1)}, bf16[4,8,40,128]{3,2,1,0:T(8,128)(2,1)S(1)}, u32[]{:S(2)}, u32[]{:S(2)}) collective-permute-start(bf16[4,8,40,128]{3,2,1,0:T(8,128)(2,1)S(1)} %get-tuple-element.60), channel_id=1, source_target_pairs={{0,12},{8,4},{16,28},{24,20},{32,44},{40,36},{48,60},{56,52},{64,7... | collective-permute-start | bytes 983048 | tf_op jit(solution)/shard_map/ppermute | solution.py:47
  58.4 6.3 %collective-permute-start.23 = (bf16[4,8,40,128]{3,2,1,0:T(8,128)(2,1)S(1)}, bf16[4,8,40,128]{3,2,1,0:T(8,128)(2,1)S(1)}, u32[]{:S(2)}, u32[]{:S(2)}) collective-permute-start(bf16[4,8,40,128]{3,2,1,0:T(8,128)(2,1)S(1)} %get-tuple-element.61), channel_id=1, source_target_pairs={{0,140},{8,132},{16,156},{24,148},{32,172},{40,164},{48,188},{56,1... | collective-permute-start | bytes 983048 | tf_op jit(solution)/shard_map/ppermute | solution.py:47
  64.7 1.0 collective-permute-done.15.refs_3_
  65.7 0.7 sum_y.1
  66.4 1.4 %collective-permute-start.16 = (bf16[8,40,128]{2,1,0:T(8,128)(2,1)S(1)}, bf16[8,40,128]{2,1,0:T(8,128)(2,1)S(1)}, u32[]{:S(2)}, u32[]{:S(2)}) collective-permute-start(bf16[8,40,128]{2,1,0:T(8,128)(2,1)S(1)} %get-tuple-element.53), channel_id=1, source_target_pairs={{0,128},{8,136},{16,144},{24,152},{32,160},{40,168},{48,176},{56,1... | collective-permute-start | bytes 245768 | tf_op jit(solution)/shard_map/ppermute | solution.py:47
  67.8 3.7 %collective-permute-start.17 = (bf16[8,40,128]{2,1,0:T(8,128)(2,1)S(1)}, bf16[8,40,128]{2,1,0:T(8,128)(2,1)S(1)}, u32[]{:S(2)}, u32[]{:S(2)}) collective-permute-start(bf16[8,40,128]{2,1,0:T(8,128)(2,1)S(1)} %get-tuple-element.54), channel_id=1, source_target_pairs={{0,12},{8,4},{16,28},{24,20},{32,44},{40,36},{48,60},{56,52},{64,7... | collective-permute-start | bytes 245768 | tf_op jit(solution)/shard_map/ppermute | solution.py:47
  71.5 1.1 collective-permute-done.22.refs_2_
  72.6 1.1 collective-permute-done.23.refs_3_
  73.8 0.2 sum_x.1
  73.9 1.0 collective-permute-start.24
  74.9 2.7 %collective-permute-start.26 = (bf16[8,40,128]{2,1,0:T(8,128)(2,1)S(1)}, bf16[8,40,128]{2,1,0:T(8,128)(2,1)S(1)}, u32[]{:S(2)}, u32[]{:S(2)}) collective-permute-start(bf16[8,40,128]{2,1,0:T(8,128)(2,1)S(1)} %get-tuple-element.65), channel_id=1, source_target_pairs={{0,3},{8,11},{16,19},{24,27},{32,35},{40,43},{48,51},{56,59},{64,6... | collective-permute-start | bytes 245768 | tf_op jit(solution)/shard_map/ppermute | solution.py:47
  77.6 2.1 %collective-permute-done.24.refs_5_ = bf16[8,40,128]{2,1,0:T(8,128)(2,1)S(1)} collective-permute-done((bf16[8,40,128]{2,1,0:T(8,128)(2,1)S(1)}, bf16[8,40,128]{2,1,0:T(8,128)(2,1)S(1)}, u32[]{:S(2)}, u32[]{:S(2)}) %collective-permute-start.24) | collective-permute-done | bytes 81952 | tf_op jit(solution)/shard_map/ppermute | solution.py:47
  79.7 1.8 %collective-permute-done.25.refs_6_ = bf16[8,40,128]{2,1,0:T(8,128)(2,1)S(1)} collective-permute-done((bf16[8,40,128]{2,1,0:T(8,128)(2,1)S(1)}, bf16[8,40,128]{2,1,0:T(8,128)(2,1)S(1)}, u32[]{:S(2)}, u32[]{:S(2)}) %collective-permute-start.25) | collective-permute-done | bytes 81952 | tf_op jit(solution)/shard_map/ppermute | solution.py:47
  81.6 16.4 %all_to_all.10 = bf16[8,80,128]{2,1,0:T(8,128)(2,1)S(1)} all-to-all(bf16[8,80,128]{2,1,0:T(8,128)(2,1)S(1)} %join.1), channel_id=1, replica_groups={{0,16,32,48,64,80,96,112},{8,24,40,56,72,88,104,120},{1,17,33,49,65,81,..., dimensions={0} | all-to-all | bytes 327680 | tf_op jit(solution)/shard_map/all_to_all | solution.py:79
  98.1 10.9 %all_to_all.11.own = bf16[8,80,128]{2,1,0:T(8,128)(2,1)S(1)} all-to-all(bf16[8,80,128]{2,1,0:T(8,128)(2,1)S(1)} %broadcast_in_dim.7), channel_id=1, replica_groups={{0,16,32,48,64,80,96,112},{8,24,40,56,72,88,104,120},{1,17,33,49,65,81,..., dimensions={0} | all-to-all | bytes 327680 | tf_op jit(solution)/shard_map/all_to_all | solution.py:79
  109.1 2.3 %collective-permute-start.27 = (bf16[8,80,128]{2,1,0:T(8,128)(2,1)S(1)}, bf16[8,80,128]{2,1,0:T(8,128)(2,1)S(1)}, u32[]{:S(2)}, u32[]{:S(2)}) collective-permute-start(bf16[8,80,128]{2,1,0:T(8,128)(2,1)S(1)} %all_to_all.11.own), channel_id=1, source_target_pairs={{0,136},{8,4},{16,152},{24,20},{32,168},{40,36},{48,184},{56,52},{... | collective-permute-start | bytes 491528 | tf_op jit(solution)/shard_map/ppermute | solution.py:47
  111.4 2.3 %collective-permute-start.28 = (bf16[8,80,128]{2,1,0:T(8,128)(2,1)S(1)}, bf16[8,80,128]{2,1,0:T(8,128)(2,1)S(1)}, u32[]{:S(2)}, u32[]{:S(2)}) collective-permute-start(bf16[8,80,128]{2,1,0:T(8,128)(2,1)S(1)} %all_to_all.11.own), channel_id=1, source_target_pairs={{0,8},{8,132},{16,24},{24,148},{32,40},{40,164},{48,56},{56,180},{... | collective-permute-start | bytes 491528 | tf_op jit(solution)/shard_map/ppermute | solution.py:47
  113.7 1.6 %collective-permute-done.27.first = bf16[8,80,128]{2,1,0:T(8,128)(2,1)S(1)} collective-permute-done((bf16[8,80,128]{2,1,0:T(8,128)(2,1)S(1)}, bf16[8,80,128]{2,1,0:T(8,128)(2,1)S(1)}, u32[]{:S(2)}, u32[]{:S(2)}) %collective-permute-start.27) | collective-permute-done | bytes 163872 | tf_op jit(solution)/shard_map/ppermute | solution.py:47
  115.3 2.9 %collective-permute-start.29 = (bf16[8,80,128]{2,1,0:T(8,128)(2,1)S(1)}, bf16[8,80,128]{2,1,0:T(8,128)(2,1)S(1)}, u32[]{:S(2)}, u32[]{:S(2)}) collective-permute-start(bf16[8,80,128]{2,1,0:T(8,128)(2,1)S(1)} %collective-permute-done.27.first), channel_id=1, source_target_pairs={{0,8},{8,0},{16,24},{24,16},{32,40},{40,32},{48,56},{56,48},{64,72... | collective-permute-start | bytes 491528 | tf_op jit(solution)/shard_map/ppermute | solution.py:47
  118.2 1.0 collective-permute-done.29.first_peer
  119.2 0.4 collective-permute-done.30.second_peer
  119.6 1.7 %finish.1 = (f32[2,640,128]{2,1,0:T(8,128)}, f32[32,8,640]{2,1,0:T(8,128)}) custom-call(s32[4]{0:T(128)S(1)} %pad_add_fusion.place, bf16[8,80,128]{2,1,0:T(8,128)(2,1)S(1)} %all_to_all.11.own, bf16[8,80,128]{2,1,0:T(8,128)(2,1)S(1)} %collective-permute-done.27.first, bf16[8,80,128]{2,1,0:T(8,128)(2,1)S(1)} %collective-permute-done.28.second, ...), custom_call_target="tpu_custom_call" | custom-call | tf_op jit(solution)/shard_map/finish/pallas_call | solution.py:408
  (44 shorter events, 0.5 us)
Async XLA Ops:
  0.6 6.2 %copy-start = (bf16[2,640,128]{2,1,0:T(8,128)(2,1)S(1)}, bf16[2,640,128]{2,1,0:T(8,128)(2,1)}, u32[]{:S(2)}) copy-start(bf16[2,640,128]{2,1,0:T(8,128)(2,1)} %param.14) | copy-start | bytes 983044
  1.6 14.2 %collective-permute-start.1 = (bf16[128,640]{1,0:T(8,128)(2,1)S(1)}, bf16[128,640]{1,0:T(8,128)(2,1)S(1)}, u32[]{:S(2)}, u32[]{:S(2)}) collective-permute-start(bf16[128,640]{1,0:T(8,128)(2,1)S(1)} %dynamic-slice_bitcast_fusion), channel_id=1, source_target_pairs={{0,140},{8,0},{16,156},{24,16},{32,172},{40,32},{48,188},{56,48},{... | collective-permute-start | bytes 491528 | tf_op jit(solution)/shard_map/ppermute | solution.py:47
  4.9 11.0 %collective-permute-start = (bf16[128,640]{1,0:T(8,128)(2,1)S(1)}, bf16[128,640]{1,0:T(8,128)(2,1)S(1)}, u32[]{:S(2)}, u32[]{:S(2)}) collective-permute-start(bf16[128,640]{1,0:T(8,128)(2,1)S(1)} %dynamic-slice_bitcast_fusion), channel_id=1, source_target_pairs={{0,0},{8,12},{16,16},{24,28},{32,32},{40,44},{48,48},{56,60},{64,6... | collective-permute-start | bytes 491528 | tf_op jit(solution)/shard_map/ppermute | solution.py:47
  6.8 9.1 %collective-permute-start.2 = (bf16[640,128]{1,0:T(8,128)(2,1)S(1)}, bf16[640,128]{1,0:T(8,128)(2,1)S(1)}, u32[]{:S(2)}, u32[]{:S(2)}) collective-permute-start(bf16[640,128]{1,0:T(8,128)(2,1)S(1)} %fusion), channel_id=1, source_target_pairs={{0,2},{8,10},{16,18},{24,26},{32,34},{40,42},{48,50},{56,58},{64,6... | collective-permute-start | bytes 491528 | tf_op jit(solution)/shard_map/ppermute | solution.py:47
  9.3 8.5 %collective-permute-start.3 = (bf16[640,128]{1,0:T(8,128)(2,1)S(1)}, bf16[640,128]{1,0:T(8,128)(2,1)S(1)}, u32[]{:S(2)}, u32[]{:S(2)}) collective-permute-start(bf16[640,128]{1,0:T(8,128)(2,1)S(1)} %fusion), channel_id=1, source_target_pairs={{0,3},{8,11},{16,19},{24,27},{32,35},{40,43},{48,51},{56,59},{64,6... | collective-permute-start | bytes 491528 | tf_op jit(solution)/shard_map/ppermute | solution.py:47
  10.1 7.7 %collective-permute-start.4 = (bf16[640,128]{1,0:T(8,128)(2,1)S(1)}, bf16[640,128]{1,0:T(8,128)(2,1)S(1)}, u32[]{:S(2)}, u32[]{:S(2)}) collective-permute-start(bf16[640,128]{1,0:T(8,128)(2,1)S(1)} %fusion), channel_id=1, source_target_pairs={{0,1},{8,9},{16,17},{24,25},{32,33},{40,41},{48,49},{56,57},{64,65... | collective-permute-start | bytes 491528 | tf_op jit(solution)/shard_map/ppermute | solution.py:47
  17.8 13.7 %collective-permute-start.5 = (bf16[5,192,2560]{2,1,0:T(8,128)(2,1)S(1)}, bf16[5,192,2560]{2,1,0:T(8,128)(2,1)S(1)}, u32[]{:S(2)}, u32[]{:S(2)}) collective-permute-start(bf16[5,192,2560]{2,1,0:T(8,128)(2,1)S(1)} %get-tuple-element.36), channel_id=1, source_target_pairs={{0,8},{8,0},{16,24},{24,16},{32,40},{40,32},{48,56},{56,48},{64,72... | collective-permute-start | bytes 14745608 | tf_op jit(solution)/shard_map/ppermute | solution.py:47
  18.4 17.4 %copy-start.4 = (bf16[192,5120]{1,0:T(8,128)(2,1)S(1)}, bf16[192,5120]{1,0:T(8,128)(2,1)}, u32[]{:S(2)}) copy-start(bf16[192,5120]{1,0:T(8,128)(2,1)} %refs_3_.3) | copy-start | bytes 5898244
  18.5 13.0 %collective-permute-start.6 = (bf16[4,640,128]{2,1,0:T(8,128)(2,1)S(1)}, bf16[4,640,128]{2,1,0:T(8,128)(2,1)S(1)}, u32[]{:S(2)}, u32[]{:S(2)}) collective-permute-start(bf16[4,640,128]{2,1,0:T(8,128)(2,1)S(1)} %pad_maximum_fusion), channel_id=1, source_target_pairs={{0,0},{8,12},{16,16},{24,28},{32,32},{40,44},{48,48},{56,60},{64,6... | collective-permute-start | bytes 1966088 | tf_op jit(solution)/shard_map/ppermute | solution.py:47
  20.6 10.9 %collective-permute-start.7 = (bf16[4,640,128]{2,1,0:T(8,128)(2,1)S(1)}, bf16[4,640,128]{2,1,0:T(8,128)(2,1)S(1)}, u32[]{:S(2)}, u32[]{:S(2)}) collective-permute-start(bf16[4,640,128]{2,1,0:T(8,128)(2,1)S(1)} %pad_maximum_fusion), channel_id=1, source_target_pairs={{0,140},{8,0},{16,156},{24,16},{32,172},{40,32},{48,188},{56,48},{... | collective-permute-start | bytes 1966088 | tf_op jit(solution)/shard_map/ppermute | solution.py:47
  20.6 15.2 %collective-permute-start.10 = (bf16[2,128,640]{2,1,0:T(8,128)(2,1)S(1)}, bf16[2,128,640]{2,1,0:T(8,128)(2,1)S(1)}, u32[]{:S(2)}, u32[]{:S(2)}) collective-permute-start(bf16[2,128,640]{2,1,0:T(8,128)(2,1)S(1)} %pad_maximum_fusion.1.refs_11_), channel_id=1, source_target_pairs={{0,3},{8,11},{16,19},{24,27},{32,35},{40,43},{48,51},{56,59},{64,6... | collective-permute-start | bytes 983048 | tf_op jit(solution)/shard_map/ppermute | solution.py:47
  23.1 12.8 %collective-permute-start.11 = (bf16[2,128,640]{2,1,0:T(8,128)(2,1)S(1)}, bf16[2,128,640]{2,1,0:T(8,128)(2,1)S(1)}, u32[]{:S(2)}, u32[]{:S(2)}) collective-permute-start(bf16[2,128,640]{2,1,0:T(8,128)(2,1)S(1)} %pad_maximum_fusion.1.refs_11_), channel_id=1, source_target_pairs={{0,1},{8,9},{16,17},{24,25},{32,33},{40,41},{48,49},{56,57},{64,65... | collective-permute-start | bytes 983048 | tf_op jit(solution)/shard_map/ppermute | solution.py:47
  31.5 4.4 %copy-start.1 = (bf16[192,5120]{1,0:T(8,128)(2,1)S(1)}, bf16[192,5120]{1,0:T(8,128)(2,1)}, u32[]{:S(2)}) copy-start(bf16[192,5120]{1,0:T(8,128)(2,1)} %refs_0_.3) | copy-start | bytes 5898244
  31.5 4.4 %copy-start.2 = (bf16[192,5120]{1,0:T(8,128)(2,1)S(1)}, bf16[192,5120]{1,0:T(8,128)(2,1)}, u32[]{:S(2)}) copy-start(bf16[192,5120]{1,0:T(8,128)(2,1)} %refs_1_.3) | copy-start | bytes 5898244
  31.5 4.4 %copy-start.3 = (bf16[192,5120]{1,0:T(8,128)(2,1)S(1)}, bf16[192,5120]{1,0:T(8,128)(2,1)}, u32[]{:S(2)}) copy-start(bf16[192,5120]{1,0:T(8,128)(2,1)} %refs_2_.3) | copy-start | bytes 5898244
  32.9 3.0 %collective-permute-start.8 = (f32[2,200,128]{2,1,0:T(8,128)S(1)}, f32[2,200,128]{2,1,0:T(8,128)S(1)}, u32[]{:S(2)}, u32[]{:S(2)}) collective-permute-start(f32[2,200,128]{2,1,0:T(8,128)S(1)} %get-tuple-element.41.refs_5_), channel_id=1, source_target_pairs={{0,8},{8,0},{16,24},{24,16},{32,40},{40,32},{48,56},{56,48},{64,72... | collective-permute-start | bytes 614408 | tf_op jit(solution)/shard_map/ppermute | solution.py:47
  33.2 2.6 %collective-permute-start.9 = (f32[2,200,128]{2,1,0:T(8,128)S(1)}, f32[2,200,128]{2,1,0:T(8,128)S(1)}, u32[]{:S(2)}, u32[]{:S(2)}) collective-permute-start(f32[2,200,128]{2,1,0:T(8,128)S(1)} %get-tuple-element.42.refs_6_), channel_id=1, source_target_pairs={{0,8},{8,0},{16,24},{24,16},{32,40},{40,32},{48,56},{56,48},{64,72... | collective-permute-start | bytes 614408 | tf_op jit(solution)/shard_map/ppermute | solution.py:47
  33.5 10.6 %collective-permute-start.13 = (bf16[2,128,640]{2,1,0:T(8,128)(2,1)S(1)}, bf16[2,128,640]{2,1,0:T(8,128)(2,1)S(1)}, u32[]{:S(2)}, u32[]{:S(2)}) collective-permute-start(bf16[2,128,640]{2,1,0:T(8,128)(2,1)S(1)} %pad_maximum_fusion.1.refs_11_), channel_id=1, source_target_pairs={{0,2},{8,10},{16,18},{24,26},{32,34},{40,42},{48,50},{56,58},{64,6... | collective-permute-start | bytes 983048 | tf_op jit(solution)/shard_map/ppermute | solution.py:47
  43.3 15.1 %collective-permute-start.12 = (bf16[4,8,40,128]{3,2,1,0:T(8,128)(2,1)S(1)}, bf16[4,8,40,128]{3,2,1,0:T(8,128)(2,1)S(1)}, u32[]{:S(2)}, u32[]{:S(2)}) collective-permute-start(bf16[4,8,40,128]{3,2,1,0:T(8,128)(2,1)S(1)} %get-tuple-element.45), channel_id=1, source_target_pairs={{0,1},{8,9},{16,17},{24,25},{32,33},{40,41},{48,49},{56,57},{64,65... | collective-permute-start | bytes 983048 | tf_op jit(solution)/shard_map/ppermute | solution.py:47
  47.0 4.6 %collective-permute-start.19 = (f32[2,192,128]{2,1,0:T(8,128)S(1)}, f32[2,192,128]{2,1,0:T(8,128)S(1)}, u32[]{:S(2)}, u32[]{:S(2)}) collective-permute-start(f32[2,192,128]{2,1,0:T(8,128)S(1)} %get-tuple-element.56.mine0), channel_id=1, source_target_pairs={{0,8},{8,0},{16,24},{24,16},{32,40},{40,32},{48,56},{56,48},{64,72... | collective-permute-start | bytes 589832 | tf_op jit(solution)/shard_map/ppermute | solution.py:47
  48.2 3.4 %collective-permute-start.20 = (f32[2,192,128]{2,1,0:T(8,128)S(1)}, f32[2,192,128]{2,1,0:T(8,128)S(1)}, u32[]{:S(2)}, u32[]{:S(2)}) collective-permute-start(f32[2,192,128]{2,1,0:T(8,128)S(1)} %get-tuple-element.57.mine1), channel_id=1, source_target_pairs={{0,8},{8,0},{16,24},{24,16},{32,40},{40,32},{48,56},{56,48},{64,72... | collective-permute-start | bytes 589832 | tf_op jit(solution)/shard_map/ppermute | solution.py:47
  48.3 16.4 %collective-permute-start.14 = (bf16[4,8,40,128]{3,2,1,0:T(8,128)(2,1)S(1)}, bf16[4,8,40,128]{3,2,1,0:T(8,128)(2,1)S(1)}, u32[]{:S(2)}, u32[]{:S(2)}) collective-permute-start(bf16[4,8,40,128]{3,2,1,0:T(8,128)(2,1)S(1)} %get-tuple-element.50), channel_id=1, source_target_pairs={{0,2},{8,10},{16,18},{24,26},{32,34},{40,42},{48,50},{56,58},{64,6... | collective-permute-start | bytes 983048 | tf_op jit(solution)/shard_map/ppermute | solution.py:47
  50.7 15.0 %collective-permute-start.15 = (bf16[4,8,40,128]{3,2,1,0:T(8,128)(2,1)S(1)}, bf16[4,8,40,128]{3,2,1,0:T(8,128)(2,1)S(1)}, u32[]{:S(2)}, u32[]{:S(2)}) collective-permute-start(bf16[4,8,40,128]{3,2,1,0:T(8,128)(2,1)S(1)} %get-tuple-element.51), channel_id=1, source_target_pairs={{0,3},{8,11},{16,19},{24,27},{32,35},{40,43},{48,51},{56,59},{64,6... | collective-permute-start | bytes 983048 | tf_op jit(solution)/shard_map/ppermute | solution.py:47
  53.5 18.0 %collective-permute-start.21 = (bf16[4,8,40,128]{3,2,1,0:T(8,128)(2,1)S(1)}, bf16[4,8,40,128]{3,2,1,0:T(8,128)(2,1)S(1)}, u32[]{:S(2)}, u32[]{:S(2)}) collective-permute-start(bf16[4,8,40,128]{3,2,1,0:T(8,128)(2,1)S(1)} %get-tuple-element.59), channel_id=1, source_target_pairs={{0,128},{8,136},{16,144},{24,152},{32,160},{40,168},{48,176},{56,1... | collective-permute-start | bytes 983048 | tf_op jit(solution)/shard_map/ppermute | solution.py:47
  54.9 17.8 %collective-permute-start.22 = (bf16[4,8,40,128]{3,2,1,0:T(8,128)(2,1)S(1)}, bf16[4,8,40,128]{3,2,1,0:T(8,128)(2,1)S(1)}, u32[]{:S(2)}, u32[]{:S(2)}) collective-permute-start(bf16[4,8,40,128]{3,2,1,0:T(8,128)(2,1)S(1)} %get-tuple-element.60), channel_id=1, source_target_pairs={{0,12},{8,4},{16,28},{24,20},{32,44},{40,36},{48,60},{56,52},{64,7... | collective-permute-start | bytes 983048 | tf_op jit(solution)/shard_map/ppermute | solution.py:47
  58.4 15.3 %collective-permute-start.23 = (bf16[4,8,40,128]{3,2,1,0:T(8,128)(2,1)S(1)}, bf16[4,8,40,128]{3,2,1,0:T(8,128)(2,1)S(1)}, u32[]{:S(2)}, u32[]{:S(2)}) collective-permute-start(bf16[4,8,40,128]{3,2,1,0:T(8,128)(2,1)S(1)} %get-tuple-element.61), channel_id=1, source_target_pairs={{0,140},{8,132},{16,156},{24,148},{32,172},{40,164},{48,188},{56,1... | collective-permute-start | bytes 983048 | tf_op jit(solution)/shard_map/ppermute | solution.py:47
  66.4 8.5 %collective-permute-start.16 = (bf16[8,40,128]{2,1,0:T(8,128)(2,1)S(1)}, bf16[8,40,128]{2,1,0:T(8,128)(2,1)S(1)}, u32[]{:S(2)}, u32[]{:S(2)}) collective-permute-start(bf16[8,40,128]{2,1,0:T(8,128)(2,1)S(1)} %get-tuple-element.53), channel_id=1, source_target_pairs={{0,128},{8,136},{16,144},{24,152},{32,160},{40,168},{48,176},{56,1... | collective-permute-start | bytes 245768 | tf_op jit(solution)/shard_map/ppermute | solution.py:47
  67.8 9.8 %collective-permute-start.17 = (bf16[8,40,128]{2,1,0:T(8,128)(2,1)S(1)}, bf16[8,40,128]{2,1,0:T(8,128)(2,1)S(1)}, u32[]{:S(2)}, u32[]{:S(2)}) collective-permute-start(bf16[8,40,128]{2,1,0:T(8,128)(2,1)S(1)} %get-tuple-element.54), channel_id=1, source_target_pairs={{0,12},{8,4},{16,28},{24,20},{32,44},{40,36},{48,60},{56,52},{64,7... | collective-permute-start | bytes 245768 | tf_op jit(solution)/shard_map/ppermute | solution.py:47
  71.5 6.1 %collective-permute-start.18 = (bf16[8,40,128]{2,1,0:T(8,128)(2,1)S(1)}, bf16[8,40,128]{2,1,0:T(8,128)(2,1)S(1)}, u32[]{:S(2)}, u32[]{:S(2)}) collective-permute-start(bf16[8,40,128]{2,1,0:T(8,128)(2,1)S(1)} %get-tuple-element.55), channel_id=1, source_target_pairs={{0,140},{8,132},{16,156},{24,148},{32,172},{40,164},{48,188},{56,1... | collective-permute-start | bytes 245768 | tf_op jit(solution)/shard_map/ppermute | solution.py:47
  73.9 5.8 %collective-permute-start.24 = (bf16[8,40,128]{2,1,0:T(8,128)(2,1)S(1)}, bf16[8,40,128]{2,1,0:T(8,128)(2,1)S(1)}, u32[]{:S(2)}, u32[]{:S(2)}) collective-permute-start(bf16[8,40,128]{2,1,0:T(8,128)(2,1)S(1)} %get-tuple-element.63), channel_id=1, source_target_pairs={{0,2},{8,10},{16,18},{24,26},{32,34},{40,42},{48,50},{56,58},{64,6... | collective-permute-start | bytes 245768 | tf_op jit(solution)/shard_map/ppermute | solution.py:47
  74.9 6.6 %collective-permute-start.25 = (bf16[8,40,128]{2,1,0:T(8,128)(2,1)S(1)}, bf16[8,40,128]{2,1,0:T(8,128)(2,1)S(1)}, u32[]{:S(2)}, u32[]{:S(2)}) collective-permute-start(bf16[8,40,128]{2,1,0:T(8,128)(2,1)S(1)} %get-tuple-element.64), channel_id=1, source_target_pairs={{0,1},{8,9},{16,17},{24,25},{32,33},{40,41},{48,49},{56,57},{64,65... | collective-permute-start | bytes 245768 | tf_op jit(solution)/shard_map/ppermute | solution.py:47
  74.9 6.6 %collective-permute-start.26 = (bf16[8,40,128]{2,1,0:T(8,128)(2,1)S(1)}, bf16[8,40,128]{2,1,0:T(8,128)(2,1)S(1)}, u32[]{:S(2)}, u32[]{:S(2)}) collective-permute-start(bf16[8,40,128]{2,1,0:T(8,128)(2,1)S(1)} %get-tuple-element.65), channel_id=1, source_target_pairs={{0,3},{8,11},{16,19},{24,27},{32,35},{40,43},{48,51},{56,59},{64,6... | collective-permute-start | bytes 245768 | tf_op jit(solution)/shard_map/ppermute | solution.py:47
  109.1 6.2 %collective-permute-start.27 = (bf16[8,80,128]{2,1,0:T(8,128)(2,1)S(1)}, bf16[8,80,128]{2,1,0:T(8,128)(2,1)S(1)}, u32[]{:S(2)}, u32[]{:S(2)}) collective-permute-start(bf16[8,80,128]{2,1,0:T(8,128)(2,1)S(1)} %all_to_all.11.own), channel_id=1, source_target_pairs={{0,136},{8,4},{16,152},{24,20},{32,168},{40,36},{48,184},{56,52},{... | collective-permute-start | bytes 491528 | tf_op jit(solution)/shard_map/ppermute | solution.py:47
  111.4 6.8 %collective-permute-start.28 = (bf16[8,80,128]{2,1,0:T(8,128)(2,1)S(1)}, bf16[8,80,128]{2,1,0:T(8,128)(2,1)S(1)}, u32[]{:S(2)}, u32[]{:S(2)}) collective-permute-start(bf16[8,80,128]{2,1,0:T(8,128)(2,1)S(1)} %all_to_all.11.own), channel_id=1, source_target_pairs={{0,8},{8,132},{16,24},{24,148},{32,40},{40,164},{48,56},{56,180},{... | collective-permute-start | bytes 491528 | tf_op jit(solution)/shard_map/ppermute | solution.py:47
  115.3 3.9 %collective-permute-start.29 = (bf16[8,80,128]{2,1,0:T(8,128)(2,1)S(1)}, bf16[8,80,128]{2,1,0:T(8,128)(2,1)S(1)}, u32[]{:S(2)}, u32[]{:S(2)}) collective-permute-start(bf16[8,80,128]{2,1,0:T(8,128)(2,1)S(1)} %collective-permute-done.27.first), channel_id=1, source_target_pairs={{0,8},{8,0},{16,24},{24,16},{32,40},{40,32},{48,56},{56,48},{64,72... | collective-permute-start | bytes 491528 | tf_op jit(solution)/shard_map/ppermute | solution.py:47
  118.2 1.4 %collective-permute-start.30 = (bf16[8,80,128]{2,1,0:T(8,128)(2,1)S(1)}, bf16[8,80,128]{2,1,0:T(8,128)(2,1)S(1)}, u32[]{:S(2)}, u32[]{:S(2)}) collective-permute-start(bf16[8,80,128]{2,1,0:T(8,128)(2,1)S(1)} %collective-permute-done.28.second), channel_id=1, source_target_pairs={{0,8},{8,0},{16,24},{24,16},{32,40},{40,32},{48,56},{56,48},{64,72... | collective-permute-start | bytes 491528 | tf_op jit(solution)/shard_map/ppermute | solution.py:47
